TPU v7x, 32 devices: a whole 2x2x4 slice. The times are simulated.
32 devices in a mesh: task: 4 (over y, core), batch: 8 (over z, x).
Axes of the slice: x: 2, y: 2, z: 4, core: 2. Of those that a mesh axis runs over, the one named last changes fastest.
Arguments:
- tokens: bfloat16 [64, 512, 768], P(('task', 'batch')), may hold values from -6 to 6
- out_cot: bfloat16 [64, 512, 768], P(('task', 'batch')), may hold values from -6 to 6
- lengths: int32 [64], P(('task', 'batch')), may hold values from 128 to 512, as said below
- labels: int32 [64], P(('task', 'batch')), may hold values from 0 to 2
- task_ids: int32 [4], P('task'), may hold values from 0 to 7
- task_weights: float32 [4], P('task'), may hold values from 0.5 to 2
- query_weight: bfloat16 [768, 768], replicated, may hold values from -0.21875 to 0.21875
- key_weight: bfloat16 [768, 768], replicated, may hold values from -0.21875 to 0.21875
- value_weight: bfloat16 [768, 768], replicated, may hold values from -0.21875 to 0.21875
- query_bias: bfloat16 [768], replicated, may hold values from -1.5 to 1.5
- value_bias: bfloat16 [768], replicated, may hold values from -1.5 to 1.5
- output_weight: bfloat16 [768, 768], replicated, may hold values from -2.5 to 2.5
- output_bias: bfloat16 [768], replicated, may hold values from -1.5 to 1.5
- norm1_gain: bfloat16 [768], replicated, may hold values from 0.5 to 1.5
- norm1_bias: bfloat16 [768], replicated, may hold values from -1.5 to 1.5
- inner_weight: bfloat16 [768, 3072], replicated, may hold values from -0.21875 to 0.21875
- inner_bias: bfloat16 [3072], replicated, may hold values from -1.5 to 1.5
- outer_weight: bfloat16 [3072, 768], replicated, may hold values from -0.21875 to 0.21875
- outer_bias: bfloat16 [768], replicated, may hold values from -1.5 to 1.5
- norm2_gain: bfloat16 [768], replicated, may hold values from 0.5 to 1.5
- norm2_bias: bfloat16 [768], replicated, may hold values from -1.5 to 1.5
- head_table: bfloat16 [8, 3, 768], replicated, may hold values from -0.625 to 0.625
Outputs:
- block_out: bfloat16 [64, 512, 768], P(('task', 'batch'))
- token_grad: float32 [64, 512, 768], P(('task', 'batch'))
- group_loss: float32 [4], P('task')
- query_weight_grad: float32 [768, 768], P(('task', 'batch'))
- key_weight_grad: float32 [768, 768], P(('task', 'batch'))
- value_weight_grad: float32 [768, 768], P(('task', 'batch'))
- query_bias_grad: float32 [768], P(('task', 'batch'))
- value_bias_grad: float32 [768], P(('task', 'batch'))
- output_weight_grad: float32 [768, 768], P(('task', 'batch'))
- output_bias_grad: float32 [768], P(('task', 'batch'))
- norm1_gain_grad: float32 [768], P(('task', 'batch'))
- norm1_bias_grad: float32 [768], P(('task', 'batch'))
- inner_weight_grad: float32 [768, 3072], P(('task', 'batch'))
- inner_bias_grad: float32 [3072], P(('task', 'batch'))
- outer_weight_grad: float32 [3072, 768], P(('task', 'batch'))
- outer_bias_grad: float32 [768], P(('task', 'batch'))
- norm2_gain_grad: float32 [768], P(('task', 'batch'))
- norm2_bias_grad: float32 [768], P(('task', 'batch'))
- head_table_grad: float32 [8, 3, 768], replicated
Inputs may be any that keep to these rules, and one draw needn't show every extreme that they name: `lengths`: at least one sequence has the full length 512; token 0 of every sequence is inside its length.
All inputs are finite; a program needn't handle non-finite values.
Results may differ from a plain program's by a relative error of at most 0.015.
Values sent between devices are 32-bit elements; how exact they have to be, the bound alone decides.
No kernel may reach another device: no remote copies, remote signals or barrier semaphores. Data moves between devices by JAX's collectives and lax.ppermute only.
A program may use at most 192 MiB of HBM per device.

v0:
```python
import functools

import jax
import jax.numpy as jnp
from jax import lax
from jax.experimental import pallas as pl
from jax.experimental.pallas import tpu as pltpu
from jax.sharding import PartitionSpec as P

HD = 64
TILE = 256
ALL_AXES = ("task", "batch")
NN = (((1,), (0,)), ((), ()))
NT = (((1,), (1,)), ((), ()))
TN = (((0,), (0,)), ((), ()))
half = jnp.bfloat16
single = jnp.float32
eps_norm = 1e-12


def dot(left, right, dims=NN):
    return lax.dot_general(left, right, dims, preferred_element_type=single)


ANY = pl.BlockSpec(memory_space=pl.ANY)
SMEM = pl.BlockSpec(memory_space=pltpu.SMEM)
VMEM = pl.BlockSpec(memory_space=pltpu.VMEM)
HBM = pl.BlockSpec(memory_space=pltpu.HBM)


def near(shape, dtype=single):
    return pltpu.VMEM(shape, dtype)


def off(shape, dtype=single):
    return pltpu.HBM(shape, dtype)


def far(shape, dtype=single):
    return jax.ShapeDtypeStruct(shape, dtype)


COSTS = {
    "attention_back_0": 3000,
    "attention_back_1": 10000,
    "attention_back_2": 30,
    "first_norm_back": 3000,
    "fourth_qkv_stage": 100,
    "fourth_stage_inner": 3000,
    "fourth_stage_outer": 1000,
    "inner_grad": 3000,
    "inner_weight_keep": 1000,
    "inner_weight_send": 10000,
    "last_outer_stage": 3000,
    "last_stage": 300,
    "outer_weight_keep": 3000,
    "outer_weight_send": 1000,
    "qkv_weight_keep": 1000,
    "qkv_weight_send": 1000,
    "second_qkv_stage": 100,
    "second_stage_inner": 10000,
    "second_stage_outer": 3000,
    "sum": 10000,
    "third_outer_stage": 10000,
    "third_qkv_stage": 3000,
    "third_stage": 10000,
    "token_grad": 3000,
}
ORDER = [
    "send_outer",
    "rest_outer",
    "inner_grad",
    "send_inner",
    "keep_outer",
    "first_norm",
    "keep_inner",
    "back_0",
    "second_outer",
    "back_1",
    "second_inner",
    "back_2",
    "third_outer",
    "send_qkv",
    "keep_qkv",
    "third_inner",
    "tokens",
    "fourth_outer",
    "second_qkv",
    "sum_outer",
    "third_qkv",
    "fourth_inner",
    "fourth_qkv",
    "last_inner",
    "last_outer",
    "last_qkv",
]


def call(kernel, name, inputs, outputs, scratch=(), megabytes=7, aliases=None):
    specs = {"v": VMEM, "s": SMEM, "a": ANY, "h": HBM}
    spaces = {"v": pltpu.VMEM, "h": pltpu.HBM}
    arrays = [
        pltpu.with_memory_space_constraint(x, spaces[p]) if p in spaces and (x.ndim > 1 or p == "h") else x for x, p in inputs
    ]
    return pl.pallas_call(
        kernel,
        in_specs=[specs[p] for _, p in inputs],
        out_specs=[specs[p] for _, p in outputs],
        out_shape=[o for o, _ in outputs],
        scratch_shapes=list(scratch),
        input_output_aliases=aliases or {},
        compiler_params=pltpu.CompilerParams(vmem_limit_bytes=megabytes << 20),
        cost_estimate=pl.CostEstimate(flops=COSTS.get(name, 1) * 10**6, bytes_accessed=1024, transcendentals=0),
        name=name,
    )(*arrays)


def at(index, size):
    return pl.ds(pl.multiple_of(index * size, size), size)


def as_row(ref):
    return ref[...].astype(single).reshape(1, -1)


def pair_operands(q, k, parity, dead, scale):
    rows = q.shape[0]
    lane = lax.broadcasted_iota(jnp.int32, (rows, 128), 1)
    inside = (lane // HD) == parity
    spare = lane == HD * (1 - parity)
    q_one = jnp.where(inside, q.astype(single) * scale, jnp.where(spare, 1.0, 0.0)).astype(half)
    k_one = jnp.where(inside, k.astype(single), jnp.where(spare & dead, -1e30, 0.0)).astype(half)
    return q_one, k_one


def attention_kernel(
    n_ref, x_hbm, wq_hbm, wk_hbm, wv_hbm, bq_hbm, bv_hbm, wo_hbm, wi_hbm, wd_hbm, cot_hbm,
    x_ref, q_hbm, k_hbm, v_hbm, ctx_ref, ctxt_hbm, lse_ref, wo_ref, wi_ref, wd_ref, cot_ref,
    ctxt_ref, q_ref, k_ref, v_ref, wq_ref, wk_ref, wv_ref, bq_vmem, bv_vmem, sems, out_sems, ctxt_sems,
    *, length,
):
    rows, width = x_ref.shape
    sides = [pl.ds(i * (rows // 2), rows // 2) for i in range(2)]
    pairs = (
        (x_hbm.at[sides[0], :], x_ref.at[sides[0], :]), (bq_hbm, bq_vmem), (wq_hbm, wq_ref),
        (x_hbm.at[sides[1], :], x_ref.at[sides[1], :]), (bv_hbm, bv_vmem), (wk_hbm, wk_ref), (wv_hbm, wv_ref),
        (wo_hbm, wo_ref), (wi_hbm, wi_ref), (wd_hbm, wd_ref), (cot_hbm, cot_ref),
    )
    copies = [pltpu.make_async_copy(src, dst, sems.at[i]) for i, (src, dst) in enumerate(pairs)]
    for copy in copies[:7]:
        copy.start()
    zero = jnp.zeros((1, width), single)
    leaving = []
    for i, (waits, w_ref, bias, out, out_hbm) in enumerate((
        ((0, 1, 2), wq_ref, bq_vmem, q_ref, q_hbm),
        ((4, 5), wk_ref, None, k_ref, k_hbm),
        ((6,), wv_ref, bv_vmem, v_ref, v_hbm),
    )):
        for wait in waits:
            copies[wait].wait()
        shift = zero if bias is None else as_row(bias)
        for part, side in enumerate(sides):
            if i == 0 and part == 1:
                copies[3].wait()
            out[side, :] = (dot(x_ref[side, :], w_ref[...]) + shift).astype(half)
        if i == 0:
            for copy in copies[7:]:
                copy.start()
        leaving.append(pltpu.make_async_copy(out, out_hbm, out_sems.at[i]))
        leaving[-1].start()

    quads = width // 256

    @pl.loop(0, (rows // length) * quads)
    def _(step):
        seq, quad = step // quads, step % quads
        tokens, cols = at(seq, length), at(quad, 256)
        dead = lax.broadcasted_iota(jnp.int32, (length, 128), 0) >= n_ref[seq]
        q, k, v = q_ref[tokens, cols], k_ref[tokens, cols], v_ref[tokens, cols]
        vt = v.T
        scores = []
        for h in range(4):
            pair = slice(h // 2 * 128, h // 2 * 128 + 128)
            q_one, k_one = pair_operands(q[:, pair], k[:, pair], h % 2, dead, HD**-0.5)
            scores.append(dot(k_one, q_one, NT))
        weights = []
        for s in scores:
            top = jnp.max(s, axis=0, keepdims=True)
            e = jnp.exp(s - top)
            weights.append((e.astype(half), top, jnp.sum(e, axis=0, keepdims=True)))
        parts = []
        for h, (e, top, total) in enumerate(weights):
            parts.append((dot(vt[h * HD : (h + 1) * HD], e) * (1.0 / total)).astype(half))
            lse_ref[step, h : h + 1, :] = top + jnp.log(total)
        ctxt = jnp.concatenate(parts, axis=0)
        ctxt_ref[cols, tokens] = ctxt
        ctx_ref[tokens, cols] = ctxt.T
        pltpu.make_async_copy(ctxt_ref.at[cols, tokens], ctxt_hbm.at[cols, tokens], ctxt_sems.at[step]).start()

    for step in range((rows // length) * quads):
        seq, quad = step // quads, step % quads
        tokens, cols = pl.ds(seq * length, length), pl.ds(quad * 256, 256)
        pltpu.make_async_copy(ctxt_ref.at[cols, tokens], ctxt_hbm.at[cols, tokens], ctxt_sems.at[step]).wait()
    for copy in copies[7:] + leaving:
        copy.wait()


def attention(tokens, lengths, wq, wk, wv, bq, bv, wo, wi, wd, cot):
    seqs, length, width = tokens.shape
    rows = seqs * length
    flat = (rows, width)
    quads = width // 256
    return call(
        functools.partial(attention_kernel, length=length),
        "attention_forward",
        [(lengths, "s"), (tokens.reshape(flat), "h"), (wq, "h"), (wk, "h"), (wv, "h"), (bq, "h"), (bv, "h")]
        + [(wo, "h"), (wi, "h"), (wd, "h"), (cot.reshape(flat), "h")],
        [(near(flat, half), "v")]
        + [(off(flat, half), "h")] * 3
        + [(near(flat, half), "v"), (off((width, rows), half), "h"), (near((seqs * quads, 8, length)), "v")]
        + [(near(w.shape, half), "v") for w in (wo, wi, wd)]
        + [(near(flat, half), "v")],
        [pltpu.VMEM((width, rows), half)]
        + [pltpu.VMEM(flat, half)] * 3
        + [pltpu.VMEM(w.shape, half) for w in (wq, wk, wv, bq, bv)]
        + [pltpu.SemaphoreType.DMA((11,)), pltpu.SemaphoreType.DMA((3,))]
        + [pltpu.SemaphoreType.DMA((seqs * quads,))],
        20,
    )


def norm_parts(resid):
    center = resid - jnp.mean(resid, axis=-1, keepdims=True)
    inv_root = lax.rsqrt(jnp.mean(center * center, axis=-1, keepdims=True) + eps_norm)
    return center * inv_root, inv_root


def norm_back(grad_out, normed, inv_root, gain):
    scaled = grad_out * gain
    return inv_root * (
        scaled
        - jnp.mean(scaled, axis=-1, keepdims=True)
        - normed * jnp.mean(scaled * normed, axis=-1, keepdims=True)
    )


def gelu_parts(u):
    u = u.astype(half)
    w = u * u
    v = jnp.minimum(w, jnp.asarray(36.0, half))
    p = (v * jnp.asarray(-0.00031594874, half) + jnp.asarray(0.0367987, half)) * v + jnp.asarray(0.79771759, half)
    h = jnp.asarray(0.5, half)
    cdf = h + h * jnp.tanh(u * p)
    bell = jnp.exp2(w * jnp.asarray(-0.72134752, half) - jnp.asarray(1.32574806, half))
    return u * cdf, cdf + u * bell


def column_sum(array):
    return jnp.sum(array, axis=0, keepdims=True)


def middle_kernel(
    task_ref, label_ref, weight_ref, x_ref, ctx_ref, cot_ref, wo_ref, wi_ref, wd_ref,
    bo_ref, g1_ref, b1_ref, bi_ref, bd_ref, g2_ref, b2_ref, head_ref,
    out_hbm, normed1_ref, root1_ref, h1t_ref, act_ref, slope_ref, ddown_ref, sums_ref,
    out_ref, h1_s, hid_s, res_s, sems,
    *, length, group_seqs,
):
    rows, width = x_ref.shape
    ff = wi_ref.shape[1]
    part = 768
    bo, g1, b1, bd, g2, b2 = [as_row(r) for r in (bo_ref, g1_ref, b1_ref, bd_ref, g2_ref, b2_ref)]
    bi = as_row(bi_ref)
    w = weight_ref[0]
    table = head_ref[...].astype(single)
    chosen = lax.broadcasted_iota(jnp.int32, table.shape, 1) == task_ref[0]
    head = jnp.sum(jnp.where(chosen, table, 0.0), axis=1)
    classes = head.shape[0]
    sums_ref[...] = jnp.zeros_like(sums_ref)
    res_s[...] = jnp.zeros_like(res_s)
    tiles = rows // TILE
    per_seq = length // TILE
    pieces = ff // part
    piece = TILE // pieces

    def rows_of(step, k):
        return pl.ds(pl.multiple_of(step * TILE + k * piece, piece), piece)

    def project(step, slot):
        tile = at(step, TILE)
        hid_s[slot] = x_ref[tile, :].astype(single) + dot(ctx_ref[tile, :], wo_ref[...]) + bo

    def norm_first(step, slot, k):
        here, to = slice(k * piece, (k + 1) * piece), rows_of(step, k)
        normed1, root1 = norm_parts(hid_s[slot, here, :])
        normed1_ref[to, :] = normed1.astype(half)
        root1_ref[to, :] = jnp.broadcast_to(root1, (piece, 128))
        hidden1 = normed1 * g1 + b1
        hid_s[slot, here, :] = hidden1
        h1_s[slot, here, :] = hidden1.astype(half)

    def norm_second(step, slot, k, valid):
        here, to = slice(k * piece, (k + 1) * piece), rows_of(step, k)
        normed2, root2 = norm_parts(res_s[slot, here, :])
        final = normed2 * g2 + b2
        low = final.astype(half)
        out_ref[to, :] = low
        d_final = cot_ref[to, :].astype(single) * w
        if k == 0:
            cls = low[0:1].astype(single)
            logits = [jnp.sum(cls * head[c : c + 1], axis=1, keepdims=True) for c in range(classes)]
            top = functools.reduce(jnp.maximum, logits)
            lse = top + jnp.log(sum(jnp.exp(v - top) for v in logits))
            label = label_ref[step // per_seq]
            weight = jnp.where(step % per_seq == 0, w / group_seqs, 0.0)
            picked = sum(jnp.where(label == c, v, 0.0) for c, v in enumerate(logits))
            slopes = [
                (jnp.exp(v - lse) - jnp.where(label == c, 1.0, 0.0)) * weight for c, v in enumerate(logits)
            ]
            d_cls = sum(s * head[c : c + 1] for c, s in enumerate(slopes))
            row = lax.broadcasted_iota(jnp.int32, d_final.shape, 0)
            d_final = d_final + jnp.where(row == 0, d_cls, 0.0)
            for c in range(classes):
                sums_ref[3 + c : 4 + c] += slopes[c] * cls * valid
            sums_ref[7:8] += jnp.broadcast_to((lse - picked) * (weight * valid), cls.shape)
        ddown = norm_back(d_final, normed2, root2, g2).astype(half)
        ddown_ref[to, :] = ddown
        sums_ref[0:1] += column_sum(d_final * normed2) * valid
        sums_ref[1:2] += column_sum(d_final) * valid
        sums_ref[2:3] += column_sum(ddown.astype(single)) * valid

    def leave(step):
        tile = at(step, TILE)
        return pltpu.make_async_copy(out_ref.at[tile, :], out_hbm.at[tile, :], sems.at[step])

    project(0, 0)
    for k in range(pieces):
        norm_first(0, 0, k)
    h1t_ref[:, :TILE] = h1_s[0].T

    @pl.loop(0, tiles)
    def _(step):
        slot = lax.rem(step, 2)
        tile = at(step, TILE)
        later, earlier = jnp.minimum(step + 1, tiles - 1), jnp.maximum(step - 1, 0)
        valid = jnp.where(step > 0, 1.0, 0.0)
        project(later, 1 - slot)
        h1 = h1_s[slot]

        def inner_part(j):
            return dot(h1, wi_ref[:, j : j + part]) + bi[:, j : j + part]

        down = None
        following = inner_part(0)
        for k in range(pieces):
            j = k * part
            inner = following
            if k + 1 < pieces:
                following = inner_part(j + part)
            norm_first(later, 1 - slot, k)
            value, slope = gelu_parts(inner)
            act = value.astype(half)
            act_ref[tile, j : j + part] = act
            slope_ref[tile, j : j + part] = slope.astype(half)
            norm_second(earlier, 1 - slot, k, valid)
            term = dot(act, wd_ref[j : j + part, :])
            down = term if down is None else down + term
        res_s[slot] = hid_s[slot] + down + bd
        h1t_ref[:, at(later, TILE)] = h1_s[1 - slot].T

        @pl.when(step > 0)
        def _():
            leave(earlier).start()

    for k in range(pieces):
        norm_second(tiles - 1, (tiles - 1) % 2, k, 1.0)
    leave(tiles - 1).start()
    for step in range(tiles):
        leave(step).wait()


def middle(x, ctx, cot, length, labels, task_ids, task_weights, wo, wi, wd, vectors, head_table, group_seqs):
    rows, width = x.shape
    ff = wi.shape[1]
    assert head_table.shape[0] <= 4
    flat = (rows, width)
    return call(
        functools.partial(middle_kernel, length=length, group_seqs=group_seqs),
        "middle_forward",
        [(task_ids, "s"), (labels, "s"), (task_weights, "s")]
        + [(a, "v") for a in (x, ctx, cot, wo, wi, wd, *vectors, head_table)],
        [(far(flat, half), "a")]
        + [
            (near(flat, half), "v"),
            (near((rows, 128)), "v"),
            (near((width, rows), half), "v"),
            (near((rows, ff), half), "v"),
            (near((rows, ff), half), "v"),
            (near(flat, half), "v"),
            (near((8, width)), "v"),
        ],
        [pltpu.VMEM(flat, half), pltpu.VMEM((2, TILE, width), half)]
        + [pltpu.VMEM((2, TILE, width), single)] * 2
        + [pltpu.SemaphoreType.DMA((rows // TILE,))],
        14,
    )


def inner_grad_kernel(after_ref, ddown_ref, wd_ref, slope_ref, dinner_ref, bias_ref):
    part = 768

    @pl.loop(0, wd_ref.shape[0] // part)
    def _(j):
        cols = at(j, part)
        d = dot(ddown_ref[...], wd_ref[cols, :], NT) * slope_ref[:, cols].astype(single)
        low = d.astype(half)
        dinner_ref[:, cols] = low
        bias_ref[pl.ds(j, 1), :] = column_sum(low.astype(single))


def inner_grad(after, ddown, wd, slope):
    ff, width = wd.shape
    return call(
        inner_grad_kernel,
        "inner_grad",
        [(after, "a"), (ddown, "v"), (wd, "v"), (slope, "v")],
        [(near(slope.shape, half), "v"), (near((ff // width, width)), "v")],
        aliases={3: 0},
    )


def first_norm_kernel(
    after_ref, dinner_ref, wi_ref, ddown_ref, normed1_ref, root1_ref, wo_ref, g1_ref, x_ref,
    dr1_ref, dattn_ref, dctx_ref, xt_ref, sums_ref,
):
    rows, width = dr1_ref.shape
    g1 = as_row(g1_ref)
    sums_ref[...] = jnp.zeros_like(sums_ref)

    @pl.loop(0, rows // TILE)
    def _(step):
        tile = at(step, TILE)
        normed1 = normed1_ref[tile, :].astype(single)
        dh1 = ddown_ref[tile, :].astype(single) + dot(dinner_ref[tile, :], wi_ref[...], NT)
        dr1 = norm_back(dh1, normed1, root1_ref[tile, 0:1], g1)
        dr1_ref[tile, :] = dr1
        dattn = dr1.astype(half)
        dattn_ref[tile, :] = dattn
        dctx_ref[tile, :] = dot(dattn, wo_ref[...], NT).astype(half)
        xt_ref[:, tile] = x_ref[tile, :].T
        sums_ref[0:1] += column_sum(dh1 * normed1)
        sums_ref[1:2] += column_sum(dh1)
        sums_ref[2:3] += column_sum(dattn.astype(single))


def first_norm(after, dinner, wi, ddown, normed1, root1, wo, g1, x):
    rows, width = ddown.shape
    flat = (rows, width)
    return call(
        first_norm_kernel,
        "first_norm_back",
        [(after, "a")] + [(a, "v") for a in (dinner, wi, ddown, normed1, root1, wo, g1, x)],
        [(near(flat), "v"), (near(flat, half), "v"), (near(flat, half), "v")]
        + [(near((width, rows), half), "v"), (near((8, width)), "v")],
    )


def attention_back_kernel(
    n_ref, after_ref, q_ref, k_ref, v_ref, ctx_ref, dctx_ref, lse_ref, dq_ref, dk_ref, dv_ref, sums_ref,
    *, length, quad,
):
    scale = HD**-0.5
    quads = q_ref.shape[1] // 256
    cols = slice(quad * 256, quad * 256 + 256)
    sums_ref[...] = jnp.zeros_like(sums_ref)

    @pl.loop(0, q_ref.shape[0] // length)
    def _(seq):
        tokens = at(seq, length)
        dead = lax.broadcasted_iota(jnp.int32, (length, 128), 0) >= n_ref[seq]
        low_half = lax.broadcasted_iota(jnp.int32, (length, 128), 1) < HD
        q, k, v, dctx = [r[tokens, cols] for r in (q_ref, k_ref, v_ref, dctx_ref)]
        kt = k.T
        prod_t = (ctx_ref[tokens, cols].astype(single) * dctx.astype(single)).T
        dqt = []
        for pair in range(2):
            side = slice(pair * 128, pair * 128 + 128)
            q_pair, k_pair, v_pair, d_pair = q[:, side], k[:, side], v[:, side], dctx[:, side]
            first = []
            for parity in range(2):
                q_one, k_one = pair_operands(q_pair, k_pair, parity, dead, scale)
                inside = low_half if parity == 0 else ~low_half
                v_one = jnp.where(inside, v_pair.astype(single), 0.0).astype(half)
                first.append((dot(k_one, q_one, NT), dot(v_one, d_pair, NT)))
            dks, dvs = [], []
            for parity, (s, dp) in enumerate(first):
                h = pair * 2 + parity
                p = jnp.exp(s - lse_ref[seq * quads + quad, h : h + 1, :])
                delta = jnp.sum(prod_t[h * HD : (h + 1) * HD], axis=0, keepdims=True)
                ds = (p * (dp - delta)).astype(half)
                dvs.append(dot(p.astype(half), d_pair))
                dks.append(dot(ds, q_pair))
                dqt.append((dot(kt[h * HD : (h + 1) * HD], ds) * scale).astype(half))
            dk_ref[tokens, side] = (jnp.where(low_half, dks[0], dks[1]) * scale).astype(half)
            dv = jnp.where(low_half, dvs[0], dvs[1]).astype(half)
            dv_ref[tokens, side] = dv
            sums_ref[1:2, side] += column_sum(dv.astype(single))
        dq = jnp.concatenate(dqt, axis=0).T
        dq_ref[tokens, :] = dq
        sums_ref[0:1, :] += column_sum(dq.astype(single))


def attention_back(lengths, after, q, k, v, ctx, dctx, lse, length, quad):
    rows = q.shape[0]
    return call(
        functools.partial(attention_back_kernel, length=length, quad=quad),
        f"attention_back_{quad}",
        [(lengths, "s"), (after, "a")] + [(a, "v") for a in (q, k, v, ctx, dctx, lse)],
        [(near((rows, 256), half), "v")] * 3 + [(near((8, 256)), "v")],
    )


def outer_half(me, act_ref, ddown_ref, y):
    part = act_ref.shape[1] // 4
    return dot(act_ref[:, at(2 * y + me, part)], ddown_ref[...], TN)


def outer_send_kernel(pos_ref, after_ref, act_ref, ddown_ref, send_ref, *, other):
    me = 1 - pos_ref[1] if other else pos_ref[1]
    for y in range(2):
        send_ref[y] = outer_half(me, act_ref, ddown_ref, y)


def outer_send(pos, after, act, ddown, other):
    width = ddown.shape[1]
    return call(
        functools.partial(outer_send_kernel, other=other),
        "outer_weight_send" if other else "outer_weight_rest",
        [(pos, "s"), (after, "a"), (act, "v"), (ddown, "v")],
        [(near((2, act.shape[1] // 4, width)), "v")],
    )[0]


def split_x(pos, block, rows, cols, lead, sx, kx, to):
    me = pos[2]
    for z in range(4):
        zero = block[(2 * z) * rows : (2 * z + 1) * rows, cols]
        one = block[(2 * z + 1) * rows : (2 * z + 2) * rows, cols]
        sx[lead + (z, slice(None), to)] = jnp.where(me == 0, one, zero)
        kx[lead + (z, slice(None), to)] = jnp.where(me == 0, zero, one)


def split_z(pos, block, rows, cols, lead, sz, kz, to):
    side = pos[3]
    for x in range(2):
        zs = [block[(2 * z + x) * rows : (2 * z + x + 1) * rows, cols] for z in range(4)]
        for hi, (even, odd) in enumerate(((0, 1), (3, 2))):
            sz[lead + (hi, x, slice(None), to)] = jnp.where(side == 0, zs[odd], zs[even])
            kz[lead + (hi, x, slice(None), to)] = jnp.where(side == 0, zs[even], zs[odd])


def split_y(pos, data, rows, sy, ky, to):
    me = pos[0]
    zero = data[: 8 * rows].reshape(4, 2, rows, data.shape[1])
    one = data[8 * rows :].reshape(4, 2, rows, data.shape[1])
    sy[:, :, :, to] = jnp.where(me == 0, one, zero)
    ky[:, :, :, to] = jnp.where(me == 0, zero, one)


def outer_keep_kernel(
    pos_ref, after_ref, own_ref, got_ref, sx_ref, kx_ref, sy_ref, ky_ref, sz_ref, kz_ref
):
    third = own_ref.shape[2] // 3
    rows = own_ref.shape[1] // 8
    me_y, me_x, side = pos_ref[0], pos_ref[2], pos_ref[3]
    xs, ys, zs = [slice(i * third, (i + 1) * third) for i in range(3)]

    def at_rows(y, z, x, cols):
        begin = (2 * z + x) * rows
        return own_ref[y, begin : begin + rows, cols] + got_ref[y, begin : begin + rows, cols]

    for y in range(2):
        for z in range(4):
            zero, one = at_rows(y, z, 0, xs), at_rows(y, z, 1, xs)
            sx_ref[y, z] = jnp.where(me_x == 0, one, zero)
            kx_ref[y, z] = jnp.where(me_x == 0, zero, one)
        for x in range(2):
            for hi, (even, odd) in enumerate(((0, 1), (3, 2))):
                zero, one = at_rows(y, even, x, zs), at_rows(y, odd, x, zs)
                sz_ref[y, hi, x] = jnp.where(side == 0, one, zero)
                kz_ref[y, hi, x] = jnp.where(side == 0, zero, one)
    for z in range(4):
        for x in range(2):
            zero, one = at_rows(0, z, x, ys), at_rows(1, z, x, ys)
            sy_ref[z, x] = jnp.where(me_y == 0, one, zero)
            ky_ref[z, x] = jnp.where(me_y == 0, zero, one)


def outer_keep(pos, after, own, got):
    width = own.shape[2]
    r, third = own.shape[1] // 8, width // 3
    shapes = [(2, 4, r, third)] * 2 + [(4, 2, r, third)] * 2 + [(2, 2, 2, r, third)] * 2
    return call(
        outer_keep_kernel,
        "outer_weight_keep",
        [(pos, "s"), (after, "a"), (own, "v"), (got, "v")],
        [(near(s), "v") for s in shapes],
    )


def row_half(left_ref, me):
    quarter = left_ref.shape[0] // 4
    return jnp.concatenate([left_ref[at(me, quarter), :], left_ref[at(2 + me, quarter), :]], axis=0)


def inner_send_kernel(pos_ref, after_ref, left_ref, right_ref, send_ref, *, other):
    me = 1 - pos_ref[1] if other else pos_ref[1]
    left = row_half(left_ref, me)
    parts, _, columns = send_ref.shape
    for j in range(parts):
        send_ref[j] = dot(left, right_ref[:, j * columns : (j + 1) * columns])


def inner_send(pos, after, left_t, right, other):
    width = left_t.shape[0]
    return call(
        functools.partial(inner_send_kernel, other=other),
        "inner_weight_send",
        [(pos, "s"), (after, "a"), (left_t, "v"), (right, "v")],
        [(near((2, width // 2, right.shape[1] // 2)), "v")],
    )[0]


def inner_keep_kernel(pos_ref, after_ref, left_ref, right_ref, got_ref, sx_ref, kx_ref, sy_ref, ky_ref):
    left = row_half(left_ref, pos_ref[1])
    count, columns = got_ref.shape[1:]
    rows = count // 16

    def block(j):
        return dot(left, right_ref[:, j * columns : (j + 1) * columns]) + got_ref[j]

    data = block(0)
    for y in range(2):
        sub = slice(y * 8 * rows, (y + 1) * 8 * rows)
        split_x(pos_ref, data[sub], rows, slice(None), (y,), sx_ref, kx_ref, slice(None))
    split_y(pos_ref, block(1), rows, sy_ref, ky_ref, slice(None))


def inner_keep(pos, after, left_t, right, got):
    r = left_t.shape[0] // 32
    wide = right.shape[1] // 2
    shapes = [(2, 4, r, wide)] * 2 + [(4, 2, r, wide)] * 2
    return call(
        inner_keep_kernel,
        "inner_weight_keep",
        [(pos, "s"), (after, "a")] + [(a, "v") for a in (left_t, right, got)],
        [(near(s), "v") for s in shapes],
    )


SMALL = 40


def small_rows(pos_ref, task_ref, sums0, sums1, inner_bias, sums2, classes, tables, out, base):
    quads = len(sums0)
    width = sums1.shape[1]
    lanes = slice(0, width)
    out[base : base + SMALL, :] = jnp.zeros((SMALL, out.shape[1]), single)
    for g in range(quads):
        out[base : base + 2, g * 256 : (g + 1) * 256] = sums0[g][0:2]
    out[base + 2 : base + 5, lanes] = sums1[0:3]
    at_row = base + 5 + inner_bias.shape[0]
    out[base + 5 : at_row, lanes] = inner_bias[...]
    out[at_row : at_row + 3, lanes] = sums2[0:3]
    lane = lax.broadcasted_iota(jnp.int32, (1, width), 1)
    out[at_row + 3 : at_row + 4, lanes] = jnp.where(lane == pos_ref[6], sums2[7:8], 0.0)
    for t in range(tables):
        mine = jnp.where(task_ref[0] == t, 1.0, 0.0)
        first = at_row + 4 + t * classes
        out[first : first + classes, lanes] = sums2[3 : 3 + classes] * mine


def quad_grads(me, left_ref, ctxt_ref, dattn_ref, parts, g):
    left = row_half(left_ref, me)
    pieces = [dot(left, part[...]) for part in parts[3 * g : 3 * g + 3]]
    pieces.append(dot(row_half(ctxt_ref, me), dattn_ref[:, g * 256 : (g + 1) * 256]))
    return pieces


def qkv_send_kernel(pos_ref, task_ref, after_ref, left_ref, ctxt_ref, dattn_ref, *refs, other, classes, tables, quads):
    parts, refs = refs[: 3 * quads], refs[3 * quads :]
    sums0, refs = refs[:quads], refs[quads:]
    sums1, inner_bias, sums2, send_ref = refs
    me = 1 - pos_ref[1] if other else pos_ref[1]
    count = left_ref.shape[0] // 2
    for g in range(quads):
        for t, piece in enumerate(quad_grads(me, left_ref, ctxt_ref, dattn_ref, parts, g)):
            send_ref[g * count : (g + 1) * count, t * 256 : (t + 1) * 256] = piece
    small_rows(pos_ref, task_ref, sums0, sums1, inner_bias, sums2, classes, tables, send_ref, quads * count)


def qkv_send(pos, task_ids, after, xt, ctxt, dattn, parts, sums0, sums1, inner_bias, sums2, classes, tables, other):
    width = xt.shape[0]
    assert 5 + inner_bias.shape[0] + 4 + classes * tables <= SMALL
    return call(
        functools.partial(qkv_send_kernel, other=other, classes=classes, tables=tables, quads=len(sums0)),
        "qkv_weight_send",
        [(pos, "s"), (task_ids, "s"), (after, "a"), (xt, "v"), (ctxt, "v"), (dattn, "v")]
        + [(p, "v") for p in (*parts, *sums0, sums1, inner_bias, sums2)],
        [(near((len(sums0) * (width // 2) + SMALL, 1024)), "v")],
    )[0]


def rows24_from(base, index, r):
    return pl.ds(pl.multiple_of(base + index * r, 8), r)


def rows24(index, r):
    return pl.ds(pl.multiple_of(index * r, 8), r)


def pack(out, row, block):
    r, w = block.shape[0] // 4, block.shape[1]
    for j in range(4):
        out[row : row + r, j * w : (j + 1) * w] = block[j * r : (j + 1) * r]


def third_outer_kernel(pos_ref, after_ref, xk, xr, yk, yr, zk, zr, sent, kept, zs, zn):
    me_x, side = pos_ref[2], pos_ref[3]
    wide = xk.shape[2]
    for hi, (keep, send) in enumerate(((side, 1 - side), (3 - side, 2 + side))):
        sent[hi, :, :wide] = xk[send] + xr[send]
        sent[hi, :, wide:] = yk[send] + yr[send]
        kept[hi, :, :wide] = xk[keep] + xr[keep]
        kept[hi, :, wide:] = yk[keep] + yr[keep]
    r = xk.shape[1] // 4
    for y in range(2):
        pack(zs, y * r, zk[y, 1 - me_x] + zr[y, 1 - me_x])
        pack(zn, y * r, zk[y, me_x] + zr[y, me_x])


def third_outer(pos, after, xk, xr, yk, yr, zk, zr):
    r, wide = xk.shape[1:]
    shapes = [(2, r, 2 * wide)] * 2 + [(r // 2, 4 * wide)] * 2
    return call(
        third_outer_kernel,
        "third_outer_stage",
        [(pos, "s"), (after, "a")] + [(a, "v") for a in (xk, xr, yk, yr, zk, zr)],
        [(near(s), "v") for s in shapes],
    )


def qkv_keep_kernel(pos_ref, after_ref, left_ref, ctxt_ref, dattn_ref, own_ref, got_ref, ozs, *refs):
    *parts, sx, kx, sy, ky, sz, kz, small = refs
    count, width = left_ref.shape[0] // 2, left_ref.shape[0]
    r = width // 32
    me_y, me_c, me_x, side = pos_ref[0], pos_ref[1], pos_ref[2], pos_ref[3]
    total = own_ref[3 * count :, :width] + got_ref[3 * count :, :width]
    small[...] = total
    sx[8 * r : 8 * r + SMALL, :width] = total
    sx[8 * r + SMALL :, :] = ozs[...]

    def grads(g):
        for t, piece in enumerate(quad_grads(me_c, left_ref, ctxt_ref, dattn_ref, parts, g)):
            cols = slice(t * 256, (t + 1) * 256)
            yield cols, piece + got_ref[g * count : (g + 1) * count, cols]

    for cols, g in grads(0):
        for y in range(2):
            for x in range(2):
                zs = [g[(y * 8 + z * 2 + x) * r : (y * 8 + z * 2 + x + 1) * r] for z in range(4)]
                for hi, (even, odd) in enumerate(((0, 1), (3, 2))):
                    begin = ((y * 2 + hi) * 2 + x) * r
                    sz[begin : begin + r, cols] = jnp.where(side == 0, zs[odd], zs[even])
                    kz[begin : begin + r, cols] = jnp.where(side == 0, zs[even], zs[odd])
    for cols, g in grads(1):
        for y in range(2):
            for z in range(4):
                begin = (y * 8 + z * 2) * r
                zero, one = g[begin : begin + r], g[begin + r : begin + 2 * r]
                to = slice((y * 4 + z) * r, (y * 4 + z + 1) * r)
                sx[to, cols] = jnp.where(me_x == 0, one, zero)
                kx[to, cols] = jnp.where(me_x == 0, zero, one)
    for cols, g in grads(2):
        sy[:, cols] = jnp.where(me_y == 0, g[8 * r :], g[: 8 * r])
        ky[:, cols] = jnp.where(me_y == 0, g[: 8 * r], g[8 * r :])


def qkv_keep(pos, after, xt, ctxt, dattn, own, got, ozs, parts):
    width = xt.shape[0]
    r = width // 32
    wide = own.shape[1]
    shapes = [(8 * r + SMALL + 2 * r, wide)] + [(8 * r, wide)] * 5 + [(SMALL, width)]
    return call(
        qkv_keep_kernel,
        "qkv_weight_keep",
        [(pos, "s"), (after, "a")]
        + [(a, "v") for a in (xt, ctxt, dattn, own, got, ozs, *parts)],
        [(near(n), "v") for n in shapes],
    )


def second_qkv_kernel(pos_ref, after_ref, kx, rx, ky, ry, kz, rz, small, oz, xs, xk, ys, yk, zs, zk, small_out, oz_out):
    me_y, me_x, me_hi = pos_ref[0], pos_ref[2], pos_ref[4]
    r, width = kx.shape[0] // 8, small.shape[1]
    total = small[...] + rx[8 * r : 8 * r + SMALL, :width]
    small_out[...] = total
    xs[4 * r : 4 * r + SMALL, :width] = total
    base = 8 * r + SMALL
    xs[4 * r + SMALL :, :] = oz[rows24(1 - me_y, r), :] + rx[rows24_from(base, 1 - me_y, r), :]
    oz_out[...] = oz[rows24(me_y, r), :] + rx[rows24_from(base, me_y, r), :]
    there, here = rows24(1 - me_y, 4 * r), rows24(me_y, 4 * r)
    xs[: 4 * r, :] = kx[there, :] + rx[there, :]
    xk[...] = kx[here, :] + rx[here, :]
    for z in range(4):
        there, here = rows24(2 * z + 1 - me_x, r), rows24(2 * z + me_x, r)
        to = slice(z * r, (z + 1) * r)
        ys[to, :] = ky[there, :] + ry[there, :]
        yk[to, :] = ky[here, :] + ry[here, :]
    for y in range(2):
        there, here = rows24(2 * y + 1 - me_hi, 2 * r), rows24(2 * y + me_hi, 2 * r)
        to = slice(y * 2 * r, (y + 1) * 2 * r)
        zs[to, :] = kz[there, :] + rz[there, :]
        zk[to, :] = kz[here, :] + rz[here, :]


def third_qkv_kernel(pos_ref, after_ref, xk, xr, yk, yr, zk, zr, small, sent, kept, zs, zn, small_out):
    me_x, side = pos_ref[2], pos_ref[3]
    r, width = xk.shape[0] // 4, small.shape[1]
    total = small[...] + xr[4 * r : 4 * r + SMALL, :width]
    small_out[...] = total
    sent[4 * r :, :width] = total
    for i, (k, got) in enumerate(((xk, xr), (yk, yr))):
        for hi, (keep, send) in enumerate(((side, 1 - side), (3 - side, 2 + side))):
            there, here = rows24(send, r), rows24(keep, r)
            to = slice((2 * i + hi) * r, (2 * i + hi + 1) * r)
            sent[to, :] = k[there, :] + got[there, :]
            kept[to, :] = k[here, :] + got[here, :]
    for y in range(2):
        there, here = rows24(2 * y + 1 - me_x, r), rows24(2 * y + me_x, r)
        to = slice(y * r, (y + 1) * r)
        zs[to, :] = zk[there, :] + zr[there, :]
        zn[to, :] = zk[here, :] + zr[here, :]


def fourth_qkv_kernel(pos_ref, after_ref, k, got, zk, zr, small, sent, kept, zs, zn, small_out):
    me_y, me_hi = pos_ref[0], pos_ref[4]
    r, width = k.shape[0] // 4, small.shape[1]
    total = small[...] + got[4 * r :, :width]
    small_out[...] = total
    sent[2 * r :, :width] = total
    for i in range(2):
        there, here = rows24(2 * i + 1 - me_hi, r), rows24(2 * i + me_hi, r)
        to = slice(i * r, (i + 1) * r)
        sent[to, :] = k[there, :] + got[there, :]
        kept[to, :] = k[here, :] + got[here, :]
    there, here = rows24(1 - me_y, r), rows24(me_y, r)
    zs[...] = zk[there, :] + zr[there, :]
    zn[...] = zk[here, :] + zr[here, :]


def qkv_stage(kernel, name, pos, after, arrays, counts, width):
    wide = arrays[0].shape[1]
    return call(
        kernel,
        name,
        [(pos, "s"), (after, "a")] + [(a, "v") for a in arrays],
        [(near((n, width if n == SMALL else wide)), "v") for n in counts],
    )


def add_kernel(after_ref, a, b, out):
    out[...] = a[...] + b[...]


def sum_kernel(after, a, b):
    return call(add_kernel, "sum", [(after, "a"), (a, "v"), (b, "v")], [(near(a.shape), "v")])[0]


def last_outer_kernel(after_ref, xy, zk, zr, out, done):
    done[...] = jnp.zeros_like(done)
    wide = xy.shape[1]
    out[:, :wide] = xy[...]
    r = zk.shape[0]
    z = zk[...] + zr[4 * r + SMALL :, :]
    w = z.shape[1] // 4
    for j in range(4):
        out[j * r : (j + 1) * r, wide:] = z[:, j * w : (j + 1) * w]


def last_outer(after, xy, zk, zr):
    shape = (xy.shape[0], xy.shape[1] + zk.shape[1] // 4)
    return call(
        last_outer_kernel,
        "last_outer_stage",
        [(after, "a")] + [(a, "v") for a in (xy, zk, zr)],
        [(far(shape), "v"), (near((8, 128)), "v")],
    )


def last_qkv_kernel(pos_ref, k, got, zk, zr, small, q_out, k_out, v_out, o_out, *outs, classes, bias_rows):
    *vectors, inner_out, loss_out, head_out = outs
    r = zk.shape[0]
    width = small.shape[1]
    xs = k[:r, :] + got[:r, :]
    ys = k[r:, :] + got[r : 2 * r, :]
    zs = zk[...] + zr[...]
    for t, out in enumerate((q_out, k_out, v_out, o_out)):
        for g, data in enumerate((zs, xs, ys)):
            out[:, g * 256 : (g + 1) * 256] = data[:, t * 256 : (t + 1) * 256]
    total = small[...] + got[2 * r :, :width]
    me = pos_ref[5]
    rolled = pltpu.roll(total, lax.rem(width - me * r, width), 1)
    after = 5 + bias_rows
    for out, row in zip(vectors, (0, 1, 2, 3, 4, after, after + 1, after + 2)):
        out[...] = rolled[row : row + 1, :r]
    part = inner_out.shape[1]
    per_row = width // part
    row = lax.broadcasted_iota(jnp.int32, total.shape, 0)
    one = jnp.sum(jnp.where(row == 5 + me // per_row, total, 0.0), axis=0, keepdims=True)
    one = jnp.broadcast_to(one, (8, width))
    inner_out[...] = pltpu.roll(one, lax.rem(width - (me % per_row) * part, width), 1)[0:1, :part]
    lane = lax.broadcasted_iota(jnp.int32, (1, width), 1)
    loss_row = total[after + 3 : after + 4]
    loss_out[...] = jnp.sum(jnp.where(lane == pos_ref[6], loss_row, 0.0), axis=1, keepdims=True)
    for t in range(head_out.shape[0]):
        first = after + 4 + t * classes
        head_out[t] = total[first : first + classes]


def last_qkv(pos, k, got, zk, zr, small, classes, tables, bias_rows):
    r, width = zk.shape[0], small.shape[1]
    shapes = [(r, width)] * 4 + [(1, r)] * 8 + [(1, r * bias_rows), (1, 1), (tables, classes, width)]
    return call(
        functools.partial(last_qkv_kernel, classes=classes, bias_rows=bias_rows),
        "last_qkv_stage",
        [(pos, "s")] + [(a, "v") for a in (k, got, zk, zr, small)],
        [(far(s), "v") for s in shapes],
    )


def token_grad_kernel(after_ref, dr1_ref, wq_ref, wk_ref, wv_ref, *refs):
    *parts, out_hbm, done_ref, out_ref, sems = refs
    done_ref[...] = jnp.zeros_like(done_ref)
    rows = out_ref.shape[0]
    quads = len(parts) // 3

    @pl.loop(0, rows // TILE)
    def _(step):
        tile = at(step, TILE)
        total = dr1_ref[tile, :]
        for t, w_ref in enumerate((wq_ref, wk_ref, wv_ref)):
            d = jnp.concatenate([parts[g * 3 + t][tile, :] for g in range(quads)], axis=1)
            total = total + dot(d, w_ref[...], NT)
        out_ref[tile, :] = total
        pltpu.make_async_copy(out_ref.at[tile, :], out_hbm.at[tile, :], sems.at[step]).start()

    for i in range(rows // TILE):
        tile = pl.ds(i * TILE, TILE)
        pltpu.make_async_copy(out_ref.at[tile, :], out_hbm.at[tile, :], sems.at[i]).wait()


def token_grads(after, dr1, wq, wk, wv, parts):
    rows, width = dr1.shape
    return call(
        token_grad_kernel,
        "token_grad",
        [(after, "a")] + [(a, "v") for a in (dr1, wq, wk, wv, *parts)],
        [(far((rows, width)), "a"), (near((8, 128)), "v")],
        [pltpu.VMEM((rows, width), single), pltpu.SemaphoreType.DMA((rows // TILE,))],
    )


def second_kernel(pos_ref, after_ref, kx, rx, ky, ry, *refs):
    me_y, me_x, me_hi = pos_ref[0], pos_ref[2], pos_ref[4]
    outs = refs[len(refs) % 4 :] if len(refs) == 4 else refs[2:]
    xs, xk, ys, yk = outs[:4]
    xs[...] = kx[1 - me_y] + rx[1 - me_y]
    xk[...] = kx[me_y] + rx[me_y]
    ys[...] = ky[:, 1 - me_x] + ry[:, 1 - me_x]
    yk[...] = ky[:, me_x] + ry[:, me_x]
    if len(refs) > 4:
        kz, rz = refs[:2]
        zs, zk = outs[4:]
        zs[...] = kz[:, 1 - me_hi] + rz[:, 1 - me_hi]
        zk[...] = kz[:, me_hi] + rz[:, me_hi]


def second(tag, pos, after, kx, rx, ky, ry, kz=None, rz=None):
    flat = (4,) + kx.shape[2:]
    inputs = [kx, rx, ky, ry]
    shapes = [flat] * 4
    if kz is not None:
        inputs += [kz, rz]
        shapes += [(2, 2) + kz.shape[3:]] * 2
    return call(
        second_kernel,
        f"second_stage_{tag}",
        [(pos, "s"), (after, "a")] + [(a, "v") for a in inputs],
        [(near(s), "v") for s in shapes],
    )


def third_kernel(pos_ref, after_ref, xk, xr, yk, yr, *refs):
    me_x, side = pos_ref[2], pos_ref[3]
    wide = xk.shape[2]
    if len(refs) == 2:
        sent, kept = refs
    else:
        zk, zr, sent, kept, zs, zn = refs
        zs[...] = zk[:, 1 - me_x] + zr[:, 1 - me_x]
        zn[...] = zk[:, me_x] + zr[:, me_x]
    for hi, (keep, send) in enumerate(((side, 1 - side), (3 - side, 2 + side))):
        sent[hi, :, :wide] = xk[send] + xr[send]
        sent[hi, :, wide:] = yk[send] + yr[send]
        kept[hi, :, :wide] = xk[keep] + xr[keep]
        kept[hi, :, wide:] = yk[keep] + yr[keep]


def third(pos, after, xk, xr, yk, yr, zk=None, zr=None):
    r, wide = xk.shape[1:]
    inputs = [xk, xr, yk, yr]
    shapes = [(2, r, 2 * wide)] * 2
    if zk is not None:
        inputs += [zk, zr]
        shapes += [(2,) + zk.shape[2:]] * 2
    return call(
        third_kernel,
        "third_stage",
        [(pos, "s"), (after, "a")] + [(a, "v") for a in inputs],
        [(near(s), "v") for s in shapes],
    )


def fourth_kernel(pos_ref, after_ref, xyk, xyr, *refs):
    me_y, me_hi = pos_ref[0], pos_ref[4]
    if len(refs) == 2:
        sent, kept = refs
    else:
        zk, zr, sent, kept, zs, zn = refs
        zs[...] = zk[1 - me_y] + zr[1 - me_y]
        zn[...] = zk[me_y] + zr[me_y]
    sent[...] = xyk[1 - me_hi] + xyr[1 - me_hi]
    kept[...] = xyk[me_hi] + xyr[me_hi]


def fourth(tag, pos, after, xyk, xyr):
    return call(
        fourth_kernel,
        f"fourth_stage_{tag}",
        [(pos, "s"), (after, "a"), (xyk, "v"), (xyr, "v")],
        [(near(xyk.shape[1:]), "v")] * 2,
    )


def last_kernel(after_ref, xyk, xyr, *refs, layout):
    count = len(layout)
    outs = refs[-count - 1 : -1]
    refs[-1][...] = jnp.zeros_like(refs[-1])
    sources = [(xyk, xyr), refs[:2]]
    for out, pieces in zip(outs, layout):
        to = 0
        for source, begin, end in pieces:
            a, b = sources[source]
            out[:, to : to + end - begin] = a[:, begin:end] + b[:, begin:end]
            to += end - begin


def last(after, xyk, xyr, zk, zr, layout):
    inputs = [xyk, xyr] + ([] if zk is None else [zk, zr])
    shapes = [(xyk.shape[0], sum(e - b for _, b, e in pieces)) for pieces in layout]
    return call(
        functools.partial(last_kernel, layout=layout),
        "last_stage",
        [(after, "a")] + [(a, "v") for a in inputs],
        [(far(s), "v") for s in shapes] + [(near((8, 128)), "v")],
    )


def pair_list(change):
    pairs = []
    for y in range(2):
        for c in range(2):
            for z in range(4):
                for x in range(2):
                    py, pc, pz, px = change(y, c, z, x)
                    pairs.append((((y * 2 + c) * 4 + z) * 2 + x, ((py * 2 + pc) * 4 + pz) * 2 + px))
    return pairs


PAIRS = {
    "y": pair_list(lambda y, c, z, x: (1 - y, c, z, x)),
    "c": pair_list(lambda y, c, z, x: (y, 1 - c, z, x)),
    "x": pair_list(lambda y, c, z, x: (y, c, z, 1 - x)),
    "near": pair_list(lambda y, c, z, x: (y, c, z ^ 1, x)),
    "far": pair_list(lambda y, c, z, x: (y, c, 3 - z, x)),
}


def swap(array, name):
    return lax.ppermute(array, ALL_AXES, PAIRS[name])


def per_device(
    tokens,
    out_cot,
    lengths,
    labels,
    task_ids,
    task_weights,
    query_weight,
    key_weight,
    value_weight,
    query_bias,
    value_bias,
    output_weight,
    output_bias,
    norm1_gain,
    norm1_bias,
    inner_weight,
    inner_bias,
    outer_weight,
    outer_bias,
    norm2_gain,
    norm2_bias,
    head_table,
    *,
    staged,
):
    seqs, length, width = tokens.shape
    rows = seqs * length
    ff = inner_weight.shape[1]
    group_seqs = seqs * lax.axis_size("batch")
    task_index = lax.axis_index("task")
    batch_index = lax.axis_index("batch")
    my_y, my_c, my_z, my_x = task_index // 2, task_index % 2, batch_index // 2, batch_index % 2
    my_hi = my_z // 2
    my_side = (my_z // 2) ^ (my_z % 2)
    where = task_index * lax.axis_size("batch") + batch_index
    pos = jnp.stack([my_y, my_c, my_x, my_side, my_hi, where, task_index]).astype(jnp.int32)
    vectors = (output_bias, norm1_gain, norm1_bias, inner_bias, outer_bias, norm2_gain, norm2_bias)

    x, q, k, v, ctx, ctxt, lse, wo, wi, wd, cot = attention(
        tokens,
        lengths,
        query_weight,
        key_weight,
        value_weight,
        query_bias,
        value_bias,
        output_weight,
        inner_weight,
        outer_weight,
        out_cot,
    )
    block_out, normed1, root1, h1t, act, slope, ddown, sums2 = middle(
        x, ctx, cot, length, labels, task_ids, task_weights, wo, wi, wd, vectors, head_table.transpose(1, 0, 2), group_seqs
    )
    block_out = block_out.reshape(tokens.shape)

    classes, tables = head_table.shape[1], head_table.shape[0]
    f2, r, quads = ff // 2, width // 32, width // 256
    parts, sums0 = [None] * (3 * quads), [None] * quads

    def back(quad, after):
        *grads, sums = attention_back(lengths, after, q, k, v, ctx, e["dctx"], lse, length, quad)
        parts[3 * quad : 3 * quad + 3] = grads
        sums0[quad] = sums
        return sums

    def small_args():
        return (ctxt, e["dattn"], parts, sums0, e["sums1"], e["inner_bias"], sums2, classes, tables)

    e = {}

    def send_outer(after):
        e["o_send"] = outer_send(pos, after, act, ddown, True)
        return e["o_send"]

    def rest_outer(after):
        e["o_rest"] = outer_send(pos, after, act, ddown, False)
        return e["o_rest"]

    def do_inner_grad(after):
        e["dinner"], e["inner_bias"] = inner_grad(after, ddown, wd, slope)
        return e["inner_bias"]

    def send_inner(after):
        e["i_send"] = inner_send(pos, after, h1t, e["dinner"], True)
        return e["i_send"]

    def do_first_norm(after):
        e["dr1"], e["dattn"], e["dctx"], e["xt"], e["sums1"] = first_norm(
            after,
            e["dinner"],
            inner_weight,
            ddown,
            normed1,
            root1,
            output_weight,
            norm1_gain,
            tokens.reshape(rows, width),
        )
        return e["sums1"]

    def do_tokens(after):
        e["token_grad"], after = token_grads(after, e["dr1"], query_weight, key_weight, value_weight, parts)
        return after

    def send_qkv(after):
        e["qkv_s"] = qkv_send(pos, task_ids, after, e["xt"], *small_args(), True)
        return e["qkv_s"]

    def keep_outer(after):
        osx, okx, osy, oky, osz, okz = outer_keep(pos, after, e["o_rest"], swap(e["o_send"], "c"))
        e["o1"] = (okx, swap(osx, "x"), oky, swap(osy, "y"), okz, swap(osz, "near"))
        return okx

    def keep_inner(after):
        isx, ikx, isy, iky = inner_keep(pos, after, h1t, e["dinner"], swap(e["i_send"], "c"))
        e["i1"] = (ikx, swap(isx, "x"), iky, swap(isy, "y"))
        return ikx

    def second_outer(after):
        xs, xk, ys, yk, zs, zk = second("outer", pos, after, *e["o1"])
        e["o2"] = (xk, swap(xs, "y"), yk, swap(ys, "x"), zk, swap(zs, "far"))
        return xk

    def second_inner(after):
        xs, xk, ys, yk = second("inner", pos, after, *e["i1"])
        e["i2"] = (xk, swap(xs, "y"), yk, swap(ys, "x"))
        return xk

    def do_third_outer(after):
        sent, kept, e["ozs"], e["oz"] = third_outer(pos, after, *e["o2"])
        e["o3"] = (kept, swap(sent, "near"))
        return kept

    def third_inner(after):
        sent, kept = third(pos, after, *e["i2"])
        e["i3"] = (kept, swap(sent, "near"))
        return kept

    def fourth_outer(after):
        sent, kept = fourth("outer", pos, after, *e["o3"])
        e["o4"] = (kept, swap(sent, "far"))
        return kept

    def fourth_inner(after):
        sent, kept = fourth("inner", pos, after, *e["i3"])
        e["i4"] = (kept, swap(sent, "far"))
        return kept

    def sum_outer(after):
        e["outer_xy"] = sum_kernel(after, *e["o4"])
        return e["outer_xy"]

    def last_inner(after):
        e["inner_s"], after = last(after, *e["i4"], None, None, (((0, 0, 2 * f2),),))
        return after

    def do_last_outer(after):
        e["outer_s"], after = last_outer(after, e["outer_xy"], e["oz2"], e["q2"][1])
        return after

    def keep_qkv(after):
        sx, kx, sy, ky, sz, kz, small = qkv_keep(
            pos, after, e["xt"], ctxt, e["dattn"], e["qkv_s"], swap(e["qkv_s"], "c"), e["ozs"], parts
        )
        e["q1"] = (kx, swap(sx, "x"), ky, swap(sy, "y"), kz, swap(sz, "near"), small, e["oz"])
        return small

    def stage(kernel, name, after, arrays, counts):
        return qkv_stage(kernel, name, pos, after, arrays, counts, width)

    def second_qkv(after):
        xs, xk, ys, yk, zs, zk, small, e["oz2"] = stage(
            second_qkv_kernel,
            "second_qkv_stage",
            after,
            e["q1"],
            [5 * r + SMALL, 4 * r, 4 * r, 4 * r, 4 * r, 4 * r, SMALL, r],
        )
        e["q2"] = (xk, swap(xs, "y"), yk, swap(ys, "x"), zk, swap(zs, "far"), small)
        return small

    def third_qkv(after):
        sent, kept, zs, zk, small = stage(
            third_qkv_kernel, "third_qkv_stage", after, e["q2"], [4 * r + SMALL, 4 * r, 2 * r, 2 * r, SMALL]
        )
        e["q3"] = (kept, swap(sent, "near"), zk, swap(zs, "x"), small)
        return small

    def fourth_qkv(after):
        sent, kept, zs, zk, small = stage(
            fourth_qkv_kernel, "fourth_qkv_stage", after, e["q3"], [2 * r + SMALL, 2 * r, r, r, SMALL]
        )
        e["q4"] = (kept, swap(sent, "far"), zk, swap(zs, "y"), small)
        return small

    def do_last_qkv(after):
        e["last"] = last_qkv(pos, *e["q4"], classes, tables, ff // width)
        return after

    steps = {
        "send_outer": send_outer,
        "rest_outer": rest_outer,
        "inner_grad": do_inner_grad,
        "send_inner": send_inner,
        "keep_outer": keep_outer,
        "first_norm": do_first_norm,
        "keep_inner": keep_inner,
        "second_outer": second_outer,
        "send_qkv": send_qkv,
        "second_inner": second_inner,
        "third_outer": do_third_outer,
        "keep_qkv": keep_qkv,
        "third_inner": third_inner,
        "tokens": do_tokens,
        "fourth_outer": fourth_outer,
        "second_qkv": second_qkv,
        "sum_outer": sum_outer,
        "third_qkv": third_qkv,
        "fourth_inner": fourth_inner,
        "fourth_qkv": fourth_qkv,
        "last_inner": last_inner,
        "last_outer": do_last_outer,
        "last_qkv": do_last_qkv,
    }
    for quad in range(quads):
        steps[f"back_{quad}"] = functools.partial(back, quad)
    if staged:
        after = sums2
        for name in ORDER:
            after = steps[name](after)
        query_s, key_s, value_s, output_s, *rest = e["last"]
        inner_s, outer_s = e["inner_s"], e["outer_s"]
        vector_s = [v.reshape(-1) for v in rest[:-1]]
        head_grad = rest[-1]
    else:
        after = do_first_norm(send_inner(do_inner_grad(send_outer(sums2))))
        o_keep = rest_outer(after)
        i_keep = inner_send(pos, after, h1t, e["dinner"], False)
        for quad in range(quads):
            after = back(quad, after)
        after = do_tokens(send_qkv(after))
        qkv_k = qkv_send(pos, task_ids, after, e["xt"], *small_args(), False)
        o_send, i_send, qkv_s = e["o_send"], e["i_send"], e["qkv_s"]

        def whole_rows(sent, kept):
            both = jnp.stack([jnp.where(my_c == 0, kept, sent), jnp.where(my_c == 0, sent, kept)], axis=1)
            return both.reshape(-1, both.shape[-1])

        def scatter(grad):
            return lax.psum_scatter(grad, ALL_AXES, scatter_dimension=0, tiled=True)

        def by_rows(array):
            return array.reshape(2, -1, array.shape[-1])

        outer_s = scatter(whole_rows(o_send, o_keep))
        inner_s = scatter(
            jnp.concatenate([whole_rows(by_rows(i_send[j]), by_rows(i_keep[j])) for j in range(2)], axis=-1)
        )
        count = width // 2

        def tensor(array, t):
            cols = slice(t * 256, (t + 1) * 256)
            return by_rows(jnp.concatenate([array[g * count : (g + 1) * count, cols] for g in range(quads)], axis=1))

        query_s, key_s, value_s, output_s = [
            scatter(whole_rows(tensor(qkv_s, t), tensor(qkv_k, t))) for t in range(4)
        ]
        small = lax.psum(qkv_s[quads * count :, :width], ALL_AXES)
        devices = lax.axis_size("task") * lax.axis_size("batch")

        def mine(array):
            flat = array.reshape(-1)
            size = flat.shape[0] // devices
            return lax.dynamic_slice(flat, (where * size,), (size,))

        last_row = 5 + ff // width
        vector_s = [mine(small[i]) for i in (0, 1, 2, 3, 4, last_row, last_row + 1, last_row + 2)]
        vector_s.append(mine(small[5:last_row]))
        vector_s.append(lax.dynamic_slice(small, (last_row + 3, task_index), (1, 1)).reshape(1))
        head_grad = small[last_row + 4 : last_row + 4 + classes * tables].reshape(head_table.shape)
    token_grad = e["token_grad"].reshape(tokens.shape)
    bias_q, bias_v, gain1, bias1, bias_o, gain2, bias2, bias_d, bias_i, loss = vector_s
    return (
        block_out,
        token_grad,
        loss,
        query_s,
        key_s,
        value_s,
        bias_q,
        bias_v,
        output_s,
        bias_o,
        gain1,
        bias1,
        inner_s,
        bias_i,
        outer_s,
        bias_d,
        gain2,
        bias2,
        head_grad,
    )


def solution(mesh):
    rows = P(ALL_AXES)
    plain = P()
    task = P("task")
    staged = mesh.shape["task"] == 4 and mesh.shape["batch"] == 8
    return jax.shard_map(
        functools.partial(per_device, staged=staged),
        mesh=mesh,
        in_specs=(rows, rows, rows, rows, task, task) + (plain,) * 16,
        out_specs=(rows, rows, task) + (rows,) * 15 + (plain,),
        check_vma=False,
    )
```

profile of v0, /device:TPU:8, one launch (start us, length us, event | category | flops | bytes accessed | tf_op | source)
XLA Modules:
  0.0 218.9 jit_solution(2139443434920388557)
XLA Ops:
  2.8 18.0 %attention_forward.1 = (bf16[1024,768]{1,0:T(8,128)(2,1)S(1)}, bf16[1024,768]{1,0:T(8,128)(2,1)}, bf16[1024,768]{1,0:T(8,128)(2,1)}, bf16[1024,768]{1,0:T(8,128)...) custom-call(s32[2]{0:T(128)S(1)} %copy-done.21, ...), custom_call_target="tpu_custom_call" | custom-call | flops 1000000 | bytes 1024 | tf_op jit(solution)/shard_map/attention_forward/pallas_call | solution.py:105
  20.9 19.6 %middle_forward.1 = (bf16[1024,768]{1,0:T(8,128)(2,1)}, bf16[1024,768]{1,0:T(8,128)(2,1)S(1)}, f32[1024,128]{1,0:T(8,128)S(1)}, bf16[768,1024]{1,0:T(8,128)(2,1)...) custom-call(s32[1]{0:T(128)S(6)} %copy.44.task_ref, ...), custom_call_target="tpu_custom_call" | custom-call | flops 1000000 | bytes 1024 | tf_op jit(solution)/shard_map/middle_forward/pallas_call | solution.py:105
  41.6 3.2 %outer_weight_send.1.after_ref = f32[2,768,768]{2,1,0:T(8,128)S(1)} custom-call(s32[7]{0:T(128)S(1)} %stack.31.pos_ref, f32[8,768]{1,0:T(8,128)S(1)} %get-tuple-element.139.after_ref.refs_14_, bf16[1024,3072]{1,0:T(8,128)(2,1)S(1)} %get-tuple-element.140.act_ref, bf16[1024,768]{1,0:T(8,128)(2,1)S(1)} %get-tuple-element.141.ddown_ref), custom_call_target="tpu_custom_call" | custom-call | flops 1000000000 | bytes 1024 | tf_op jit(solution)/shard_map/outer_weight_send/pallas_call | solution.py:105
  44.9 3.2 %outer_weight_rest.1.after_ref.own_ref = f32[2,768,768]{2,1,0:T(8,128)S(1)} custom-call(s32[7]{0:T(128)S(1)} %stack.31.pos_ref, f32[2,768,768]{2,1,0:T(8,128)S(1)} %outer_weight_send.1.after_ref, bf16[1024,3072]{1,0:T(8,128)(2,1)S(1)} %get-tuple-element.140.act_ref, bf16[1024,768]{1,0:T(8,128)(2,1)S(1)} %get-tuple-element.141.ddown_ref), custom_call_target="tpu_custom_call" | custom-call | flops 1000000 | bytes 1024 | tf_op jit(solution)/shard_map/outer_weight_rest/pallas_call | solution.py:105
  48.1 6.9 %inner_grad.1 = (bf16[1024,3072]{1,0:T(8,128)(2,1)S(1)}, f32[4,768]{1,0:T(4,128)S(1)}) custom-call(f32[2,768,768]{2,1,0:T(8,128)S(1)} %outer_weight_rest.1.after_ref.own_ref, bf16[1024,768]{1,0:T(8,128)(2,1)S(1)} %get-tuple-element.141.ddown_ref, bf16[3072,768]{1,0:T(8,128)(2,1)S(1)} %get-tuple-element.137.wd_ref, ...), custom_call_target="tpu_custom_call", output_to_operand_aliasing={{0}: (3, {})} | custom-call | flops 3000000000 | bytes 1024 | tf_op jit(solution)/shard_map/inner_grad/pallas_call | solution.py:105
  55.0 3.2 %inner_weight_send.1.after_ref = f32[2,384,1536]{2,1,0:T(8,128)S(1)} custom-call(s32[7]{0:T(128)S(1)} %stack.31.pos_ref, f32[4,768]{1,0:T(4,128)S(1)} %get-tuple-element.143.after_ref.refs_13_, bf16[768,1024]{1,0:T(8,128)(2,1)S(1)} %get-tuple-element.144.left_ref, bf16[1024,3072]{1,0:T(8,128)(2,1)S(1)} %get-tuple-element.145.right_ref.dinner_ref), custom_call_target="tpu_custom_call" | custom-call | flops 10000000000 | bytes 1024 | tf_op jit(solution)/shard_map/inner_weight_send/pallas_call | solution.py:105
  63.5 10.6 %first_norm_back.1 = (f32[1024,768]{1,0:T(8,128)S(1)}, bf16[1024,768]{1,0:T(8,128)(2,1)S(1)}, bf16[1024,768]{1,0:T(8,128)(2,1)S(1)}, bf16[768,1024]{1,0:T(8,128)(2,1)S(1)}, f32[8,768]{1,0:T(8,128)S(1)}) custom-call(f32[2,4,96,256]{3,2,1,0:T(8,128)S(1)} %get-tuple-element.146.after_ref.kx, bf16[1024,3072]{1,0:T(8,128)(2,1)S(1)} %get-tuple-element.145.right_ref.dinner_ref, ...), custom_call_target="tpu_custom_call" | custom-call | flops 3000000000 | bytes 1024 | tf_op jit(solution)/shard_map/first_norm_back/pallas_call | solution.py:105
  74.2 3.2 %inner_weight_keep.1 = (f32[2,4,24,1536]{3,2,1,0:T(8,128)S(1)}, f32[2,4,24,1536]{3,2,1,0:T(8,128)S(1)}, f32[4,2,24,1536]{3,2,1,0:T(8,128)S(1)}, f32[4,2,24,1536]{3,2,1,0:T(8,128)S(1)}) custom-call(s32[7]{0:T(128)S(1)} %stack.31.pos_ref, f32[8,768]{1,0:T(8,128)S(1)} %get-tuple-element.149.after_ref.refs_12_, bf16[768,1024]{1,0:T(8,128)(2,1)S(1)} %copy-done.12, ...), custom_call_target="tpu_custom_call" | custom-call | flops 1000000000 | bytes 1024 | tf_op jit(solution)/shard_map/inner_weight_keep/pallas_call | solution.py:105
  78.1 6.4 %attention_back_0.1 = (bf16[1024,256]{1,0:T(8,128)(2,1)S(1)}, bf16[1024,256]{1,0:T(8,128)(2,1)S(1)}, bf16[1024,256]{1,0:T(8,128)(2,1)S(1)}, f32[8,256]{1,0:T(8,128)S(1)}) custom-call(s32[2]{0:T(128)S(1)} %copy-done.22, f32[2,4,24,1536]{3,2,1,0:T(8,128)S(1)} %get-tuple-element.150.after_ref.kx, bf16[1024,768]{1,0:T(8,128)(2,1)S(1)} %copy-done.6, ...), custom_call_target="tpu_custom_call" | custom-call | flops 3000000000 | bytes 1024 | tf_op jit(solution)/shard_map/attention_back_0/pallas_call | solution.py:105
  85.3 2.0 collective-permute-start.7
  88.8 2.7 %collective-permute-start.9 = (f32[2,2,96,256]{3,2,1,0:T(8,128)S(1)}, f32[2,2,96,256]{3,2,1,0:T(8,128)S(1)}, u32[]{:S(2)}, u32[]{:S(2)}) collective-permute-start(f32[2,2,96,256]{3,2,1,0:T(8,128)S(1)} %get-tuple-element.173), channel_id=1, source_target_pairs={{0,6},{1,7},{2,4},{3,5},{4,2},{5,3},{6,0},{7,1},{8,14},{9,15},{10,... | collective-permute-start | bytes 1179656 | tf_op jit(solution)/shard_map/ppermute | solution.py:1101
  91.5 6.6 %attention_back_1.1 = (bf16[1024,256]{1,0:T(8,128)(2,1)S(1)}, bf16[1024,256]{1,0:T(8,128)(2,1)S(1)}, bf16[1024,256]{1,0:T(8,128)(2,1)S(1)}, f32[8,256]{1,0:T(8,128)S(1)}) custom-call(s32[2]{0:T(128)S(1)} %copy-done.22, f32[4,96,256]{2,1,0:T(8,128)S(1)} %get-tuple-element.162.after_ref.xk, bf16[1024,768]{1,0:T(8,128)(2,1)S(1)} %copy-done.6, ...), custom_call_target="tpu_custom_call" | custom-call | flops 10000000000 | bytes 1024 | tf_op jit(solution)/shard_map/attention_back_1/pallas_call | solution.py:105
  98.1 8.3 %collective-permute-done.5.rx = f32[2,4,24,1536]{3,2,1,0:T(8,128)S(1)} collective-permute-done((f32[2,4,24,1536]{3,2,1,0:T(8,128)S(1)}, f32[2,4,24,1536]{3,2,1,0:T(8,128)S(1)}, u32[]{:S(2)}, u32[]{:S(2)}) %collective-permute-start.5) | collective-permute-done | bytes 1179680 | tf_op jit(solution)/shard_map/ppermute | solution.py:1101
  107.9 6.4 %attention_back_2.1 = (bf16[1024,256]{1,0:T(8,128)(2,1)S(1)}, bf16[1024,256]{1,0:T(8,128)(2,1)S(1)}, bf16[1024,256]{1,0:T(8,128)(2,1)S(1)}, f32[8,256]{1,0:T(8,128)S(1)}) custom-call(s32[2]{0:T(128)S(1)} %copy-done.22, f32[4,24,1536]{2,1,0:T(8,128)S(1)} %get-tuple-element.167.after_ref.xk, bf16[1024,768]{1,0:T(8,128)(2,1)S(1)} %copy-done.6, ...), custom_call_target="tpu_custom_call" | custom-call | flops 30000000 | bytes 1024 | tf_op jit(solution)/shard_map/attention_back_2/pallas_call | solution.py:105
  115.8 3.2 %qkv_weight_send.1.after_ref.own_ref = f32[1192,1024]{1,0:T(8,128)S(1)} custom-call(s32[7]{0:T(128)S(1)} %stack.31.pos_ref, s32[1]{0:T(128)S(6)} %copy.44.task_ref, f32[2,96,512]{2,1,0:T(8,128)S(1)} %get-tuple-element.174.after_ref.xyk, bf16[768,1024]{1,0:T(8,128)(2,1)S(1)} %get-tuple-element.175.left_ref, bf16[768,1024]{1,0:T(8,128)(2,1)S(1)} %copy-done.1, ...), custom_call_target="tpu_custom_call" | custom-call | flops 1000000000 | bytes 1024 | tf_op jit(solution)/shard_map/qkv_weight_send/pallas_call | solution.py:105
  122.5 4.8 %collective-permute-done.10.got_ref = f32[1192,1024]{1,0:T(8,128)S(1)} collective-permute-done((f32[1192,1024]{1,0:T(8,128)S(1)}, f32[1192,1024]{1,0:T(8,128)S(1)}, u32[]{:S(2)}, u32[]{:S(2)}) %collective-permute-start.10) | collective-permute-done | bytes 4882464 | tf_op jit(solution)/shard_map/ppermute | solution.py:1101
  127.3 3.4 %qkv_weight_keep.1 = (f32[280,1024]{1,0:T(8,128)S(1)}, f32[192,1024]{1,0:T(8,128)S(1)}, f32[192,1024]{1,0:T(8,128)S(1)}, f32[192,1024]{1,0:T(8,128)S(1)}, f32[19...) custom-call(s32[7]{0:T(128)S(1)} %stack.31.pos_ref, ...), custom_call_target="tpu_custom_call" | custom-call | flops 1000000000 | bytes 1024 | tf_op jit(solution)/shard_map/qkv_weight_keep/pallas_call | solution.py:105
  132.8 2.5 %collective-permute-done.11.xr = f32[4,24,1536]{2,1,0:T(8,128)S(1)} collective-permute-done((f32[4,24,1536]{2,1,0:T(8,128)S(1)}, f32[4,24,1536]{2,1,0:T(8,128)S(1)}, u32[]{:S(2)}, u32[]{:S(2)}) %collective-permute-start.11) | collective-permute-done | bytes 589856 | tf_op jit(solution)/shard_map/ppermute | solution.py:1101
  138.9 5.4 %token_grad.1 = (f32[1024,768]{1,0:T(8,128)}, f32[8,128]{1,0:T(8,128)S(1)}) custom-call(f32[2,24,3072]{2,1,0:T(8,128)S(1)} %get-tuple-element.192.after_ref.xyk, f32[1024,768]{1,0:T(8,128)S(1)} %get-tuple-element.193.dr1_ref, bf16[768,768]{1,0:T(8,128)(2,1)S(1)} %copy-done.3, bf16[768,768]{1,0:T(8,128)(2,1)S(1)} %copy-done.4, ...), custom_call_target="tpu_custom_call" | custom-call | flops 3000000000 | bytes 1024 | tf_op jit(solution)/shard_map/token_grad/pallas_call | solution.py:105
  144.9 1.6 collective-permute-start.17
  146.6 2.5 %collective-permute-start.21 = (f32[2,24,3072]{2,1,0:T(8,128)S(1)}, f32[2,24,3072]{2,1,0:T(8,128)S(1)}, u32[]{:S(2)}, u32[]{:S(2)}) collective-permute-start(f32[2,24,3072]{2,1,0:T(8,128)S(1)} %get-tuple-element.214), channel_id=1, source_target_pairs={{0,2},{1,3},{2,0},{3,1},{4,6},{5,7},{6,4},{7,5},{8,10},{9,11},{10,... | collective-permute-start | bytes 1769480 | tf_op jit(solution)/shard_map/ppermute | solution.py:1101
  149.1 2.7 %collective-permute-done.15.ry = f32[192,1024]{1,0:T(8,128)S(1)} collective-permute-done((f32[192,1024]{1,0:T(8,128)S(1)}, f32[192,1024]{1,0:T(8,128)S(1)}, u32[]{:S(2)}, u32[]{:S(2)}) %collective-permute-start.15) | collective-permute-done | bytes 786464 | tf_op jit(solution)/shard_map/ppermute | solution.py:1101
  151.7 4.1 %collective-permute-done.16.rz = f32[192,1024]{1,0:T(8,128)S(1)} collective-permute-done((f32[192,1024]{1,0:T(8,128)S(1)}, f32[192,1024]{1,0:T(8,128)S(1)}, u32[]{:S(2)}, u32[]{:S(2)}) %collective-permute-start.16) | collective-permute-done | bytes 786464 | tf_op jit(solution)/shard_map/ppermute | solution.py:1101
  155.8 4.9 %collective-permute-done.14.rx = f32[280,1024]{1,0:T(8,128)S(1)} collective-permute-done((f32[280,1024]{1,0:T(8,128)S(1)}, f32[280,1024]{1,0:T(8,128)S(1)}, u32[]{:S(2)}, u32[]{:S(2)}) %collective-permute-start.14) | collective-permute-done | bytes 1146912 | tf_op jit(solution)/shard_map/ppermute | solution.py:1101
  163.3 2.7 %collective-permute-start.20 = (f32[96,1024]{1,0:T(8,128)S(1)}, f32[96,1024]{1,0:T(8,128)S(1)}, u32[]{:S(2)}, u32[]{:S(2)}) collective-permute-start(f32[96,1024]{1,0:T(8,128)S(1)} %get-tuple-element.212), channel_id=1, source_target_pairs={{0,6},{1,7},{2,4},{3,5},{4,2},{5,3},{6,0},{7,1},{8,14},{9,15},{10,... | collective-permute-start | bytes 1179656 | tf_op jit(solution)/shard_map/ppermute | solution.py:1101
  166.0 6.1 %collective-permute-done.19.yr = f32[96,1024]{1,0:T(8,128)S(1)} collective-permute-done((f32[96,1024]{1,0:T(8,128)S(1)}, f32[96,1024]{1,0:T(8,128)S(1)}, u32[]{:S(2)}, u32[]{:S(2)}) %collective-permute-start.19) | collective-permute-done | bytes 393248 | tf_op jit(solution)/shard_map/ppermute | solution.py:1101
  172.2 10.3 %collective-permute-done.20.zr = f32[96,1024]{1,0:T(8,128)S(1)} collective-permute-done((f32[96,1024]{1,0:T(8,128)S(1)}, f32[96,1024]{1,0:T(8,128)S(1)}, u32[]{:S(2)}, u32[]{:S(2)}) %collective-permute-start.20) | collective-permute-done | bytes 393248 | tf_op jit(solution)/shard_map/ppermute | solution.py:1101
  186.2 5.1 %collective-permute-done.23.zr = f32[48,1024]{1,0:T(8,128)S(1)} collective-permute-done((f32[48,1024]{1,0:T(8,128)S(1)}, f32[48,1024]{1,0:T(8,128)S(1)}, u32[]{:S(2)}, u32[]{:S(2)}) %collective-permute-start.23) | collective-permute-done | bytes 196640 | tf_op jit(solution)/shard_map/ppermute | solution.py:1101
  191.4 6.8 %collective-permute-done.22.got = f32[136,1024]{1,0:T(8,128)S(1)} collective-permute-done((f32[136,1024]{1,0:T(8,128)S(1)}, f32[136,1024]{1,0:T(8,128)S(1)}, u32[]{:S(2)}, u32[]{:S(2)}) %collective-permute-start.22) | collective-permute-done | bytes 557088 | tf_op jit(solution)/shard_map/ppermute | solution.py:1101
  198.8 2.5 %collective-permute-start.24 = (f32[88,1024]{1,0:T(8,128)S(1)}, f32[88,1024]{1,0:T(8,128)S(1)}, u32[]{:S(2)}, u32[]{:S(2)}) collective-permute-start(f32[88,1024]{1,0:T(8,128)S(1)} %get-tuple-element.221), channel_id=1, source_target_pairs={{0,6},{1,7},{2,4},{3,5},{4,2},{5,3},{6,0},{7,1},{8,14},{9,15},{10,... | collective-permute-start | bytes 1081352 | tf_op jit(solution)/shard_map/ppermute | solution.py:1101
  203.2 2.6 %collective-permute-done.25.zr = f32[24,1024]{1,0:T(8,128)S(1)} collective-permute-done((f32[24,1024]{1,0:T(8,128)S(1)}, f32[24,1024]{1,0:T(8,128)S(1)}, u32[]{:S(2)}, u32[]{:S(2)}) %collective-permute-start.25) | collective-permute-done | bytes 98336 | tf_op jit(solution)/shard_map/ppermute | solution.py:1101
  205.9 10.6 %collective-permute-done.24.got = f32[88,1024]{1,0:T(8,128)S(1)} collective-permute-done((f32[88,1024]{1,0:T(8,128)S(1)}, f32[88,1024]{1,0:T(8,128)S(1)}, u32[]{:S(2)}, u32[]{:S(2)}) %collective-permute-start.24) | collective-permute-done | bytes 360480 | tf_op jit(solution)/shard_map/ppermute | solution.py:1101
  (105 shorter events, 34.0 us)
Async XLA Ops:
  2.8 18.1 %copy-start.16 = (bf16[768]{0:T(1024)(128)(2,1)S(1)}, bf16[768]{0:T(1024)(128)(2,1)}, u32[]{:S(2)}) copy-start(bf16[768]{0:T(1024)(128)(2,1)} %bo_ref.1) | copy-start | bytes 4612
  2.8 18.1 %copy-start.17 = (bf16[768]{0:T(1024)(128)(2,1)S(1)}, bf16[768]{0:T(1024)(128)(2,1)}, u32[]{:S(2)}) copy-start(bf16[768]{0:T(1024)(128)(2,1)} %b1_ref.1) | copy-start | bytes 4612
  2.8 18.1 %copy-start.18 = (bf16[768]{0:T(1024)(128)(2,1)S(1)}, bf16[768]{0:T(1024)(128)(2,1)}, u32[]{:S(2)}) copy-start(bf16[768]{0:T(1024)(128)(2,1)} %bd_ref.1) | copy-start | bytes 4612
  2.8 18.1 %copy-start.19 = (bf16[768]{0:T(1024)(128)(2,1)S(1)}, bf16[768]{0:T(1024)(128)(2,1)}, u32[]{:S(2)}) copy-start(bf16[768]{0:T(1024)(128)(2,1)} %g2_ref.1) | copy-start | bytes 4612
  2.8 18.1 %copy-start.20 = (bf16[768]{0:T(1024)(128)(2,1)S(1)}, bf16[768]{0:T(1024)(128)(2,1)}, u32[]{:S(2)}) copy-start(bf16[768]{0:T(1024)(128)(2,1)} %b2_ref.1) | copy-start | bytes 4612
  44.8 14.0 %collective-permute-start = (f32[2,768,768]{2,1,0:T(8,128)S(1)}, f32[2,768,768]{2,1,0:T(8,128)S(1)}, u32[]{:S(2)}, u32[]{:S(2)}) collective-permute-start(f32[2,768,768]{2,1,0:T(8,128)S(1)} %outer_weight_send.1.after_ref), channel_id=1, source_target_pairs={{0,8},{1,9},{2,10},{3,11},{4,12},{5,13},{6,14},{7,15},{8,0},{9,1},... | collective-permute-start | bytes 14155784 | tf_op jit(solution)/shard_map/ppermute | solution.py:1101
  58.2 15.9 %collective-permute-start.1 = (f32[2,384,1536]{2,1,0:T(8,128)S(1)}, f32[2,384,1536]{2,1,0:T(8,128)S(1)}, u32[]{:S(2)}, u32[]{:S(2)}) collective-permute-start(f32[2,384,1536]{2,1,0:T(8,128)S(1)} %inner_weight_send.1.after_ref), channel_id=1, source_target_pairs={{0,8},{1,9},{2,10},{3,11},{4,12},{5,13},{6,14},{7,15},{8,0},{9,1},... | collective-permute-start | bytes 14155784 | tf_op jit(solution)/shard_map/ppermute | solution.py:1101
  60.0 24.5 %collective-permute-start.2 = (f32[2,4,96,256]{3,2,1,0:T(8,128)S(1)}, f32[2,4,96,256]{3,2,1,0:T(8,128)S(1)}, u32[]{:S(2)}, u32[]{:S(2)}) collective-permute-start(f32[2,4,96,256]{3,2,1,0:T(8,128)S(1)} %get-tuple-element.157), channel_id=1, source_target_pairs={{0,1},{1,0},{2,3},{3,2},{4,5},{5,4},{6,7},{7,6},{8,9},{9,8},{10,11... | collective-permute-start | bytes 2359304 | tf_op jit(solution)/shard_map/ppermute | solution.py:1101
  61.5 23.0 %collective-permute-start.3 = (f32[4,2,96,256]{3,2,1,0:T(8,128)S(1)}, f32[4,2,96,256]{3,2,1,0:T(8,128)S(1)}, u32[]{:S(2)}, u32[]{:S(2)}) collective-permute-start(f32[4,2,96,256]{3,2,1,0:T(8,128)S(1)} %get-tuple-element.159), channel_id=1, source_target_pairs={{0,16},{1,17},{2,18},{3,19},{4,20},{5,21},{6,22},{7,23},{8,24},{9,... | collective-permute-start | bytes 2359304 | tf_op jit(solution)/shard_map/ppermute | solution.py:1101
  63.0 21.4 %collective-permute-start.4 = (f32[2,2,2,96,256]{4,3,2,1,0:T(8,128)S(1)}, f32[2,2,2,96,256]{4,3,2,1,0:T(8,128)S(1)}, u32[]{:S(2)}, u32[]{:S(2)}) collective-permute-start(f32[2,2,2,96,256]{4,3,2,1,0:T(8,128)S(1)} %get-tuple-element.161), channel_id=1, source_target_pairs={{0,2},{1,3},{2,0},{3,1},{4,6},{5,7},{6,4},{7,5},{8,10},{9,11},{10,... | collective-permute-start | bytes 2359304 | tf_op jit(solution)/shard_map/ppermute | solution.py:1101
  77.4 29.0 %collective-permute-start.5 = (f32[2,4,24,1536]{3,2,1,0:T(8,128)S(1)}, f32[2,4,24,1536]{3,2,1,0:T(8,128)S(1)}, u32[]{:S(2)}, u32[]{:S(2)}) collective-permute-start(f32[2,4,24,1536]{3,2,1,0:T(8,128)S(1)} %get-tuple-element.164), channel_id=1, source_target_pairs={{0,1},{1,0},{2,3},{3,2},{4,5},{5,4},{6,7},{7,6},{8,9},{9,8},{10,11... | collective-permute-start | bytes 3538952 | tf_op jit(solution)/shard_map/ppermute | solution.py:1101
  78.0 29.1 %collective-permute-start.6 = (f32[4,2,24,1536]{3,2,1,0:T(8,128)S(1)}, f32[4,2,24,1536]{3,2,1,0:T(8,128)S(1)}, u32[]{:S(2)}, u32[]{:S(2)}) collective-permute-start(f32[4,2,24,1536]{3,2,1,0:T(8,128)S(1)} %get-tuple-element.166), channel_id=1, source_target_pairs={{0,16},{1,17},{2,18},{3,19},{4,20},{5,21},{6,22},{7,23},{8,24},{9,... | collective-permute-start | bytes 3538952 | tf_op jit(solution)/shard_map/ppermute | solution.py:1101
  85.3 29.1 %collective-permute-start.7 = (f32[4,96,256]{2,1,0:T(8,128)S(1)}, f32[4,96,256]{2,1,0:T(8,128)S(1)}, u32[]{:S(2)}, u32[]{:S(2)}) collective-permute-start(f32[4,96,256]{2,1,0:T(8,128)S(1)} %get-tuple-element.169), channel_id=1, source_target_pairs={{0,16},{1,17},{2,18},{3,19},{4,20},{5,21},{6,22},{7,23},{8,24},{9,... | collective-permute-start | bytes 1179656 | tf_op jit(solution)/shard_map/ppermute | solution.py:1101
  87.3 27.1 %collective-permute-start.8 = (f32[4,96,256]{2,1,0:T(8,128)S(1)}, f32[4,96,256]{2,1,0:T(8,128)S(1)}, u32[]{:S(2)}, u32[]{:S(2)}) collective-permute-start(f32[4,96,256]{2,1,0:T(8,128)S(1)} %get-tuple-element.171), channel_id=1, source_target_pairs={{0,1},{1,0},{2,3},{3,2},{4,5},{5,4},{6,7},{7,6},{8,9},{9,8},{10,11... | collective-permute-start | bytes 1179656 | tf_op jit(solution)/shard_map/ppermute | solution.py:1101
  88.8 25.6 %collective-permute-start.9 = (f32[2,2,96,256]{3,2,1,0:T(8,128)S(1)}, f32[2,2,96,256]{3,2,1,0:T(8,128)S(1)}, u32[]{:S(2)}, u32[]{:S(2)}) collective-permute-start(f32[2,2,96,256]{3,2,1,0:T(8,128)S(1)} %get-tuple-element.173), channel_id=1, source_target_pairs={{0,6},{1,7},{2,4},{3,5},{4,2},{5,3},{6,0},{7,1},{8,14},{9,15},{10,... | collective-permute-start | bytes 1179656 | tf_op jit(solution)/shard_map/ppermute | solution.py:1101
  119.0 8.2 %collective-permute-start.10 = (f32[1192,1024]{1,0:T(8,128)S(1)}, f32[1192,1024]{1,0:T(8,128)S(1)}, u32[]{:S(2)}, u32[]{:S(2)}) collective-permute-start(f32[1192,1024]{1,0:T(8,128)S(1)} %qkv_weight_send.1.after_ref.own_ref), channel_id=1, source_target_pairs={{0,8},{1,9},{2,10},{3,11},{4,12},{5,13},{6,14},{7,15},{8,0},{9,1},... | collective-permute-start | bytes 14647304 | tf_op jit(solution)/shard_map/ppermute | solution.py:1101
  119.1 16.2 %collective-permute-start.11 = (f32[4,24,1536]{2,1,0:T(8,128)S(1)}, f32[4,24,1536]{2,1,0:T(8,128)S(1)}, u32[]{:S(2)}, u32[]{:S(2)}) collective-permute-start(f32[4,24,1536]{2,1,0:T(8,128)S(1)} %get-tuple-element.189), channel_id=1, source_target_pairs={{0,16},{1,17},{2,18},{3,19},{4,20},{5,21},{6,22},{7,23},{8,24},{9,... | collective-permute-start | bytes 1769480 | tf_op jit(solution)/shard_map/ppermute | solution.py:1101
  120.7 16.2 %collective-permute-start.12 = (f32[4,24,1536]{2,1,0:T(8,128)S(1)}, f32[4,24,1536]{2,1,0:T(8,128)S(1)}, u32[]{:S(2)}, u32[]{:S(2)}) collective-permute-start(f32[4,24,1536]{2,1,0:T(8,128)S(1)} %get-tuple-element.191), channel_id=1, source_target_pairs={{0,1},{1,0},{2,3},{3,2},{4,5},{5,4},{6,7},{7,6},{8,9},{9,8},{10,11... | collective-permute-start | bytes 1769480 | tf_op jit(solution)/shard_map/ppermute | solution.py:1101
  121.3 23.0 %collective-permute-start.13 = (f32[2,96,512]{2,1,0:T(8,128)S(1)}, f32[2,96,512]{2,1,0:T(8,128)S(1)}, u32[]{:S(2)}, u32[]{:S(2)}) collective-permute-start(f32[2,96,512]{2,1,0:T(8,128)S(1)} %get-tuple-element.196), channel_id=1, source_target_pairs={{0,2},{1,3},{2,0},{3,1},{4,6},{5,7},{6,4},{7,5},{8,10},{9,11},{10,... | collective-permute-start | bytes 1179656 | tf_op jit(solution)/shard_map/ppermute | solution.py:1101
  130.6 30.1 %collective-permute-start.14 = (f32[280,1024]{1,0:T(8,128)S(1)}, f32[280,1024]{1,0:T(8,128)S(1)}, u32[]{:S(2)}, u32[]{:S(2)}) collective-permute-start(f32[280,1024]{1,0:T(8,128)S(1)} %get-tuple-element.199), channel_id=1, source_target_pairs={{0,1},{1,0},{2,3},{3,2},{4,5},{5,4},{6,7},{7,6},{8,9},{9,8},{10,11... | collective-permute-start | bytes 3440648 | tf_op jit(solution)/shard_map/ppermute | solution.py:1101
  131.9 19.8 %collective-permute-start.15 = (f32[192,1024]{1,0:T(8,128)S(1)}, f32[192,1024]{1,0:T(8,128)S(1)}, u32[]{:S(2)}, u32[]{:S(2)}) collective-permute-start(f32[192,1024]{1,0:T(8,128)S(1)} %get-tuple-element.201), channel_id=1, source_target_pairs={{0,16},{1,17},{2,18},{3,19},{4,20},{5,21},{6,22},{7,23},{8,24},{9,... | collective-permute-start | bytes 2359304 | tf_op jit(solution)/shard_map/ppermute | solution.py:1101
  135.3 20.5 %collective-permute-start.16 = (f32[192,1024]{1,0:T(8,128)S(1)}, f32[192,1024]{1,0:T(8,128)S(1)}, u32[]{:S(2)}, u32[]{:S(2)}) collective-permute-start(f32[192,1024]{1,0:T(8,128)S(1)} %get-tuple-element.203), channel_id=1, source_target_pairs={{0,2},{1,3},{2,0},{3,1},{4,6},{5,7},{6,4},{7,5},{8,10},{9,11},{10,... | collective-permute-start | bytes 2359304 | tf_op jit(solution)/shard_map/ppermute | solution.py:1101
  144.9 21.0 %collective-permute-start.17 = (f32[96,512]{1,0:T(8,128)S(1)}, f32[96,512]{1,0:T(8,128)S(1)}, u32[]{:S(2)}, u32[]{:S(2)}) collective-permute-start(f32[96,512]{1,0:T(8,128)S(1)} %get-tuple-element.206), channel_id=1, source_target_pairs={{0,6},{1,7},{2,4},{3,5},{4,2},{5,3},{6,0},{7,1},{8,14},{9,15},{10,... | collective-permute-start | bytes 589832 | tf_op jit(solution)/shard_map/ppermute | solution.py:1101
  146.6 36.9 %collective-permute-start.21 = (f32[2,24,3072]{2,1,0:T(8,128)S(1)}, f32[2,24,3072]{2,1,0:T(8,128)S(1)}, u32[]{:S(2)}, u32[]{:S(2)}) collective-permute-start(f32[2,24,3072]{2,1,0:T(8,128)S(1)} %get-tuple-element.214), channel_id=1, source_target_pairs={{0,2},{1,3},{2,0},{3,1},{4,6},{5,7},{6,4},{7,5},{8,10},{9,11},{10,... | collective-permute-start | bytes 1769480 | tf_op jit(solution)/shard_map/ppermute | solution.py:1101
  161.5 20.9 %collective-permute-start.18 = (f32[160,1024]{1,0:T(8,128)S(1)}, f32[160,1024]{1,0:T(8,128)S(1)}, u32[]{:S(2)}, u32[]{:S(2)}) collective-permute-start(f32[160,1024]{1,0:T(8,128)S(1)} %get-tuple-element.208), channel_id=1, source_target_pairs={{0,16},{1,17},{2,18},{3,19},{4,20},{5,21},{6,22},{7,23},{8,24},{9,... | collective-permute-start | bytes 1966088 | tf_op jit(solution)/shard_map/ppermute | solution.py:1101
  162.1 10.1 %collective-permute-start.19 = (f32[96,1024]{1,0:T(8,128)S(1)}, f32[96,1024]{1,0:T(8,128)S(1)}, u32[]{:S(2)}, u32[]{:S(2)}) collective-permute-start(f32[96,1024]{1,0:T(8,128)S(1)} %get-tuple-element.210), channel_id=1, source_target_pairs={{0,1},{1,0},{2,3},{3,2},{4,5},{5,4},{6,7},{7,6},{8,9},{9,8},{10,11... | collective-permute-start | bytes 1179656 | tf_op jit(solution)/shard_map/ppermute | solution.py:1101
  163.3 19.2 %collective-permute-start.20 = (f32[96,1024]{1,0:T(8,128)S(1)}, f32[96,1024]{1,0:T(8,128)S(1)}, u32[]{:S(2)}, u32[]{:S(2)}) collective-permute-start(f32[96,1024]{1,0:T(8,128)S(1)} %get-tuple-element.212), channel_id=1, source_target_pairs={{0,6},{1,7},{2,4},{3,5},{4,2},{5,3},{6,0},{7,1},{8,14},{9,15},{10,... | collective-permute-start | bytes 1179656 | tf_op jit(solution)/shard_map/ppermute | solution.py:1101
  183.2 15.0 %collective-permute-start.22 = (f32[136,1024]{1,0:T(8,128)S(1)}, f32[136,1024]{1,0:T(8,128)S(1)}, u32[]{:S(2)}, u32[]{:S(2)}) collective-permute-start(f32[136,1024]{1,0:T(8,128)S(1)} %get-tuple-element.217), channel_id=1, source_target_pairs={{0,2},{1,3},{2,0},{3,1},{4,6},{5,7},{6,4},{7,5},{8,10},{9,11},{10,... | collective-permute-start | bytes 1671176 | tf_op jit(solution)/shard_map/ppermute | solution.py:1101
  184.1 17.7 %collective-permute-start.26 = (f32[24,3072]{1,0:T(8,128)S(1)}, f32[24,3072]{1,0:T(8,128)S(1)}, u32[]{:S(2)}, u32[]{:S(2)}) collective-permute-start(f32[24,3072]{1,0:T(8,128)S(1)} %get-tuple-element.235), channel_id=1, source_target_pairs={{0,6},{1,7},{2,4},{3,5},{4,2},{5,3},{6,0},{7,1},{8,14},{9,15},{10,... | collective-permute-start | bytes 884744 | tf_op jit(solution)/shard_map/ppermute | solution.py:1101
  185.7 5.7 %collective-permute-start.23 = (f32[48,1024]{1,0:T(8,128)S(1)}, f32[48,1024]{1,0:T(8,128)S(1)}, u32[]{:S(2)}, u32[]{:S(2)}) collective-permute-start(f32[48,1024]{1,0:T(8,128)S(1)} %get-tuple-element.219), channel_id=1, source_target_pairs={{0,1},{1,0},{2,3},{3,2},{4,5},{5,4},{6,7},{7,6},{8,9},{9,8},{10,11... | collective-permute-start | bytes 589832 | tf_op jit(solution)/shard_map/ppermute | solution.py:1101
  198.8 17.7 %collective-permute-start.24 = (f32[88,1024]{1,0:T(8,128)S(1)}, f32[88,1024]{1,0:T(8,128)S(1)}, u32[]{:S(2)}, u32[]{:S(2)}) collective-permute-start(f32[88,1024]{1,0:T(8,128)S(1)} %get-tuple-element.221), channel_id=1, source_target_pairs={{0,6},{1,7},{2,4},{3,5},{4,2},{5,3},{6,0},{7,1},{8,14},{9,15},{10,... | collective-permute-start | bytes 1081352 | tf_op jit(solution)/shard_map/ppermute | solution.py:1101
  201.2 4.6 %collective-permute-start.25 = (f32[24,1024]{1,0:T(8,128)S(1)}, f32[24,1024]{1,0:T(8,128)S(1)}, u32[]{:S(2)}, u32[]{:S(2)}) collective-permute-start(f32[24,1024]{1,0:T(8,128)S(1)} %get-tuple-element.223), channel_id=1, source_target_pairs={{0,16},{1,17},{2,18},{3,19},{4,20},{5,21},{6,22},{7,23},{8,24},{9,... | collective-permute-start | bytes 294920 | tf_op jit(solution)/shard_map/ppermute | solution.py:1101
  (21 other events, 152.9 us)
where the time goes:
time: 222 us; the launch traced here: 219 us
  Pallas kernels  109 us (49%)
  waiting for transfers between devices  70.3 us (32%)
  starting transfers between devices  31.6 us (14%)
  local copies, waits for them, and re-layouts  4.68 us (2%)
  between operations  2.92 us (1%)
    pallas_call x28, Pallas kernels, call(): pl.pallas_call(kernel, in_specs=[specs[p] for _, p in inputs], out_specs=...  109 us
    ppermute x27, waiting for transfers between devices, swap(): return lax.ppermute(array, ALL_AXES, PAIRS[name])  70.3 us
    ppermute x27, starting transfers between devices, swap(): return lax.ppermute(array, ALL_AXES, PAIRS[name])  31.6 us
    unnamed x53, local copies, waits for them, and re-layouts  4.59 us
  transfers between devices with their start and end apart: 27, of which 15 were waited for; matrix products, arithmetic and copies ran while one was open for 0% of the time, Pallas kernels for 29%

commit v1 on v0

--- a/solution.py
+++ b/solution.py
@@ -41,12 +41,12 @@
 
 
 COSTS = {
-    "attention_back_0": 3000,
+    "attention_back_0": 1,
     "attention_back_1": 10000,
-    "attention_back_2": 30,
-    "first_norm_back": 3000,
+    "attention_back_2": 10000,
+    "first_norm_back": 1,
     "fourth_qkv_stage": 100,
-    "fourth_stage_inner": 3000,
+    "fourth_stage_inner": 1,
     "fourth_stage_outer": 1000,
     "inner_grad": 3000,
     "inner_weight_keep": 1000,
@@ -54,9 +54,10 @@
     "last_outer_stage": 3000,
     "last_stage": 300,
     "outer_weight_keep": 3000,
-    "outer_weight_send": 1000,
-    "qkv_weight_keep": 1000,
-    "qkv_weight_send": 1000,
+    "outer_weight_rest": 1,
+    "outer_weight_send": 3000,
+    "qkv_weight_keep": 100,
+    "qkv_weight_send": 3000,
     "second_qkv_stage": 100,
     "second_stage_inner": 10000,
     "second_stage_outer": 3000,
@@ -68,12 +69,12 @@
 }
 ORDER = [
     "send_outer",
-    "rest_outer",
     "inner_grad",
     "send_inner",
+    "rest_outer",
     "keep_outer",
+    "keep_inner",
     "first_norm",
-    "keep_inner",
     "back_0",
     "second_outer",
     "back_1",
@@ -89,9 +90,9 @@
     "sum_outer",
     "third_qkv",
     "fourth_inner",
+    "last_outer",
     "fourth_qkv",
     "last_inner",
-    "last_outer",
     "last_qkv",
 ]
 
@@ -263,7 +264,7 @@
     task_ref, label_ref, weight_ref, x_ref, ctx_ref, cot_ref, wo_ref, wi_ref, wd_ref,
     bo_ref, g1_ref, b1_ref, bi_ref, bd_ref, g2_ref, b2_ref, head_ref,
     out_hbm, normed1_ref, root1_ref, h1t_ref, act_ref, slope_ref, ddown_ref, sums_ref,
-    out_ref, h1_s, hid_s, res_s, sems,
+    out_ref, sems,
     *, length, group_seqs,
 ):
     rows, width = x_ref.shape
@@ -277,106 +278,66 @@
     head = jnp.sum(jnp.where(chosen, table, 0.0), axis=1)
     classes = head.shape[0]
     sums_ref[...] = jnp.zeros_like(sums_ref)
-    res_s[...] = jnp.zeros_like(res_s)
-    tiles = rows // TILE
-    per_seq = length // TILE
-    pieces = ff // part
-    piece = TILE // pieces
-
-    def rows_of(step, k):
-        return pl.ds(pl.multiple_of(step * TILE + k * piece, piece), piece)
-
-    def project(step, slot):
-        tile = at(step, TILE)
-        hid_s[slot] = x_ref[tile, :].astype(single) + dot(ctx_ref[tile, :], wo_ref[...]) + bo
-
-    def norm_first(step, slot, k):
-        here, to = slice(k * piece, (k + 1) * piece), rows_of(step, k)
-        normed1, root1 = norm_parts(hid_s[slot, here, :])
-        normed1_ref[to, :] = normed1.astype(half)
-        root1_ref[to, :] = jnp.broadcast_to(root1, (piece, 128))
+
+    @pl.loop(0, rows // (2 * TILE))
+    def _(step):
+        tile = at(step, (2 * TILE))
+        x = x_ref[tile, :].astype(single)
+        normed1, root1 = norm_parts(x + dot(ctx_ref[tile, :], wo_ref[...]) + bo)
+        normed1_ref[tile, :] = normed1.astype(half)
+        root1_ref[tile, :] = jnp.broadcast_to(root1, ((2 * TILE), 128))
         hidden1 = normed1 * g1 + b1
-        hid_s[slot, here, :] = hidden1
-        h1_s[slot, here, :] = hidden1.astype(half)
-
-    def norm_second(step, slot, k, valid):
-        here, to = slice(k * piece, (k + 1) * piece), rows_of(step, k)
-        normed2, root2 = norm_parts(res_s[slot, here, :])
-        final = normed2 * g2 + b2
-        low = final.astype(half)
-        out_ref[to, :] = low
-        d_final = cot_ref[to, :].astype(single) * w
-        if k == 0:
-            cls = low[0:1].astype(single)
-            logits = [jnp.sum(cls * head[c : c + 1], axis=1, keepdims=True) for c in range(classes)]
-            top = functools.reduce(jnp.maximum, logits)
-            lse = top + jnp.log(sum(jnp.exp(v - top) for v in logits))
-            label = label_ref[step // per_seq]
-            weight = jnp.where(step % per_seq == 0, w / group_seqs, 0.0)
-            picked = sum(jnp.where(label == c, v, 0.0) for c, v in enumerate(logits))
-            slopes = [
-                (jnp.exp(v - lse) - jnp.where(label == c, 1.0, 0.0)) * weight for c, v in enumerate(logits)
-            ]
-            d_cls = sum(s * head[c : c + 1] for c, s in enumerate(slopes))
-            row = lax.broadcasted_iota(jnp.int32, d_final.shape, 0)
-            d_final = d_final + jnp.where(row == 0, d_cls, 0.0)
-            for c in range(classes):
-                sums_ref[3 + c : 4 + c] += slopes[c] * cls * valid
-            sums_ref[7:8] += jnp.broadcast_to((lse - picked) * (weight * valid), cls.shape)
-        ddown = norm_back(d_final, normed2, root2, g2).astype(half)
-        ddown_ref[to, :] = ddown
-        sums_ref[0:1] += column_sum(d_final * normed2) * valid
-        sums_ref[1:2] += column_sum(d_final) * valid
-        sums_ref[2:3] += column_sum(ddown.astype(single)) * valid
-
-    def leave(step):
-        tile = at(step, TILE)
-        return pltpu.make_async_copy(out_ref.at[tile, :], out_hbm.at[tile, :], sems.at[step])
-
-    project(0, 0)
-    for k in range(pieces):
-        norm_first(0, 0, k)
-    h1t_ref[:, :TILE] = h1_s[0].T
-
-    @pl.loop(0, tiles)
-    def _(step):
-        slot = lax.rem(step, 2)
-        tile = at(step, TILE)
-        later, earlier = jnp.minimum(step + 1, tiles - 1), jnp.maximum(step - 1, 0)
-        valid = jnp.where(step > 0, 1.0, 0.0)
-        project(later, 1 - slot)
-        h1 = h1_s[slot]
+        h1 = hidden1.astype(half)
+        h1t_ref[:, tile] = h1.T
 
         def inner_part(j):
             return dot(h1, wi_ref[:, j : j + part]) + bi[:, j : j + part]
 
         down = None
         following = inner_part(0)
-        for k in range(pieces):
-            j = k * part
+        for j in range(0, ff, part):
             inner = following
-            if k + 1 < pieces:
+            if j + part < ff:
                 following = inner_part(j + part)
-            norm_first(later, 1 - slot, k)
             value, slope = gelu_parts(inner)
             act = value.astype(half)
             act_ref[tile, j : j + part] = act
             slope_ref[tile, j : j + part] = slope.astype(half)
-            norm_second(earlier, 1 - slot, k, valid)
             term = dot(act, wd_ref[j : j + part, :])
             down = term if down is None else down + term
-        res_s[slot] = hid_s[slot] + down + bd
-        h1t_ref[:, at(later, TILE)] = h1_s[1 - slot].T
-
-        @pl.when(step > 0)
-        def _():
-            leave(earlier).start()
-
-    for k in range(pieces):
-        norm_second(tiles - 1, (tiles - 1) % 2, k, 1.0)
-    leave(tiles - 1).start()
-    for step in range(tiles):
-        leave(step).wait()
+        normed2, root2 = norm_parts(hidden1 + down + bd)
+        final = normed2 * g2 + b2
+        low = final.astype(half)
+        out_ref[tile, :] = low
+        pltpu.make_async_copy(out_ref.at[tile, :], out_hbm.at[tile, :], sems.at[step]).start()
+        cls = low[0:1].astype(single)
+        logits = [jnp.sum(cls * head[c : c + 1], axis=1, keepdims=True) for c in range(classes)]
+        top = functools.reduce(jnp.maximum, logits)
+        lse = top + jnp.log(sum(jnp.exp(v - top) for v in logits))
+        per_seq = length // (2 * TILE)
+        label = label_ref[step // per_seq]
+        first = jnp.where(step % per_seq == 0, 1.0, 0.0)
+        picked = sum(jnp.where(label == c, v, 0.0) for c, v in enumerate(logits))
+        slopes = [
+            (jnp.exp(v - lse) - jnp.where(label == c, 1.0, 0.0)) * (w / group_seqs * first)
+            for c, v in enumerate(logits)
+        ]
+        d_cls = sum(s * head[c : c + 1] for c, s in enumerate(slopes))
+        row = lax.broadcasted_iota(jnp.int32, final.shape, 0)
+        d_final = cot_ref[tile, :].astype(single) * w + jnp.where(row == 0, d_cls, 0.0)
+        dr2 = norm_back(d_final, normed2, root2, g2)
+        ddown = dr2.astype(half)
+        ddown_ref[tile, :] = ddown
+        sums_ref[0:1] += column_sum(d_final * normed2)
+        sums_ref[1:2] += column_sum(d_final)
+        sums_ref[2:3] += column_sum(ddown.astype(single))
+        for c in range(classes):
+            sums_ref[3 + c : 4 + c] += slopes[c] * cls
+        sums_ref[7:8] += jnp.broadcast_to((lse - picked) * (w / group_seqs * first), cls.shape)
+
+    for i in range(rows // (2 * TILE)):
+        tile = pl.ds(i * (2 * TILE), (2 * TILE))
+        pltpu.make_async_copy(out_ref.at[tile, :], out_hbm.at[tile, :], sems.at[i]).wait()
 
 
 def middle(x, ctx, cot, length, labels, task_ids, task_weights, wo, wi, wd, vectors, head_table, group_seqs):
@@ -399,10 +360,8 @@
             (near(flat, half), "v"),
             (near((8, width)), "v"),
         ],
-        [pltpu.VMEM(flat, half), pltpu.VMEM((2, TILE, width), half)]
-        + [pltpu.VMEM((2, TILE, width), single)] * 2
-        + [pltpu.SemaphoreType.DMA((rows // TILE,))],
-        14,
+        [pltpu.VMEM(flat, half), pltpu.SemaphoreType.DMA((rows // (2 * TILE),))],
+        20,
     )
 
 
@@ -525,19 +484,50 @@
     return dot(act_ref[:, at(2 * y + me, part)], ddown_ref[...], TN)
 
 
-def outer_send_kernel(pos_ref, after_ref, act_ref, ddown_ref, send_ref, *, other):
-    me = 1 - pos_ref[1] if other else pos_ref[1]
+TABLE = 32
+
+
+def table_rows(pos_ref, task_ref, sums2, out, classes, tables):
+    width = out.shape[1]
+    out[...] = jnp.zeros_like(out)
+    out[0:3, :] = sums2[0:3]
+    lane = lax.broadcasted_iota(jnp.int32, (1, width), 1)
+    out[3:4, :] = jnp.where(lane == pos_ref[6], sums2[7:8], 0.0)
+    for t in range(tables):
+        mine = jnp.where(task_ref[0] == t, 1.0, 0.0)
+        out[4 + t * classes : 4 + (t + 1) * classes, :] = sums2[3 : 3 + classes] * mine
+
+
+def outer_send_kernel(pos_ref, task_ref, after_ref, act_ref, ddown_ref, sums2, send_ref, table_ref, *, classes, tables):
+    part = act_ref.shape[1] // 4
     for y in range(2):
-        send_ref[y] = outer_half(me, act_ref, ddown_ref, y)
-
-
-def outer_send(pos, after, act, ddown, other):
+        send_ref[y * part : (y + 1) * part, :] = outer_half(1 - pos_ref[1], act_ref, ddown_ref, y)
+    table_rows(pos_ref, task_ref, sums2, table_ref, classes, tables)
+    send_ref[2 * part :, :] = table_ref[...]
+
+
+def outer_rest_kernel(pos_ref, after_ref, act_ref, ddown_ref, rest_ref):
+    for y in range(2):
+        rest_ref[y] = outer_half(pos_ref[1], act_ref, ddown_ref, y)
+
+
+def outer_send(pos, task_ids, after, act, ddown, sums2, classes, tables):
     width = ddown.shape[1]
-    return call(
-        functools.partial(outer_send_kernel, other=other),
-        "outer_weight_send" if other else "outer_weight_rest",
+    assert 4 + classes * tables <= TABLE
+    return call(
+        functools.partial(outer_send_kernel, classes=classes, tables=tables),
+        "outer_weight_send",
+        [(pos, "s"), (task_ids, "s"), (after, "a"), (act, "v"), (ddown, "v"), (sums2, "v")],
+        [(near((act.shape[1] // 2 + TABLE, width)), "v"), (near((TABLE, width)), "v")],
+    )
+
+
+def outer_rest(pos, after, act, ddown):
+    return call(
+        outer_rest_kernel,
+        "outer_weight_rest",
         [(pos, "s"), (after, "a"), (act, "v"), (ddown, "v")],
-        [(near((2, act.shape[1] // 4, width)), "v")],
+        [(near((2, act.shape[1] // 4, ddown.shape[1])), "v")],
     )[0]
 
 
@@ -568,22 +558,27 @@
 
 
 def outer_keep_kernel(
-    pos_ref, after_ref, own_ref, got_ref, sx_ref, kx_ref, sy_ref, ky_ref, sz_ref, kz_ref
+    pos_ref, after_ref, own_ref, got_ref, table_ref, sx_ref, kx_ref, sy_ref, ky_ref, sz_ref, kz_ref, block_ref
 ):
-    third = own_ref.shape[2] // 3
+    third, part = own_ref.shape[2] // 3, own_ref.shape[1]
     rows = own_ref.shape[1] // 8
     me_y, me_x, side = pos_ref[0], pos_ref[2], pos_ref[3]
     xs, ys, zs = [slice(i * third, (i + 1) * third) for i in range(3)]
 
     def at_rows(y, z, x, cols):
         begin = (2 * z + x) * rows
-        return own_ref[y, begin : begin + rows, cols] + got_ref[y, begin : begin + rows, cols]
+        there = y * part + begin
+        return own_ref[y, begin : begin + rows, cols] + got_ref[there : there + rows, cols]
+
+    table = table_ref[...] + got_ref[2 * part :, :]
+    block_ref[...] = jnp.concatenate([table[:, i * third : (i + 1) * third] for i in range(3)], axis=0)
+    sx_ref[8] = block_ref[...]
 
     for y in range(2):
         for z in range(4):
             zero, one = at_rows(y, z, 0, xs), at_rows(y, z, 1, xs)
-            sx_ref[y, z] = jnp.where(me_x == 0, one, zero)
-            kx_ref[y, z] = jnp.where(me_x == 0, zero, one)
+            sx_ref[4 * y + z] = jnp.where(me_x == 0, one, zero)
+            kx_ref[4 * y + z] = jnp.where(me_x == 0, zero, one)
         for x in range(2):
             for hi, (even, odd) in enumerate(((0, 1), (3, 2))):
                 zero, one = at_rows(y, even, x, zs), at_rows(y, odd, x, zs)
@@ -596,14 +591,15 @@
             ky_ref[z, x] = jnp.where(me_y == 0, zero, one)
 
 
-def outer_keep(pos, after, own, got):
+def outer_keep(pos, after, own, got, table):
     width = own.shape[2]
     r, third = own.shape[1] // 8, width // 3
-    shapes = [(2, 4, r, third)] * 2 + [(4, 2, r, third)] * 2 + [(2, 2, 2, r, third)] * 2
+    assert 3 * TABLE == r and third == 256
+    shapes = [(9, r, third), (8, r, third)] + [(4, 2, r, third)] * 2 + [(2, 2, 2, r, third)] * 2 + [(r, third)]
     return call(
         outer_keep_kernel,
         "outer_weight_keep",
-        [(pos, "s"), (after, "a"), (own, "v"), (got, "v")],
+        [(pos, "s"), (after, "a"), (own, "v"), (got, "v"), (table, "v")],
         [(near(s), "v") for s in shapes],
     )
 
@@ -658,26 +654,20 @@
     )
 
 
-SMALL = 40
-
-
-def small_rows(pos_ref, task_ref, sums0, sums1, inner_bias, sums2, classes, tables, out, base):
-    quads = len(sums0)
+SMALL = 8
+
+
+def small_rows(sums0, sums1, inner_bias, out, base):
     width = sums1.shape[1]
+    count = inner_bias.shape[0]
     lanes = slice(0, width)
     out[base : base + SMALL, :] = jnp.zeros((SMALL, out.shape[1]), single)
-    for g in range(quads):
-        out[base : base + 2, g * 256 : (g + 1) * 256] = sums0[g][0:2]
+    for g, sums in enumerate(sums0):
+        out[base : base + 2, g * 256 : (g + 1) * 256] = sums[0:2]
     out[base + 2 : base + 5, lanes] = sums1[0:3]
-    at_row = base + 5 + inner_bias.shape[0]
-    out[base + 5 : at_row, lanes] = inner_bias[...]
-    out[at_row : at_row + 3, lanes] = sums2[0:3]
-    lane = lax.broadcasted_iota(jnp.int32, (1, width), 1)
-    out[at_row + 3 : at_row + 4, lanes] = jnp.where(lane == pos_ref[6], sums2[7:8], 0.0)
-    for t in range(tables):
-        mine = jnp.where(task_ref[0] == t, 1.0, 0.0)
-        first = at_row + 4 + t * classes
-        out[first : first + classes, lanes] = sums2[3 : 3 + classes] * mine
+    out[base + 5 : base + 4 + count, lanes] = inner_bias[: count - 1, :]
+    for i in range(3):
+        out[base + i : base + i + 1, width:] = inner_bias[count - 1 : count, i * 256 : (i + 1) * 256]
 
 
 def quad_grads(me, left_ref, ctxt_ref, dattn_ref, parts, g):
@@ -687,26 +677,26 @@
     return pieces
 
 
-def qkv_send_kernel(pos_ref, task_ref, after_ref, left_ref, ctxt_ref, dattn_ref, *refs, other, classes, tables, quads):
+def qkv_send_kernel(pos_ref, after_ref, left_ref, ctxt_ref, dattn_ref, *refs, other, quads):
     parts, refs = refs[: 3 * quads], refs[3 * quads :]
     sums0, refs = refs[:quads], refs[quads:]
-    sums1, inner_bias, sums2, send_ref = refs
+    sums1, inner_bias, send_ref = refs
     me = 1 - pos_ref[1] if other else pos_ref[1]
     count = left_ref.shape[0] // 2
     for g in range(quads):
         for t, piece in enumerate(quad_grads(me, left_ref, ctxt_ref, dattn_ref, parts, g)):
             send_ref[g * count : (g + 1) * count, t * 256 : (t + 1) * 256] = piece
-    small_rows(pos_ref, task_ref, sums0, sums1, inner_bias, sums2, classes, tables, send_ref, quads * count)
-
-
-def qkv_send(pos, task_ids, after, xt, ctxt, dattn, parts, sums0, sums1, inner_bias, sums2, classes, tables, other):
+    small_rows(sums0, sums1, inner_bias, send_ref, quads * count)
+
+
+def qkv_send(pos, after, xt, ctxt, dattn, parts, sums0, sums1, inner_bias, other):
     width = xt.shape[0]
-    assert 5 + inner_bias.shape[0] + 4 + classes * tables <= SMALL
-    return call(
-        functools.partial(qkv_send_kernel, other=other, classes=classes, tables=tables, quads=len(sums0)),
+    assert inner_bias.shape[0] == 4 and width == 768
+    return call(
+        functools.partial(qkv_send_kernel, other=other, quads=len(sums0)),
         "qkv_weight_send",
-        [(pos, "s"), (task_ids, "s"), (after, "a"), (xt, "v"), (ctxt, "v"), (dattn, "v")]
-        + [(p, "v") for p in (*parts, *sums0, sums1, inner_bias, sums2)],
+        [(pos, "s"), (after, "a"), (xt, "v"), (ctxt, "v"), (dattn, "v")]
+        + [(p, "v") for p in (*parts, *sums0, sums1, inner_bias)],
         [(near((len(sums0) * (width // 2) + SMALL, 1024)), "v")],
     )[0]
 
@@ -725,27 +715,54 @@
         out[row : row + r, j * w : (j + 1) * w] = block[j * r : (j + 1) * r]
 
 
-def third_outer_kernel(pos_ref, after_ref, xk, xr, yk, yr, zk, zr, sent, kept, zs, zn):
+def third_outer_kernel(pos_ref, after_ref, xk, xr, yk, yr, zk, zr, block, sent, kept, zs, zn, table_out):
     me_x, side = pos_ref[2], pos_ref[3]
-    wide = xk.shape[2]
+    rows, wide = xk.shape[1:]
     for hi, (keep, send) in enumerate(((side, 1 - side), (3 - side, 2 + side))):
-        sent[hi, :, :wide] = xk[send] + xr[send]
-        sent[hi, :, wide:] = yk[send] + yr[send]
-        kept[hi, :, :wide] = xk[keep] + xr[keep]
-        kept[hi, :, wide:] = yk[keep] + yr[keep]
-    r = xk.shape[1] // 4
+        to = slice(hi * rows, (hi + 1) * rows)
+        sent[to, :wide] = xk[send] + xr[send]
+        sent[to, wide:] = yk[send] + yr[send]
+        kept[to, :wide] = xk[keep] + xr[keep]
+        kept[to, wide:] = yk[keep] + yr[keep]
+    table = block[...] + xr[4]
+    table = jnp.concatenate([table[: rows // 2], table[rows // 2 :]], axis=1)
+    table_out[...] = table
+    sent[2 * rows :, :] = table
+    r = rows // 4
     for y in range(2):
         pack(zs, y * r, zk[y, 1 - me_x] + zr[y, 1 - me_x])
         pack(zn, y * r, zk[y, me_x] + zr[y, me_x])
 
 
-def third_outer(pos, after, xk, xr, yk, yr, zk, zr):
-    r, wide = xk.shape[1:]
-    shapes = [(2, r, 2 * wide)] * 2 + [(r // 2, 4 * wide)] * 2
+def third_outer(pos, after, *arrays):
+    r, wide = arrays[0].shape[1:]
+    shapes = [(2 * r + r // 2, 2 * wide), (2 * r, 2 * wide)] + [(r // 2, 4 * wide)] * 2 + [(r // 2, 2 * wide)]
     return call(
         third_outer_kernel,
         "third_outer_stage",
-        [(pos, "s"), (after, "a")] + [(a, "v") for a in (xk, xr, yk, yr, zk, zr)],
+        [(pos, "s"), (after, "a")] + [(a, "v") for a in arrays],
+        [(near(s), "v") for s in shapes],
+    )
+
+
+def fourth_outer_kernel(pos_ref, after_ref, k, got, table, sent, kept, table_out):
+    me_hi = pos_ref[4]
+    rows = k.shape[0] // 2
+    there, here = rows24(1 - me_hi, rows), rows24(me_hi, rows)
+    sent[:rows, :] = k[there, :] + got[there, :]
+    kept[...] = k[here, :] + got[here, :]
+    total = table[...] + got[2 * rows :, :]
+    table_out[...] = total
+    sent[rows:, :] = total
+
+
+def fourth_outer_stage(pos, after, k, got, table):
+    rows, wide = k.shape[0] // 2, k.shape[1]
+    shapes = [(rows + rows // 2, wide), (rows, wide), (rows // 2, wide)]
+    return call(
+        fourth_outer_kernel,
+        "fourth_stage_outer",
+        [(pos, "s"), (after, "a"), (k, "v"), (got, "v"), (table, "v")],
         [(near(s), "v") for s in shapes],
     )
 
@@ -755,10 +772,10 @@
     count, width = left_ref.shape[0] // 2, left_ref.shape[0]
     r = width // 32
     me_y, me_c, me_x, side = pos_ref[0], pos_ref[1], pos_ref[2], pos_ref[3]
-    total = own_ref[3 * count :, :width] + got_ref[3 * count :, :width]
+    total = own_ref[3 * count :, :] + got_ref[3 * count :, :]
     small[...] = total
-    sx[8 * r : 8 * r + SMALL, :width] = total
-    sx[8 * r + SMALL :, :] = ozs[...]
+    sy[8 * r :, :] = total
+    sx[8 * r :, :] = ozs[...]
 
     def grads(g):
         for t, piece in enumerate(quad_grads(me_c, left_ref, ctxt_ref, dattn_ref, parts, g)):
@@ -782,7 +799,7 @@
                 sx[to, cols] = jnp.where(me_x == 0, one, zero)
                 kx[to, cols] = jnp.where(me_x == 0, zero, one)
     for cols, g in grads(2):
-        sy[:, cols] = jnp.where(me_y == 0, g[8 * r :], g[: 8 * r])
+        sy[: 8 * r, cols] = jnp.where(me_y == 0, g[8 * r :], g[: 8 * r])
         ky[:, cols] = jnp.where(me_y == 0, g[: 8 * r], g[8 * r :])
 
 
@@ -790,7 +807,7 @@
     width = xt.shape[0]
     r = width // 32
     wide = own.shape[1]
-    shapes = [(8 * r + SMALL + 2 * r, wide)] + [(8 * r, wide)] * 5 + [(SMALL, width)]
+    shapes = [(n, wide) for n in (10 * r, 8 * r, 8 * r + SMALL, 8 * r, 8 * r, 8 * r, SMALL)]
     return call(
         qkv_keep_kernel,
         "qkv_weight_keep",
@@ -802,12 +819,12 @@
 
 def second_qkv_kernel(pos_ref, after_ref, kx, rx, ky, ry, kz, rz, small, oz, xs, xk, ys, yk, zs, zk, small_out, oz_out):
     me_y, me_x, me_hi = pos_ref[0], pos_ref[2], pos_ref[4]
-    r, width = kx.shape[0] // 8, small.shape[1]
-    total = small[...] + rx[8 * r : 8 * r + SMALL, :width]
+    r = kx.shape[0] // 8
+    total = small[...] + ry[8 * r :, :]
     small_out[...] = total
-    xs[4 * r : 4 * r + SMALL, :width] = total
-    base = 8 * r + SMALL
-    xs[4 * r + SMALL :, :] = oz[rows24(1 - me_y, r), :] + rx[rows24_from(base, 1 - me_y, r), :]
+    ys[4 * r :, :] = total
+    base = 8 * r
+    xs[4 * r :, :] = oz[rows24(1 - me_y, r), :] + rx[rows24_from(base, 1 - me_y, r), :]
     oz_out[...] = oz[rows24(me_y, r), :] + rx[rows24_from(base, me_y, r), :]
     there, here = rows24(1 - me_y, 4 * r), rows24(me_y, 4 * r)
     xs[: 4 * r, :] = kx[there, :] + rx[there, :]
@@ -826,10 +843,10 @@
 
 def third_qkv_kernel(pos_ref, after_ref, xk, xr, yk, yr, zk, zr, small, sent, kept, zs, zn, small_out):
     me_x, side = pos_ref[2], pos_ref[3]
-    r, width = xk.shape[0] // 4, small.shape[1]
-    total = small[...] + xr[4 * r : 4 * r + SMALL, :width]
+    r = xk.shape[0] // 4
+    total = small[...] + yr[4 * r :, :]
     small_out[...] = total
-    sent[4 * r :, :width] = total
+    sent[4 * r :, :] = total
     for i, (k, got) in enumerate(((xk, xr), (yk, yr))):
         for hi, (keep, send) in enumerate(((side, 1 - side), (3 - side, 2 + side))):
             there, here = rows24(send, r), rows24(keep, r)
@@ -845,10 +862,10 @@
 
 def fourth_qkv_kernel(pos_ref, after_ref, k, got, zk, zr, small, sent, kept, zs, zn, small_out):
     me_y, me_hi = pos_ref[0], pos_ref[4]
-    r, width = k.shape[0] // 4, small.shape[1]
-    total = small[...] + got[4 * r :, :width]
+    r = k.shape[0] // 4
+    total = small[...] + got[4 * r :, :]
     small_out[...] = total
-    sent[2 * r :, :width] = total
+    sent[2 * r :, :] = total
     for i in range(2):
         there, here = rows24(2 * i + 1 - me_hi, r), rows24(2 * i + me_hi, r)
         to = slice(i * r, (i + 1) * r)
@@ -859,22 +876,32 @@
     zn[...] = zk[here, :] + zr[here, :]
 
 
-def qkv_stage(kernel, name, pos, after, arrays, counts, width):
+def qkv_stage(kernel, name, pos, after, arrays, counts):
     wide = arrays[0].shape[1]
     return call(
         kernel,
         name,
         [(pos, "s"), (after, "a")] + [(a, "v") for a in arrays],
-        [(near((n, width if n == SMALL else wide)), "v") for n in counts],
-    )
-
-
-def add_kernel(after_ref, a, b, out):
-    out[...] = a[...] + b[...]
-
-
-def sum_kernel(after, a, b):
-    return call(add_kernel, "sum", [(after, "a"), (a, "v"), (b, "v")], [(near(a.shape), "v")])[0]
+        [(near((n, wide)), "v") for n in counts],
+    )
+
+
+def sum_outer_kernel(after_ref, k, got, table, out, table_out):
+    rows, wide = k.shape
+    out[...] = k[...] + got[:rows, :]
+    total = table[...] + got[rows:, :]
+    block = jnp.concatenate([total[:, : wide // 2], total[:, wide // 2 :]], axis=0)
+    for i in range(3):
+        table_out[:, i * 256 : (i + 1) * 256] = block[i * TABLE : (i + 1) * TABLE]
+
+
+def sum_outer_stage(after, k, got, table):
+    return call(
+        sum_outer_kernel,
+        "sum",
+        [(after, "a"), (k, "v"), (got, "v"), (table, "v")],
+        [(near(k.shape), "v"), (near((TABLE, 768)), "v")],
+    )
 
 
 def last_outer_kernel(after_ref, xy, zk, zr, out, done):
@@ -882,7 +909,7 @@
     wide = xy.shape[1]
     out[:, :wide] = xy[...]
     r = zk.shape[0]
-    z = zk[...] + zr[4 * r + SMALL :, :]
+    z = zk[...] + zr[4 * r :, :]
     w = z.shape[1] // 4
     for j in range(4):
         out[j * r : (j + 1) * r, wide:] = z[:, j * w : (j + 1) * w]
@@ -898,43 +925,46 @@
     )
 
 
-def last_qkv_kernel(pos_ref, k, got, zk, zr, small, q_out, k_out, v_out, o_out, *outs, classes, bias_rows):
+def last_qkv_kernel(pos_ref, k, got, zk, zr, small, table, q_out, k_out, v_out, o_out, *outs, classes, bias_rows):
     *vectors, inner_out, loss_out, head_out = outs
     r = zk.shape[0]
-    width = small.shape[1]
+    width = table.shape[1]
     xs = k[:r, :] + got[:r, :]
     ys = k[r:, :] + got[r : 2 * r, :]
     zs = zk[...] + zr[...]
     for t, out in enumerate((q_out, k_out, v_out, o_out)):
         for g, data in enumerate((zs, xs, ys)):
             out[:, g * 256 : (g + 1) * 256] = data[:, t * 256 : (t + 1) * 256]
-    total = small[...] + got[2 * r :, :width]
+    small_sum = small[...] + got[2 * r :, :]
+    total = small_sum[:, :width]
+    tables = table[...]
     me = pos_ref[5]
-    rolled = pltpu.roll(total, lax.rem(width - me * r, width), 1)
-    after = 5 + bias_rows
-    for out, row in zip(vectors, (0, 1, 2, 3, 4, after, after + 1, after + 2)):
-        out[...] = rolled[row : row + 1, :r]
+    shift = lax.rem(width - me * r, width)
+    rolled, rolled_table = pltpu.roll(total, shift, 1), pltpu.roll(tables[:8], shift, 1)
+    for i, out in enumerate(vectors):
+        out[...] = rolled[i : i + 1, :r] if i < 5 else rolled_table[i - 5 : i - 4, :r]
     part = inner_out.shape[1]
     per_row = width // part
     row = lax.broadcasted_iota(jnp.int32, total.shape, 0)
-    one = jnp.sum(jnp.where(row == 5 + me // per_row, total, 0.0), axis=0, keepdims=True)
+    tail = jnp.concatenate([small_sum[i : i + 1, width:] for i in range(3)], axis=1)
+    mine = me // per_row
+    one = jnp.sum(jnp.where(row == 5 + mine, total, 0.0), axis=0, keepdims=True)
+    one = jnp.where(mine == bias_rows - 1, tail, one)
     one = jnp.broadcast_to(one, (8, width))
     inner_out[...] = pltpu.roll(one, lax.rem(width - (me % per_row) * part, width), 1)[0:1, :part]
     lane = lax.broadcasted_iota(jnp.int32, (1, width), 1)
-    loss_row = total[after + 3 : after + 4]
-    loss_out[...] = jnp.sum(jnp.where(lane == pos_ref[6], loss_row, 0.0), axis=1, keepdims=True)
+    loss_out[...] = jnp.sum(jnp.where(lane == pos_ref[6], tables[3:4], 0.0), axis=1, keepdims=True)
     for t in range(head_out.shape[0]):
-        first = after + 4 + t * classes
-        head_out[t] = total[first : first + classes]
-
-
-def last_qkv(pos, k, got, zk, zr, small, classes, tables, bias_rows):
-    r, width = zk.shape[0], small.shape[1]
+        head_out[t] = tables[4 + t * classes : 4 + (t + 1) * classes]
+
+
+def last_qkv(pos, k, got, zk, zr, small, table, classes, tables, bias_rows):
+    r, width = zk.shape[0], table.shape[1]
     shapes = [(r, width)] * 4 + [(1, r)] * 8 + [(1, r * bias_rows), (1, 1), (tables, classes, width)]
     return call(
         functools.partial(last_qkv_kernel, classes=classes, bias_rows=bias_rows),
         "last_qkv_stage",
-        [(pos, "s")] + [(a, "v") for a in (k, got, zk, zr, small)],
+        [(pos, "s")] + [(a, "v") for a in (k, got, zk, zr, small, table)],
         [(far(s), "v") for s in shapes],
     )
 
@@ -971,33 +1001,46 @@
     )
 
 
-def second_kernel(pos_ref, after_ref, kx, rx, ky, ry, *refs):
+def second_outer_kernel(pos_ref, after_ref, kx, rx, ky, ry, kz, rz, block, xs, xk, ys, yk, zs, zk, block_out):
     me_y, me_x, me_hi = pos_ref[0], pos_ref[2], pos_ref[4]
-    outs = refs[len(refs) % 4 :] if len(refs) == 4 else refs[2:]
-    xs, xk, ys, yk = outs[:4]
+    table = block[...] + rx[8]
+    block_out[...] = table
+    xs[4] = table
+    for z in range(4):
+        there, here = 4 * (1 - me_y) + z, 4 * me_y + z
+        xs[z] = kx[there] + rx[there]
+        xk[z] = kx[here] + rx[here]
+    ys[...] = ky[:, 1 - me_x] + ry[:, 1 - me_x]
+    yk[...] = ky[:, me_x] + ry[:, me_x]
+    zs[...] = kz[:, 1 - me_hi] + rz[:, 1 - me_hi]
+    zk[...] = kz[:, me_hi] + rz[:, me_hi]
+
+
+def second_outer_stage(pos, after, *arrays):
+    r, third = arrays[0].shape[1:]
+    shapes = [(5, r, third)] + [(4, r, third)] * 3 + [(2, 2, r, third)] * 2 + [(r, third)]
+    return call(
+        second_outer_kernel,
+        "second_stage_outer",
+        [(pos, "s"), (after, "a")] + [(a, "v") for a in arrays],
+        [(near(s), "v") for s in shapes],
+    )
+
+
+def second_kernel(pos_ref, after_ref, kx, rx, ky, ry, xs, xk, ys, yk):
+    me_y, me_x = pos_ref[0], pos_ref[2]
     xs[...] = kx[1 - me_y] + rx[1 - me_y]
     xk[...] = kx[me_y] + rx[me_y]
     ys[...] = ky[:, 1 - me_x] + ry[:, 1 - me_x]
     yk[...] = ky[:, me_x] + ry[:, me_x]
-    if len(refs) > 4:
-        kz, rz = refs[:2]
-        zs, zk = outs[4:]
-        zs[...] = kz[:, 1 - me_hi] + rz[:, 1 - me_hi]
-        zk[...] = kz[:, me_hi] + rz[:, me_hi]
-
-
-def second(tag, pos, after, kx, rx, ky, ry, kz=None, rz=None):
-    flat = (4,) + kx.shape[2:]
-    inputs = [kx, rx, ky, ry]
-    shapes = [flat] * 4
-    if kz is not None:
-        inputs += [kz, rz]
-        shapes += [(2, 2) + kz.shape[3:]] * 2
+
+
+def second(pos, after, kx, rx, ky, ry):
     return call(
         second_kernel,
-        f"second_stage_{tag}",
-        [(pos, "s"), (after, "a")] + [(a, "v") for a in inputs],
-        [(near(s), "v") for s in shapes],
+        "second_stage_inner",
+        [(pos, "s"), (after, "a")] + [(a, "v") for a in (kx, rx, ky, ry)],
+        [(near((4,) + kx.shape[2:]), "v")] * 4,
     )
 
 
@@ -1044,10 +1087,10 @@
     kept[...] = xyk[me_hi] + xyr[me_hi]
 
 
-def fourth(tag, pos, after, xyk, xyr):
+def fourth(pos, after, xyk, xyr):
     return call(
         fourth_kernel,
-        f"fourth_stage_{tag}",
+        "fourth_stage_inner",
         [(pos, "s"), (after, "a"), (xyk, "v"), (xyr, "v")],
         [(near(xyk.shape[1:]), "v")] * 2,
     )
@@ -1169,16 +1212,16 @@
         return sums
 
     def small_args():
-        return (ctxt, e["dattn"], parts, sums0, e["sums1"], e["inner_bias"], sums2, classes, tables)
+        return (ctxt, e["dattn"], parts, sums0, e["sums1"], e["inner_bias"])
 
     e = {}
 
     def send_outer(after):
-        e["o_send"] = outer_send(pos, after, act, ddown, True)
-        return e["o_send"]
+        e["o_send"], e["table"] = outer_send(pos, task_ids, after, act, ddown, sums2, classes, tables)
+        return e["table"]
 
     def rest_outer(after):
-        e["o_rest"] = outer_send(pos, after, act, ddown, False)
+        e["o_rest"] = outer_rest(pos, after, act, ddown)
         return e["o_rest"]
 
     def do_inner_grad(after):
@@ -1208,13 +1251,14 @@
         return after
 
     def send_qkv(after):
-        e["qkv_s"] = qkv_send(pos, task_ids, after, e["xt"], *small_args(), True)
+        e["qkv_s"] = qkv_send(pos, after, e["xt"], *small_args(), True)
         return e["qkv_s"]
 
     def keep_outer(after):
-        osx, okx, osy, oky, osz, okz = outer_keep(pos, after, e["o_rest"], swap(e["o_send"], "c"))
-        e["o1"] = (okx, swap(osx, "x"), oky, swap(osy, "y"), okz, swap(osz, "near"))
-        return okx
+        got = swap(e["o_send"], "c")
+        osx, okx, osy, oky, osz, okz, block = outer_keep(pos, after, e["o_rest"], got, e["table"])
+        e["o1"] = (okx, swap(osx, "x"), oky, swap(osy, "y"), okz, swap(osz, "near"), block)
+        return block
 
     def keep_inner(after):
         isx, ikx, isy, iky = inner_keep(pos, after, h1t, e["dinner"], swap(e["i_send"], "c"))
@@ -1222,19 +1266,19 @@
         return ikx
 
     def second_outer(after):
-        xs, xk, ys, yk, zs, zk = second("outer", pos, after, *e["o1"])
-        e["o2"] = (xk, swap(xs, "y"), yk, swap(ys, "x"), zk, swap(zs, "far"))
-        return xk
+        xs, xk, ys, yk, zs, zk, block = second_outer_stage(pos, after, *e["o1"])
+        e["o2"] = (xk, swap(xs, "y"), yk, swap(ys, "x"), zk, swap(zs, "far"), block)
+        return block
 
     def second_inner(after):
-        xs, xk, ys, yk = second("inner", pos, after, *e["i1"])
+        xs, xk, ys, yk = second(pos, after, *e["i1"])
         e["i2"] = (xk, swap(xs, "y"), yk, swap(ys, "x"))
         return xk
 
     def do_third_outer(after):
-        sent, kept, e["ozs"], e["oz"] = third_outer(pos, after, *e["o2"])
-        e["o3"] = (kept, swap(sent, "near"))
-        return kept
+        sent, kept, e["ozs"], e["oz"], table = third_outer(pos, after, *e["o2"])
+        e["o3"] = (kept, swap(sent, "near"), table)
+        return table
 
     def third_inner(after):
         sent, kept = third(pos, after, *e["i2"])
@@ -1242,18 +1286,18 @@
         return kept
 
     def fourth_outer(after):
-        sent, kept = fourth("outer", pos, after, *e["o3"])
-        e["o4"] = (kept, swap(sent, "far"))
-        return kept
+        sent, kept, table = fourth_outer_stage(pos, after, *e["o3"])
+        e["o4"] = (kept, swap(sent, "far"), table)
+        return table
 
     def fourth_inner(after):
-        sent, kept = fourth("inner", pos, after, *e["i3"])
+        sent, kept = fourth(pos, after, *e["i3"])
         e["i4"] = (kept, swap(sent, "far"))
         return kept
 
     def sum_outer(after):
-        e["outer_xy"] = sum_kernel(after, *e["o4"])
-        return e["outer_xy"]
+        e["outer_xy"], e["table_sum"] = sum_outer_stage(after, *e["o4"])
+        return e["table_sum"]
 
     def last_inner(after):
         e["inner_s"], after = last(after, *e["i4"], None, None, (((0, 0, 2 * f2),),))
@@ -1271,7 +1315,7 @@
         return small
 
     def stage(kernel, name, after, arrays, counts):
-        return qkv_stage(kernel, name, pos, after, arrays, counts, width)
+        return qkv_stage(kernel, name, pos, after, arrays, counts)
 
     def second_qkv(after):
         xs, xk, ys, yk, zs, zk, small, e["oz2"] = stage(
@@ -1279,7 +1323,7 @@
             "second_qkv_stage",
             after,
             e["q1"],
-            [5 * r + SMALL, 4 * r, 4 * r, 4 * r, 4 * r, 4 * r, SMALL, r],
+            [5 * r, 4 * r, 4 * r + SMALL, 4 * r, 4 * r, 4 * r, SMALL, r],
         )
         e["q2"] = (xk, swap(xs, "y"), yk, swap(ys, "x"), zk, swap(zs, "far"), small)
         return small
@@ -1299,7 +1343,7 @@
         return small
 
     def do_last_qkv(after):
-        e["last"] = last_qkv(pos, *e["q4"], classes, tables, ff // width)
+        e["last"] = last_qkv(pos, *e["q4"], e["table_sum"], classes, tables, ff // width)
         return after
 
     steps = {
@@ -1339,12 +1383,12 @@
         head_grad = rest[-1]
     else:
         after = do_first_norm(send_inner(do_inner_grad(send_outer(sums2))))
-        o_keep = rest_outer(after)
+        after = rest_outer(after)
         i_keep = inner_send(pos, after, h1t, e["dinner"], False)
         for quad in range(quads):
             after = back(quad, after)
         after = do_tokens(send_qkv(after))
-        qkv_k = qkv_send(pos, task_ids, after, e["xt"], *small_args(), False)
+        qkv_k = qkv_send(pos, after, e["xt"], *small_args(), False)
         o_send, i_send, qkv_s = e["o_send"], e["i_send"], e["qkv_s"]
 
         def whole_rows(sent, kept):
@@ -1357,7 +1401,8 @@
         def by_rows(array):
             return array.reshape(2, -1, array.shape[-1])
 
-        outer_s = scatter(whole_rows(o_send, o_keep))
+        part = ff // 4
+        outer_s = scatter(whole_rows(o_send[: 2 * part].reshape(2, part, width), e["o_rest"]))
         inner_s = scatter(
             jnp.concatenate([whole_rows(by_rows(i_send[j]), by_rows(i_keep[j])) for j in range(2)], axis=-1)
         )
@@ -1370,7 +1415,7 @@
         query_s, key_s, value_s, output_s = [
             scatter(whole_rows(tensor(qkv_s, t), tensor(qkv_k, t))) for t in range(4)
         ]
-        small = lax.psum(qkv_s[quads * count :, :width], ALL_AXES)
+        small = lax.psum(jnp.concatenate([qkv_s[quads * count :, :width], e["inner_bias"], e["table"]]), ALL_AXES)
         devices = lax.axis_size("task") * lax.axis_size("batch")
 
         def mine(array):
@@ -1378,11 +1423,10 @@
             size = flat.shape[0] // devices
             return lax.dynamic_slice(flat, (where * size,), (size,))
 
-        last_row = 5 + ff // width
-        vector_s = [mine(small[i]) for i in (0, 1, 2, 3, 4, last_row, last_row + 1, last_row + 2)]
-        vector_s.append(mine(small[5:last_row]))
-        vector_s.append(lax.dynamic_slice(small, (last_row + 3, task_index), (1, 1)).reshape(1))
-        head_grad = small[last_row + 4 : last_row + 4 + classes * tables].reshape(head_table.shape)
+        table = small[SMALL + ff // width :]
+        vector_s = [mine(a) for a in (*small[:5], *table[:3], small[SMALL : SMALL + ff // width])]
+        vector_s.append(lax.dynamic_slice(table, (3, task_index), (1, 1)).reshape(1))
+        head_grad = table[4 : 4 + classes * tables].reshape(head_table.shape)
     token_grad = e["token_grad"].reshape(tokens.shape)
     bias_q, bias_v, gain1, bias1, bias_o, gain2, bias2, bias_d, bias_i, loss = vector_s
     return (

time: 222 us -> 217 us (0.977)
  the two profiles are of different devices: /device:TPU:8 before, /device:TPU:0 now
where the time goes in v1:
time: 217 us; the launch traced here: 213 us
  Pallas kernels  109 us (50%)
  waiting for transfers between devices  63.9 us (29%)
  starting transfers between devices  34.3 us (16%)
  local copies, waits for them, and re-layouts  3.48 us (2%)
  between operations  2.72 us (1%)
    pallas_call x28, Pallas kernels, call(): pl.pallas_call(kernel, in_specs=[specs[p] for _, p in inputs], out_specs=...  109 us
    ppermute x27, waiting for transfers between devices, swap(): return lax.ppermute(array, ALL_AXES, PAIRS[name])  63.9 us
    ppermute x27, starting transfers between devices, swap(): return lax.ppermute(array, ALL_AXES, PAIRS[name])  34.3 us
  transfers between devices with their start and end apart: 27, of which 14 were waited for; matrix products, arithmetic and copies ran while one was open for 0% of the time, Pallas kernels for 30%

profile of v1, /device:TPU:0, one launch (start us, length us, event | category | flops | bytes accessed | tf_op | source)
XLA Modules:
  0.0 213.4 jit_solution(11532175935509213668)
XLA Ops:
  2.8 18.3 %attention_forward.1 = (bf16[1024,768]{1,0:T(8,128)(2,1)S(1)}, bf16[1024,768]{1,0:T(8,128)(2,1)}, bf16[1024,768]{1,0:T(8,128)(2,1)}, bf16[1024,768]{1,0:T(8,128)...) custom-call(s32[2]{0:T(128)S(1)} %copy-done.17, ...), custom_call_target="tpu_custom_call" | custom-call | flops 1000000 | bytes 1024 | tf_op jit(solution)/shard_map/attention_forward/pallas_call | solution.py:106
  21.2 18.9 %middle_forward.1 = (bf16[1024,768]{1,0:T(8,128)(2,1)}, bf16[1024,768]{1,0:T(8,128)(2,1)S(1)}, f32[1024,128]{1,0:T(8,128)S(1)}, bf16[768,1024]{1,0:T(8,128)(2,1)...) custom-call(s32[1]{0:T(128)S(6)} %copy.44.task_ref, ...), custom_call_target="tpu_custom_call" | custom-call | flops 1000000 | bytes 1024 | tf_op jit(solution)/shard_map/middle_forward/pallas_call | solution.py:106
  40.1 3.2 %outer_weight_send.1 = (f32[1568,768]{1,0:T(8,128)S(1)}, f32[32,768]{1,0:T(8,128)S(1)}) custom-call(s32[7]{0:T(128)S(1)} %stack.31.pos_ref, s32[1]{0:T(128)S(6)} %copy.44.task_ref, f32[8,768]{1,0:T(8,128)S(1)} %get-tuple-element.147.after_ref.sums2, bf16[1024,3072]{1,0:T(8,128)(2,1)S(1)} %get-tuple-element.148.act_ref, ...), custom_call_target="tpu_custom_call" | custom-call | flops 3000000000 | bytes 1024 | tf_op jit(solution)/shard_map/outer_weight_send/pallas_call | solution.py:106
  43.8 6.8 %inner_grad.1 = (bf16[1024,3072]{1,0:T(8,128)(2,1)S(1)}, f32[4,768]{1,0:T(4,128)S(1)}) custom-call(f32[32,768]{1,0:T(8,128)S(1)} %get-tuple-element.150.after_ref.table_ref, bf16[1024,768]{1,0:T(8,128)(2,1)S(1)} %get-tuple-element.149.ddown_ref, bf16[3072,768]{1,0:T(8,128)(2,1)S(1)} %get-tuple-element.145.wd_ref, ...), custom_call_target="tpu_custom_call", output_to_operand_aliasing={{0}: (3, {})} | custom-call | flops 3000000000 | bytes 1024 | tf_op jit(solution)/shard_map/inner_grad/pallas_call | solution.py:106
  50.6 3.2 %inner_weight_send.1.after_ref = f32[2,384,1536]{2,1,0:T(8,128)S(1)} custom-call(s32[7]{0:T(128)S(1)} %stack.31.pos_ref, f32[4,768]{1,0:T(4,128)S(1)} %get-tuple-element.152.after_ref.refs_13_, bf16[768,1024]{1,0:T(8,128)(2,1)S(1)} %get-tuple-element.153.left_ref, bf16[1024,3072]{1,0:T(8,128)(2,1)S(1)} %get-tuple-element.154.right_ref.dinner_ref), custom_call_target="tpu_custom_call" | custom-call | flops 10000000000 | bytes 1024 | tf_op jit(solution)/shard_map/inner_weight_send/pallas_call | solution.py:106
  53.9 3.2 %outer_weight_rest.1.after_ref.own_ref = f32[2,768,768]{2,1,0:T(8,128)S(1)} custom-call(s32[7]{0:T(128)S(1)} %stack.31.pos_ref, f32[2,384,1536]{2,1,0:T(8,128)S(1)} %inner_weight_send.1.after_ref, bf16[1024,3072]{1,0:T(8,128)(2,1)S(1)} %get-tuple-element.148.act_ref, bf16[1024,768]{1,0:T(8,128)(2,1)S(1)} %get-tuple-element.149.ddown_ref), custom_call_target="tpu_custom_call" | custom-call | flops 1000000 | bytes 1024 | tf_op jit(solution)/shard_map/outer_weight_rest/pallas_call | solution.py:106
  58.2 3.0 %collective-permute-start.2 = (f32[9,96,256]{2,1,0:T(8,128)S(1)}, f32[9,96,256]{2,1,0:T(8,128)S(1)}, u32[]{:S(2)}, u32[]{:S(2)}) collective-permute-start(f32[9,96,256]{2,1,0:T(8,128)S(1)} %get-tuple-element.168), channel_id=1, source_target_pairs={{0,1},{1,0},{2,3},{3,2},{4,5},{5,4},{6,7},{7,6},{8,9},{9,8},{10,11... | collective-permute-start | bytes 2654216 | tf_op jit(solution)/shard_map/ppermute | solution.py:1144
  62.8 1.6 collective-permute-start.4
  64.4 3.2 %inner_weight_keep.1 = (f32[2,4,24,1536]{3,2,1,0:T(8,128)S(1)}, f32[2,4,24,1536]{3,2,1,0:T(8,128)S(1)}, f32[4,2,24,1536]{3,2,1,0:T(8,128)S(1)}, f32[4,2,24,1536]{3,2,1,0:T(8,128)S(1)}) custom-call(s32[7]{0:T(128)S(1)} %stack.31.pos_ref, f32[96,256]{1,0:T(8,128)S(1)} %get-tuple-element.156.after_ref.block, bf16[768,1024]{1,0:T(8,128)(2,1)S(1)} %get-tuple-element.153.left_ref, ...), custom_call_target="tpu_custom_call" | custom-call | flops 1000000000 | bytes 1024 | tf_op jit(solution)/shard_map/inner_weight_keep/pallas_call | solution.py:106
  69.3 10.5 %first_norm_back.1 = (f32[1024,768]{1,0:T(8,128)S(1)}, bf16[1024,768]{1,0:T(8,128)(2,1)S(1)}, bf16[1024,768]{1,0:T(8,128)(2,1)S(1)}, bf16[768,1024]{1,0:T(8,128)(2,1)S(1)}, f32[8,768]{1,0:T(8,128)S(1)}) custom-call(f32[2,4,24,1536]{3,2,1,0:T(8,128)S(1)} %get-tuple-element.157.after_ref.kx, bf16[1024,3072]{1,0:T(8,128)(2,1)S(1)} %get-tuple-element.154.right_ref.dinner_ref, ...), custom_call_target="tpu_custom_call" | custom-call | flops 1000000 | bytes 1024 | tf_op jit(solution)/shard_map/first_norm_back/pallas_call | solution.py:106
  79.9 6.6 %attention_back_0.1 = (bf16[1024,256]{1,0:T(8,128)(2,1)S(1)}, bf16[1024,256]{1,0:T(8,128)(2,1)S(1)}, bf16[1024,256]{1,0:T(8,128)(2,1)S(1)}, f32[8,256]{1,0:T(8,128)S(1)}) custom-call(s32[2]{0:T(128)S(1)} %copy-done.18, f32[8,768]{1,0:T(8,128)S(1)} %get-tuple-element.160.after_ref.refs_12_, bf16[1024,768]{1,0:T(8,128)(2,1)S(1)} %copy-done.6, ...), custom_call_target="tpu_custom_call" | custom-call | flops 1000000 | bytes 1024 | tf_op jit(solution)/shard_map/attention_back_0/pallas_call | solution.py:106
  88.4 3.2 %collective-permute-start.9 = (f32[2,2,96,256]{3,2,1,0:T(8,128)S(1)}, f32[2,2,96,256]{3,2,1,0:T(8,128)S(1)}, u32[]{:S(2)}, u32[]{:S(2)}) collective-permute-start(f32[2,2,96,256]{3,2,1,0:T(8,128)S(1)} %get-tuple-element.185), channel_id=1, source_target_pairs={{0,6},{1,7},{2,4},{3,5},{4,2},{5,3},{6,0},{7,1},{8,14},{9,15},{10,... | collective-permute-start | bytes 1179656 | tf_op jit(solution)/shard_map/ppermute | solution.py:1144
  92.4 6.4 %attention_back_1.1 = (bf16[1024,256]{1,0:T(8,128)(2,1)S(1)}, bf16[1024,256]{1,0:T(8,128)(2,1)S(1)}, bf16[1024,256]{1,0:T(8,128)(2,1)S(1)}, f32[8,256]{1,0:T(8,128)S(1)}) custom-call(s32[2]{0:T(128)S(1)} %copy-done.18, f32[96,256]{1,0:T(8,128)S(1)} %get-tuple-element.173.after_ref.block, bf16[1024,768]{1,0:T(8,128)(2,1)S(1)} %copy-done.6, ...), custom_call_target="tpu_custom_call" | custom-call | flops 10000000000 | bytes 1024 | tf_op jit(solution)/shard_map/attention_back_1/pallas_call | solution.py:106
  98.7 8.2 %collective-permute-done.5.rx = f32[2,4,24,1536]{3,2,1,0:T(8,128)S(1)} collective-permute-done((f32[2,4,24,1536]{3,2,1,0:T(8,128)S(1)}, f32[2,4,24,1536]{3,2,1,0:T(8,128)S(1)}, u32[]{:S(2)}, u32[]{:S(2)}) %collective-permute-start.5) | collective-permute-done | bytes 1179680 | tf_op jit(solution)/shard_map/ppermute | solution.py:1144
  107.8 6.6 %attention_back_2.1 = (bf16[1024,256]{1,0:T(8,128)(2,1)S(1)}, bf16[1024,256]{1,0:T(8,128)(2,1)S(1)}, bf16[1024,256]{1,0:T(8,128)(2,1)S(1)}, f32[8,256]{1,0:T(8,128)S(1)}) custom-call(s32[2]{0:T(128)S(1)} %copy-done.18, f32[4,24,1536]{2,1,0:T(8,128)S(1)} %get-tuple-element.178.after_ref.xk, bf16[1024,768]{1,0:T(8,128)(2,1)S(1)} %copy-done.6, ...), custom_call_target="tpu_custom_call" | custom-call | flops 10000000000 | bytes 1024 | tf_op jit(solution)/shard_map/attention_back_2/pallas_call | solution.py:106
  117.7 3.2 %qkv_weight_send.1.after_ref.own_ref = f32[1160,1024]{1,0:T(8,128)S(1)} custom-call(s32[7]{0:T(128)S(1)} %stack.31.pos_ref, f32[48,512]{1,0:T(8,128)S(1)} %get-tuple-element.186.after_ref.table, bf16[768,1024]{1,0:T(8,128)(2,1)S(1)} %get-tuple-element.187.left_ref, bf16[768,1024]{1,0:T(8,128)(2,1)S(1)} %copy-done.1, ...), custom_call_target="tpu_custom_call" | custom-call | flops 3000000000 | bytes 1024 | tf_op jit(solution)/shard_map/qkv_weight_send/pallas_call | solution.py:106
  121.0 1.6 collective-permute-start.11
  123.1 1.6 collective-permute-start.13
  124.6 4.3 %collective-permute-done.10.got_ref = f32[1160,1024]{1,0:T(8,128)S(1)} collective-permute-done((f32[1160,1024]{1,0:T(8,128)S(1)}, f32[1160,1024]{1,0:T(8,128)S(1)}, u32[]{:S(2)}, u32[]{:S(2)}) %collective-permute-start.10) | collective-permute-done | bytes 4751392 | tf_op jit(solution)/shard_map/ppermute | solution.py:1144
  128.9 3.3 %qkv_weight_keep.1 = (f32[240,1024]{1,0:T(8,128)S(1)}, f32[192,1024]{1,0:T(8,128)S(1)}, f32[200,1024]{1,0:T(8,128)S(1)}, f32[192,1024]{1,0:T(8,128)S(1)}, f32[19...) custom-call(s32[7]{0:T(128)S(1)} %stack.31.pos_ref, ...), custom_call_target="tpu_custom_call" | custom-call | flops 100000000 | bytes 1024 | tf_op jit(solution)/shard_map/qkv_weight_keep/pallas_call | solution.py:106
  132.2 1.6 collective-permute-start.16
  135.3 1.8 collective-permute-done.11.xr
  139.9 5.4 %token_grad.1 = (f32[1024,768]{1,0:T(8,128)}, f32[8,128]{1,0:T(8,128)S(1)}) custom-call(f32[2,24,3072]{2,1,0:T(8,128)S(1)} %get-tuple-element.204.after_ref.xyk, f32[1024,768]{1,0:T(8,128)S(1)} %get-tuple-element.205.dr1_ref, bf16[768,768]{1,0:T(8,128)(2,1)S(1)} %copy-done.3, bf16[768,768]{1,0:T(8,128)(2,1)S(1)} %copy-done.4, ...), custom_call_target="tpu_custom_call" | custom-call | flops 3000000000 | bytes 1024 | tf_op jit(solution)/shard_map/token_grad/pallas_call | solution.py:106
  146.0 3.7 %collective-permute-start.17 = (f32[144,512]{1,0:T(8,128)S(1)}, f32[144,512]{1,0:T(8,128)S(1)}, u32[]{:S(2)}, u32[]{:S(2)}) collective-permute-start(f32[144,512]{1,0:T(8,128)S(1)} %get-tuple-element.220), channel_id=1, source_target_pairs={{0,6},{1,7},{2,4},{3,5},{4,2},{5,3},{6,0},{7,1},{8,14},{9,15},{10,... | collective-permute-start | bytes 884744 | tf_op jit(solution)/shard_map/ppermute | solution.py:1144
  149.6 4.6 %collective-permute-done.16.rz = f32[192,1024]{1,0:T(8,128)S(1)} collective-permute-done((f32[192,1024]{1,0:T(8,128)S(1)}, f32[192,1024]{1,0:T(8,128)S(1)}, u32[]{:S(2)}, u32[]{:S(2)}) %collective-permute-start.16) | collective-permute-done | bytes 786464 | tf_op jit(solution)/shard_map/ppermute | solution.py:1144
  154.3 5.8 %collective-permute-done.14.rx = f32[240,1024]{1,0:T(8,128)S(1)} collective-permute-done((f32[240,1024]{1,0:T(8,128)S(1)}, f32[240,1024]{1,0:T(8,128)S(1)}, u32[]{:S(2)}, u32[]{:S(2)}) %collective-permute-start.14) | collective-permute-done | bytes 983072 | tf_op jit(solution)/shard_map/ppermute | solution.py:1144
  160.8 4.0 %collective-permute-start.20 = (f32[96,1024]{1,0:T(8,128)S(1)}, f32[96,1024]{1,0:T(8,128)S(1)}, u32[]{:S(2)}, u32[]{:S(2)}) collective-permute-start(f32[96,1024]{1,0:T(8,128)S(1)} %get-tuple-element.227), channel_id=1, source_target_pairs={{0,6},{1,7},{2,4},{3,5},{4,2},{5,3},{6,0},{7,1},{8,14},{9,15},{10,... | collective-permute-start | bytes 1179656 | tf_op jit(solution)/shard_map/ppermute | solution.py:1144
  166.8 15.6 %collective-permute-done.20.zr = f32[96,1024]{1,0:T(8,128)S(1)} collective-permute-done((f32[96,1024]{1,0:T(8,128)S(1)}, f32[96,1024]{1,0:T(8,128)S(1)}, u32[]{:S(2)}, u32[]{:S(2)}) %collective-permute-start.20) | collective-permute-done | bytes 393248 | tf_op jit(solution)/shard_map/ppermute | solution.py:1144
  185.3 1.6 collective-permute-start.26
  189.1 13.6 %collective-permute-done.22.got = f32[104,1024]{1,0:T(8,128)S(1)} collective-permute-done((f32[104,1024]{1,0:T(8,128)S(1)}, f32[104,1024]{1,0:T(8,128)S(1)}, u32[]{:S(2)}, u32[]{:S(2)}) %collective-permute-start.22) | collective-permute-done | bytes 426016 | tf_op jit(solution)/shard_map/ppermute | solution.py:1144
  205.1 2.9 %collective-permute-done.25.zr = f32[24,1024]{1,0:T(8,128)S(1)} collective-permute-done((f32[24,1024]{1,0:T(8,128)S(1)}, f32[24,1024]{1,0:T(8,128)S(1)}, u32[]{:S(2)}, u32[]{:S(2)}) %collective-permute-start.25) | collective-permute-done | bytes 98336 | tf_op jit(solution)/shard_map/ppermute | solution.py:1144
  208.1 3.1 %collective-permute-done.24.got = f32[56,1024]{1,0:T(8,128)S(1)} collective-permute-done((f32[56,1024]{1,0:T(8,128)S(1)}, f32[56,1024]{1,0:T(8,128)S(1)}, u32[]{:S(2)}, u32[]{:S(2)}) %collective-permute-start.24) | collective-permute-done | bytes 229408 | tf_op jit(solution)/shard_map/ppermute | solution.py:1144
  (97 shorter events, 30.3 us)
Async XLA Ops:
  2.8 18.4 %copy-start.12 = (bf16[768]{0:T(1024)(128)(2,1)S(1)}, bf16[768]{0:T(1024)(128)(2,1)}, u32[]{:S(2)}) copy-start(bf16[768]{0:T(1024)(128)(2,1)} %bo_ref.1) | copy-start | bytes 4612
  2.8 18.4 %copy-start.13 = (bf16[768]{0:T(1024)(128)(2,1)S(1)}, bf16[768]{0:T(1024)(128)(2,1)}, u32[]{:S(2)}) copy-start(bf16[768]{0:T(1024)(128)(2,1)} %b1_ref.1) | copy-start | bytes 4612
  2.8 18.4 %copy-start.14 = (bf16[768]{0:T(1024)(128)(2,1)S(1)}, bf16[768]{0:T(1024)(128)(2,1)}, u32[]{:S(2)}) copy-start(bf16[768]{0:T(1024)(128)(2,1)} %bd_ref.1) | copy-start | bytes 4612
  2.8 18.4 %copy-start.15 = (bf16[768]{0:T(1024)(128)(2,1)S(1)}, bf16[768]{0:T(1024)(128)(2,1)}, u32[]{:S(2)}) copy-start(bf16[768]{0:T(1024)(128)(2,1)} %g2_ref.1) | copy-start | bytes 4612
  2.8 18.4 %copy-start.16 = (bf16[768]{0:T(1024)(128)(2,1)S(1)}, bf16[768]{0:T(1024)(128)(2,1)}, u32[]{:S(2)}) copy-start(bf16[768]{0:T(1024)(128)(2,1)} %b2_ref.1) | copy-start | bytes 4612
  43.3 13.8 %collective-permute-start = (f32[1568,768]{1,0:T(8,128)S(1)}, f32[1568,768]{1,0:T(8,128)S(1)}, u32[]{:S(2)}, u32[]{:S(2)}) collective-permute-start(f32[1568,768]{1,0:T(8,128)S(1)} %get-tuple-element.155), channel_id=1, source_target_pairs={{0,8},{1,9},{2,10},{3,11},{4,12},{5,13},{6,14},{7,15},{8,0},{9,1},... | collective-permute-start | bytes 14450696 | tf_op jit(solution)/shard_map/ppermute | solution.py:1144
  53.8 10.6 %collective-permute-start.1 = (f32[2,384,1536]{2,1,0:T(8,128)S(1)}, f32[2,384,1536]{2,1,0:T(8,128)S(1)}, u32[]{:S(2)}, u32[]{:S(2)}) collective-permute-start(f32[2,384,1536]{2,1,0:T(8,128)S(1)} %inner_weight_send.1.after_ref), channel_id=1, source_target_pairs={{0,8},{1,9},{2,10},{3,11},{4,12},{5,13},{6,14},{7,15},{8,0},{9,1},... | collective-permute-start | bytes 14155784 | tf_op jit(solution)/shard_map/ppermute | solution.py:1144
  58.2 28.2 %collective-permute-start.2 = (f32[9,96,256]{2,1,0:T(8,128)S(1)}, f32[9,96,256]{2,1,0:T(8,128)S(1)}, u32[]{:S(2)}, u32[]{:S(2)}) collective-permute-start(f32[9,96,256]{2,1,0:T(8,128)S(1)} %get-tuple-element.168), channel_id=1, source_target_pairs={{0,1},{1,0},{2,3},{3,2},{4,5},{5,4},{6,7},{7,6},{8,9},{9,8},{10,11... | collective-permute-start | bytes 2654216 | tf_op jit(solution)/shard_map/ppermute | solution.py:1144
  61.3 25.2 %collective-permute-start.3 = (f32[4,2,96,256]{3,2,1,0:T(8,128)S(1)}, f32[4,2,96,256]{3,2,1,0:T(8,128)S(1)}, u32[]{:S(2)}, u32[]{:S(2)}) collective-permute-start(f32[4,2,96,256]{3,2,1,0:T(8,128)S(1)} %get-tuple-element.170), channel_id=1, source_target_pairs={{0,16},{1,17},{2,18},{3,19},{4,20},{5,21},{6,22},{7,23},{8,24},{9,... | collective-permute-start | bytes 2359304 | tf_op jit(solution)/shard_map/ppermute | solution.py:1144
  62.8 23.7 %collective-permute-start.4 = (f32[2,2,2,96,256]{4,3,2,1,0:T(8,128)S(1)}, f32[2,2,2,96,256]{4,3,2,1,0:T(8,128)S(1)}, u32[]{:S(2)}, u32[]{:S(2)}) collective-permute-start(f32[2,2,2,96,256]{4,3,2,1,0:T(8,128)S(1)} %get-tuple-element.172), channel_id=1, source_target_pairs={{0,2},{1,3},{2,0},{3,1},{4,6},{5,7},{6,4},{7,5},{8,10},{9,11},{10,... | collective-permute-start | bytes 2359304 | tf_op jit(solution)/shard_map/ppermute | solution.py:1144
  67.6 39.3 %collective-permute-start.5 = (f32[2,4,24,1536]{3,2,1,0:T(8,128)S(1)}, f32[2,4,24,1536]{3,2,1,0:T(8,128)S(1)}, u32[]{:S(2)}, u32[]{:S(2)}) collective-permute-start(f32[2,4,24,1536]{3,2,1,0:T(8,128)S(1)} %get-tuple-element.175), channel_id=1, source_target_pairs={{0,1},{1,0},{2,3},{3,2},{4,5},{5,4},{6,7},{7,6},{8,9},{9,8},{10,11... | collective-permute-start | bytes 3538952 | tf_op jit(solution)/shard_map/ppermute | solution.py:1144
  68.2 38.8 %collective-permute-start.6 = (f32[4,2,24,1536]{3,2,1,0:T(8,128)S(1)}, f32[4,2,24,1536]{3,2,1,0:T(8,128)S(1)}, u32[]{:S(2)}, u32[]{:S(2)}) collective-permute-start(f32[4,2,24,1536]{3,2,1,0:T(8,128)S(1)} %get-tuple-element.177), channel_id=1, source_target_pairs={{0,16},{1,17},{2,18},{3,19},{4,20},{5,21},{6,22},{7,23},{8,24},{9,... | collective-permute-start | bytes 3538952 | tf_op jit(solution)/shard_map/ppermute | solution.py:1144
  87.3 27.5 %collective-permute-start.8 = (f32[4,96,256]{2,1,0:T(8,128)S(1)}, f32[4,96,256]{2,1,0:T(8,128)S(1)}, u32[]{:S(2)}, u32[]{:S(2)}) collective-permute-start(f32[4,96,256]{2,1,0:T(8,128)S(1)} %get-tuple-element.183), channel_id=1, source_target_pairs={{0,1},{1,0},{2,3},{3,2},{4,5},{5,4},{6,7},{7,6},{8,9},{9,8},{10,11... | collective-permute-start | bytes 1179656 | tf_op jit(solution)/shard_map/ppermute | solution.py:1144
  88.4 26.4 %collective-permute-start.9 = (f32[2,2,96,256]{3,2,1,0:T(8,128)S(1)}, f32[2,2,96,256]{3,2,1,0:T(8,128)S(1)}, u32[]{:S(2)}, u32[]{:S(2)}) collective-permute-start(f32[2,2,96,256]{3,2,1,0:T(8,128)S(1)} %get-tuple-element.185), channel_id=1, source_target_pairs={{0,6},{1,7},{2,4},{3,5},{4,2},{5,3},{6,0},{7,1},{8,14},{9,15},{10,... | collective-permute-start | bytes 1179656 | tf_op jit(solution)/shard_map/ppermute | solution.py:1144
  91.6 24.7 %collective-permute-start.7 = (f32[5,96,256]{2,1,0:T(8,128)S(1)}, f32[5,96,256]{2,1,0:T(8,128)S(1)}, u32[]{:S(2)}, u32[]{:S(2)}) collective-permute-start(f32[5,96,256]{2,1,0:T(8,128)S(1)} %get-tuple-element.181), channel_id=1, source_target_pairs={{0,16},{1,17},{2,18},{3,19},{4,20},{5,21},{6,22},{7,23},{8,24},{9,... | collective-permute-start | bytes 1474568 | tf_op jit(solution)/shard_map/ppermute | solution.py:1144
  120.9 8.0 %collective-permute-start.10 = (f32[1160,1024]{1,0:T(8,128)S(1)}, f32[1160,1024]{1,0:T(8,128)S(1)}, u32[]{:S(2)}, u32[]{:S(2)}) collective-permute-start(f32[1160,1024]{1,0:T(8,128)S(1)} %qkv_weight_send.1.after_ref.own_ref), channel_id=1, source_target_pairs={{0,8},{1,9},{2,10},{3,11},{4,12},{5,13},{6,14},{7,15},{8,0},{9,1},... | collective-permute-start | bytes 14254088 | tf_op jit(solution)/shard_map/ppermute | solution.py:1144
  121.0 16.1 %collective-permute-start.11 = (f32[4,24,1536]{2,1,0:T(8,128)S(1)}, f32[4,24,1536]{2,1,0:T(8,128)S(1)}, u32[]{:S(2)}, u32[]{:S(2)}) collective-permute-start(f32[4,24,1536]{2,1,0:T(8,128)S(1)} %get-tuple-element.201), channel_id=1, source_target_pairs={{0,16},{1,17},{2,18},{3,19},{4,20},{5,21},{6,22},{7,23},{8,24},{9,... | collective-permute-start | bytes 1769480 | tf_op jit(solution)/shard_map/ppermute | solution.py:1144
  122.5 15.4 %collective-permute-start.12 = (f32[4,24,1536]{2,1,0:T(8,128)S(1)}, f32[4,24,1536]{2,1,0:T(8,128)S(1)}, u32[]{:S(2)}, u32[]{:S(2)}) collective-permute-start(f32[4,24,1536]{2,1,0:T(8,128)S(1)} %get-tuple-element.203), channel_id=1, source_target_pairs={{0,1},{1,0},{2,3},{3,2},{4,5},{5,4},{6,7},{7,6},{8,9},{9,8},{10,11... | collective-permute-start | bytes 1769480 | tf_op jit(solution)/shard_map/ppermute | solution.py:1144
  123.1 22.3 %collective-permute-start.13 = (f32[240,512]{1,0:T(8,128)S(1)}, f32[240,512]{1,0:T(8,128)S(1)}, u32[]{:S(2)}, u32[]{:S(2)}) collective-permute-start(f32[240,512]{1,0:T(8,128)S(1)} %get-tuple-element.209), channel_id=1, source_target_pairs={{0,2},{1,3},{2,0},{3,1},{4,6},{5,7},{6,4},{7,5},{8,10},{9,11},{10,... | collective-permute-start | bytes 1474568 | tf_op jit(solution)/shard_map/ppermute | solution.py:1144
  132.2 22.0 %collective-permute-start.16 = (f32[192,1024]{1,0:T(8,128)S(1)}, f32[192,1024]{1,0:T(8,128)S(1)}, u32[]{:S(2)}, u32[]{:S(2)}) collective-permute-start(f32[192,1024]{1,0:T(8,128)S(1)} %get-tuple-element.216), channel_id=1, source_target_pairs={{0,2},{1,3},{2,0},{3,1},{4,6},{5,7},{6,4},{7,5},{8,10},{9,11},{10,... | collective-permute-start | bytes 2359304 | tf_op jit(solution)/shard_map/ppermute | solution.py:1144
  133.8 20.4 %collective-permute-start.15 = (f32[200,1024]{1,0:T(8,128)S(1)}, f32[200,1024]{1,0:T(8,128)S(1)}, u32[]{:S(2)}, u32[]{:S(2)}) collective-permute-start(f32[200,1024]{1,0:T(8,128)S(1)} %get-tuple-element.214), channel_id=1, source_target_pairs={{0,16},{1,17},{2,18},{3,19},{4,20},{5,21},{6,22},{7,23},{8,24},{9,... | collective-permute-start | bytes 2457608 | tf_op jit(solution)/shard_map/ppermute | solution.py:1144
  137.1 22.9 %collective-permute-start.14 = (f32[240,1024]{1,0:T(8,128)S(1)}, f32[240,1024]{1,0:T(8,128)S(1)}, u32[]{:S(2)}, u32[]{:S(2)}) collective-permute-start(f32[240,1024]{1,0:T(8,128)S(1)} %get-tuple-element.212), channel_id=1, source_target_pairs={{0,1},{1,0},{2,3},{3,2},{4,5},{5,4},{6,7},{7,6},{8,9},{9,8},{10,11... | collective-permute-start | bytes 2949128 | tf_op jit(solution)/shard_map/ppermute | solution.py:1144
  146.0 20.8 %collective-permute-start.17 = (f32[144,512]{1,0:T(8,128)S(1)}, f32[144,512]{1,0:T(8,128)S(1)}, u32[]{:S(2)}, u32[]{:S(2)}) collective-permute-start(f32[144,512]{1,0:T(8,128)S(1)} %get-tuple-element.220), channel_id=1, source_target_pairs={{0,6},{1,7},{2,4},{3,5},{4,2},{5,3},{6,0},{7,1},{8,14},{9,15},{10,... | collective-permute-start | bytes 884744 | tf_op jit(solution)/shard_map/ppermute | solution.py:1144
  149.6 35.0 %collective-permute-start.21 = (f32[2,24,3072]{2,1,0:T(8,128)S(1)}, f32[2,24,3072]{2,1,0:T(8,128)S(1)}, u32[]{:S(2)}, u32[]{:S(2)}) collective-permute-start(f32[2,24,3072]{2,1,0:T(8,128)S(1)} %get-tuple-element.229), channel_id=1, source_target_pairs={{0,2},{1,3},{2,0},{3,1},{4,6},{5,7},{6,4},{7,5},{8,10},{9,11},{10,... | collective-permute-start | bytes 1769480 | tf_op jit(solution)/shard_map/ppermute | solution.py:1144
  160.8 21.6 %collective-permute-start.20 = (f32[96,1024]{1,0:T(8,128)S(1)}, f32[96,1024]{1,0:T(8,128)S(1)}, u32[]{:S(2)}, u32[]{:S(2)}) collective-permute-start(f32[96,1024]{1,0:T(8,128)S(1)} %get-tuple-element.227), channel_id=1, source_target_pairs={{0,6},{1,7},{2,4},{3,5},{4,2},{5,3},{6,0},{7,1},{8,14},{9,15},{10,... | collective-permute-start | bytes 1179656 | tf_op jit(solution)/shard_map/ppermute | solution.py:1144
  164.8 17.6 %collective-permute-start.19 = (f32[104,1024]{1,0:T(8,128)S(1)}, f32[104,1024]{1,0:T(8,128)S(1)}, u32[]{:S(2)}, u32[]{:S(2)}) collective-permute-start(f32[104,1024]{1,0:T(8,128)S(1)} %get-tuple-element.225), channel_id=1, source_target_pairs={{0,1},{1,0},{2,3},{3,2},{4,5},{5,4},{6,7},{7,6},{8,9},{9,8},{10,11... | collective-permute-start | bytes 1277960 | tf_op jit(solution)/shard_map/ppermute | solution.py:1144
  166.3 16.1 %collective-permute-start.18 = (f32[120,1024]{1,0:T(8,128)S(1)}, f32[120,1024]{1,0:T(8,128)S(1)}, u32[]{:S(2)}, u32[]{:S(2)}) collective-permute-start(f32[120,1024]{1,0:T(8,128)S(1)} %get-tuple-element.223), channel_id=1, source_target_pairs={{0,16},{1,17},{2,18},{3,19},{4,20},{5,21},{6,22},{7,23},{8,24},{9,... | collective-permute-start | bytes 1474568 | tf_op jit(solution)/shard_map/ppermute | solution.py:1144
  183.1 19.6 %collective-permute-start.22 = (f32[104,1024]{1,0:T(8,128)S(1)}, f32[104,1024]{1,0:T(8,128)S(1)}, u32[]{:S(2)}, u32[]{:S(2)}) collective-permute-start(f32[104,1024]{1,0:T(8,128)S(1)} %get-tuple-element.235), channel_id=1, source_target_pairs={{0,2},{1,3},{2,0},{3,1},{4,6},{5,7},{6,4},{7,5},{8,10},{9,11},{10,... | collective-permute-start | bytes 1277960 | tf_op jit(solution)/shard_map/ppermute | solution.py:1144
  183.2 5.9 %collective-permute-start.23 = (f32[48,1024]{1,0:T(8,128)S(1)}, f32[48,1024]{1,0:T(8,128)S(1)}, u32[]{:S(2)}, u32[]{:S(2)}) collective-permute-start(f32[48,1024]{1,0:T(8,128)S(1)} %get-tuple-element.237), channel_id=1, source_target_pairs={{0,1},{1,0},{2,3},{3,2},{4,5},{5,4},{6,7},{7,6},{8,9},{9,8},{10,11... | collective-permute-start | bytes 589832 | tf_op jit(solution)/shard_map/ppermute | solution.py:1144
  185.3 19.1 %collective-permute-start.26 = (f32[24,3072]{1,0:T(8,128)S(1)}, f32[24,3072]{1,0:T(8,128)S(1)}, u32[]{:S(2)}, u32[]{:S(2)}) collective-permute-start(f32[24,3072]{1,0:T(8,128)S(1)} %get-tuple-element.253), channel_id=1, source_target_pairs={{0,6},{1,7},{2,4},{3,5},{4,2},{5,3},{6,0},{7,1},{8,14},{9,15},{10,... | collective-permute-start | bytes 884744 | tf_op jit(solution)/shard_map/ppermute | solution.py:1144
  203.3 7.9 %collective-permute-start.24 = (f32[56,1024]{1,0:T(8,128)S(1)}, f32[56,1024]{1,0:T(8,128)S(1)}, u32[]{:S(2)}, u32[]{:S(2)}) collective-permute-start(f32[56,1024]{1,0:T(8,128)S(1)} %get-tuple-element.239), channel_id=1, source_target_pairs={{0,6},{1,7},{2,4},{3,5},{4,2},{5,3},{6,0},{7,1},{8,14},{9,15},{10,... | collective-permute-start | bytes 688136 | tf_op jit(solution)/shard_map/ppermute | solution.py:1144
  203.4 4.7 %collective-permute-start.25 = (f32[24,1024]{1,0:T(8,128)S(1)}, f32[24,1024]{1,0:T(8,128)S(1)}, u32[]{:S(2)}, u32[]{:S(2)}) collective-permute-start(f32[24,1024]{1,0:T(8,128)S(1)} %get-tuple-element.241), channel_id=1, source_target_pairs={{0,16},{1,17},{2,18},{3,19},{4,20},{5,21},{6,22},{7,23},{8,24},{9,... | collective-permute-start | bytes 294920 | tf_op jit(solution)/shard_map/ppermute | solution.py:1144
  (17 other events, 142.4 us)

commit v2 on v1

--- a/solution.py
+++ b/solution.py
@@ -42,9 +42,9 @@
 
 COSTS = {
     "attention_back_0": 1,
-    "attention_back_1": 10000,
-    "attention_back_2": 10000,
-    "first_norm_back": 1,
+    "attention_back_1": 1000,
+    "attention_back_2": 1,
+    "first_norm_back": 300,
     "fourth_qkv_stage": 100,
     "fourth_stage_inner": 1,
     "fourth_stage_outer": 1000,
@@ -59,10 +59,10 @@
     "qkv_weight_keep": 100,
     "qkv_weight_send": 3000,
     "second_qkv_stage": 100,
-    "second_stage_inner": 10000,
+    "second_stage_inner": 1,
     "second_stage_outer": 3000,
     "sum": 10000,
-    "third_outer_stage": 10000,
+    "third_outer_stage": 65000,
     "third_qkv_stage": 3000,
     "third_stage": 10000,
     "token_grad": 3000,
@@ -78,10 +78,10 @@
     "back_0",
     "second_outer",
     "back_1",
+    "back_2",
+    "send_qkv",
     "second_inner",
-    "back_2",
     "third_outer",
-    "send_qkv",
     "keep_qkv",
     "third_inner",
     "tokens",

time: 217 us -> 208 us (0.959)
  waiting for transfers between devices: 63.9 us -> 54.3 us
    ppermute x27, waiting for transfers between devices: 63.9 us -> 54.3 us  [swap(): return lax.ppermute(array, ALL_AXES, PAIRS[name])]
  transfers between devices with their start and end apart: 27 -> 27, of which waited for: 14 -> 9; matrix products, arithmetic and copies ran while one was open for 0% -> 0% of each run, Pallas kernels for 30% -> 33%
where the time goes in v2:
time: 208 us; the launch traced here: 205 us
  Pallas kernels  109 us (52%)
  waiting for transfers between devices  54.3 us (26%)
  starting transfers between devices  35.9 us (17%)
  local copies, waits for them, and re-layouts  2.78 us (1%)
  between operations  2.77 us (1%)
    pallas_call x28, Pallas kernels, call(): pl.pallas_call(kernel, in_specs=[specs[p] for _, p in inputs], out_specs=...  109 us
    ppermute x27, waiting for transfers between devices, swap(): return lax.ppermute(array, ALL_AXES, PAIRS[name])  54.3 us
    ppermute x27, starting transfers between devices, swap(): return lax.ppermute(array, ALL_AXES, PAIRS[name])  35.9 us
  transfers between devices with their start and end apart: 27, of which 9 were waited for; matrix products, arithmetic and copies ran while one was open for 0% of the time, Pallas kernels for 33%

profile of v2, /device:TPU:0, one launch (start us, length us, event | category | flops | bytes accessed | tf_op | source)
XLA Modules:
  0.0 204.8 jit_solution(1570630981714384759)
XLA Ops:
  2.8 18.3 %attention_forward.1 = (bf16[1024,768]{1,0:T(8,128)(2,1)S(1)}, bf16[1024,768]{1,0:T(8,128)(2,1)}, bf16[1024,768]{1,0:T(8,128)(2,1)}, bf16[1024,768]{1,0:T(8,128)...) custom-call(s32[2]{0:T(128)S(1)} %copy-done.11, ...), custom_call_target="tpu_custom_call" | custom-call | flops 1000000 | bytes 1024 | tf_op jit(solution)/shard_map/attention_forward/pallas_call | solution.py:106
  21.2 18.9 %middle_forward.1 = (bf16[1024,768]{1,0:T(8,128)(2,1)}, bf16[1024,768]{1,0:T(8,128)(2,1)S(1)}, f32[1024,128]{1,0:T(8,128)S(1)}, bf16[768,1024]{1,0:T(8,128)(2,1)...) custom-call(s32[1]{0:T(128)S(6)} %copy.44.task_ref, ...), custom_call_target="tpu_custom_call" | custom-call | flops 1000000 | bytes 1024 | tf_op jit(solution)/shard_map/middle_forward/pallas_call | solution.py:106
  40.1 3.2 %outer_weight_send.1 = (f32[1568,768]{1,0:T(8,128)S(1)}, f32[32,768]{1,0:T(8,128)S(1)}) custom-call(s32[7]{0:T(128)S(1)} %stack.31.pos_ref, s32[1]{0:T(128)S(6)} %copy.44.task_ref, f32[8,768]{1,0:T(8,128)S(1)} %get-tuple-element.147.after_ref.sums2, bf16[1024,3072]{1,0:T(8,128)(2,1)S(1)} %get-tuple-element.148.act_ref, ...), custom_call_target="tpu_custom_call" | custom-call | flops 3000000000 | bytes 1024 | tf_op jit(solution)/shard_map/outer_weight_send/pallas_call | solution.py:106
  43.8 6.8 %inner_grad.1 = (bf16[1024,3072]{1,0:T(8,128)(2,1)S(1)}, f32[4,768]{1,0:T(4,128)S(1)}) custom-call(f32[32,768]{1,0:T(8,128)S(1)} %get-tuple-element.150.after_ref.table_ref, bf16[1024,768]{1,0:T(8,128)(2,1)S(1)} %get-tuple-element.149.ddown_ref, bf16[3072,768]{1,0:T(8,128)(2,1)S(1)} %get-tuple-element.145.wd_ref, ...), custom_call_target="tpu_custom_call", output_to_operand_aliasing={{0}: (3, {})} | custom-call | flops 3000000000 | bytes 1024 | tf_op jit(solution)/shard_map/inner_grad/pallas_call | solution.py:106
  50.6 3.2 %inner_weight_send.1.after_ref = f32[2,384,1536]{2,1,0:T(8,128)S(1)} custom-call(s32[7]{0:T(128)S(1)} %stack.31.pos_ref, f32[4,768]{1,0:T(4,128)S(1)} %get-tuple-element.152.after_ref.refs_13_, bf16[768,1024]{1,0:T(8,128)(2,1)S(1)} %get-tuple-element.153.left_ref, bf16[1024,3072]{1,0:T(8,128)(2,1)S(1)} %get-tuple-element.154.right_ref.dinner_ref), custom_call_target="tpu_custom_call" | custom-call | flops 10000000000 | bytes 1024 | tf_op jit(solution)/shard_map/inner_weight_send/pallas_call | solution.py:106
  53.9 3.2 %outer_weight_rest.1.after_ref.own_ref = f32[2,768,768]{2,1,0:T(8,128)S(1)} custom-call(s32[7]{0:T(128)S(1)} %stack.31.pos_ref, f32[2,384,1536]{2,1,0:T(8,128)S(1)} %inner_weight_send.1.after_ref, bf16[1024,3072]{1,0:T(8,128)(2,1)S(1)} %get-tuple-element.148.act_ref, bf16[1024,768]{1,0:T(8,128)(2,1)S(1)} %get-tuple-element.149.ddown_ref), custom_call_target="tpu_custom_call" | custom-call | flops 1000000 | bytes 1024 | tf_op jit(solution)/shard_map/outer_weight_rest/pallas_call | solution.py:106
  58.3 3.0 %collective-permute-start.2 = (f32[9,96,256]{2,1,0:T(8,128)S(1)}, f32[9,96,256]{2,1,0:T(8,128)S(1)}, u32[]{:S(2)}, u32[]{:S(2)}) collective-permute-start(f32[9,96,256]{2,1,0:T(8,128)S(1)} %get-tuple-element.168), channel_id=1, source_target_pairs={{0,1},{1,0},{2,3},{3,2},{4,5},{5,4},{6,7},{7,6},{8,9},{9,8},{10,11... | collective-permute-start | bytes 2654216 | tf_op jit(solution)/shard_map/ppermute | solution.py:1144
  61.3 1.5 collective-permute-start.3
  62.8 1.6 collective-permute-start.4
  64.4 3.2 %inner_weight_keep.1 = (f32[2,4,24,1536]{3,2,1,0:T(8,128)S(1)}, f32[2,4,24,1536]{3,2,1,0:T(8,128)S(1)}, f32[4,2,24,1536]{3,2,1,0:T(8,128)S(1)}, f32[4,2,24,1536]{3,2,1,0:T(8,128)S(1)}) custom-call(s32[7]{0:T(128)S(1)} %stack.31.pos_ref, f32[96,256]{1,0:T(8,128)S(1)} %get-tuple-element.156.after_ref.block, bf16[768,1024]{1,0:T(8,128)(2,1)S(1)} %get-tuple-element.153.left_ref, ...), custom_call_target="tpu_custom_call" | custom-call | flops 1000000000 | bytes 1024 | tf_op jit(solution)/shard_map/inner_weight_keep/pallas_call | solution.py:106
  69.3 10.5 %first_norm_back.1 = (f32[1024,768]{1,0:T(8,128)S(1)}, bf16[1024,768]{1,0:T(8,128)(2,1)S(1)}, bf16[1024,768]{1,0:T(8,128)(2,1)S(1)}, bf16[768,1024]{1,0:T(8,128)(2,1)S(1)}, f32[8,768]{1,0:T(8,128)S(1)}) custom-call(f32[2,4,24,1536]{3,2,1,0:T(8,128)S(1)} %get-tuple-element.157.after_ref.kx, bf16[1024,3072]{1,0:T(8,128)(2,1)S(1)} %get-tuple-element.154.right_ref.dinner_ref, ...), custom_call_target="tpu_custom_call" | custom-call | flops 300000000 | bytes 1024 | tf_op jit(solution)/shard_map/first_norm_back/pallas_call | solution.py:106
  79.9 6.6 %attention_back_0.1 = (bf16[1024,256]{1,0:T(8,128)(2,1)S(1)}, bf16[1024,256]{1,0:T(8,128)(2,1)S(1)}, bf16[1024,256]{1,0:T(8,128)(2,1)S(1)}, f32[8,256]{1,0:T(8,128)S(1)}) custom-call(s32[2]{0:T(128)S(1)} %copy-done.12, f32[8,768]{1,0:T(8,128)S(1)} %get-tuple-element.160.after_ref.refs_12_, bf16[1024,768]{1,0:T(8,128)(2,1)S(1)} %copy-done, ...), custom_call_target="tpu_custom_call" | custom-call | flops 1000000 | bytes 1024 | tf_op jit(solution)/shard_map/attention_back_0/pallas_call | solution.py:106
  89.9 2.5 %collective-permute-start.9 = (f32[2,2,96,256]{3,2,1,0:T(8,128)S(1)}, f32[2,2,96,256]{3,2,1,0:T(8,128)S(1)}, u32[]{:S(2)}, u32[]{:S(2)}) collective-permute-start(f32[2,2,96,256]{3,2,1,0:T(8,128)S(1)} %get-tuple-element.197), channel_id=1, source_target_pairs={{0,6},{1,7},{2,4},{3,5},{4,2},{5,3},{6,0},{7,1},{8,14},{9,15},{10,... | collective-permute-start | bytes 1179656 | tf_op jit(solution)/shard_map/ppermute | solution.py:1144
  92.4 6.4 %attention_back_1.1 = (bf16[1024,256]{1,0:T(8,128)(2,1)S(1)}, bf16[1024,256]{1,0:T(8,128)(2,1)S(1)}, bf16[1024,256]{1,0:T(8,128)(2,1)S(1)}, f32[8,256]{1,0:T(8,128)S(1)}) custom-call(s32[2]{0:T(128)S(1)} %copy-done.12, f32[96,256]{1,0:T(8,128)S(1)} %get-tuple-element.173.after_ref.block, bf16[1024,768]{1,0:T(8,128)(2,1)S(1)} %copy-done, ...), custom_call_target="tpu_custom_call" | custom-call | flops 1000000000 | bytes 1024 | tf_op jit(solution)/shard_map/attention_back_1/pallas_call | solution.py:106
  98.7 6.6 %attention_back_2.1 = (bf16[1024,256]{1,0:T(8,128)(2,1)S(1)}, bf16[1024,256]{1,0:T(8,128)(2,1)S(1)}, bf16[1024,256]{1,0:T(8,128)(2,1)S(1)}, f32[8,256]{1,0:T(8,128)S(1)}) custom-call(s32[2]{0:T(128)S(1)} %copy-done.12, f32[8,256]{1,0:T(8,128)S(1)} %get-tuple-element.174.after_ref.refs_10_, bf16[1024,768]{1,0:T(8,128)(2,1)S(1)} %copy-done, ...), custom_call_target="tpu_custom_call" | custom-call | flops 1000000 | bytes 1024 | tf_op jit(solution)/shard_map/attention_back_2/pallas_call | solution.py:106
  105.4 3.2 %qkv_weight_send.1.after_ref.own_ref = f32[1160,1024]{1,0:T(8,128)S(1)} custom-call(s32[7]{0:T(128)S(1)} %stack.31.pos_ref, f32[8,256]{1,0:T(8,128)S(1)} %get-tuple-element.175.after_ref.refs_11_, bf16[768,1024]{1,0:T(8,128)(2,1)S(1)} %get-tuple-element.176.left_ref, bf16[768,1024]{1,0:T(8,128)(2,1)S(1)} %copy-done.4, ...), custom_call_target="tpu_custom_call" | custom-call | flops 3000000000 | bytes 1024 | tf_op jit(solution)/shard_map/qkv_weight_send/pallas_call | solution.py:106
  110.7 4.1 %collective-permute-done.8.yr = f32[4,96,256]{2,1,0:T(8,128)S(1)} collective-permute-done((f32[4,96,256]{2,1,0:T(8,128)S(1)}, f32[4,96,256]{2,1,0:T(8,128)S(1)}, u32[]{:S(2)}, u32[]{:S(2)}) %collective-permute-start.8) | collective-permute-done | bytes 393248 | tf_op jit(solution)/shard_map/ppermute | solution.py:1144
  114.8 1.7 collective-permute-start.12
  118.2 1.6 collective-permute-start.13
  119.9 3.3 %qkv_weight_keep.1 = (f32[240,1024]{1,0:T(8,128)S(1)}, f32[192,1024]{1,0:T(8,128)S(1)}, f32[200,1024]{1,0:T(8,128)S(1)}, f32[192,1024]{1,0:T(8,128)S(1)}, f32[19...) custom-call(s32[7]{0:T(128)S(1)} %stack.31.pos_ref, ...), custom_call_target="tpu_custom_call" | custom-call | flops 100000000 | bytes 1024 | tf_op jit(solution)/shard_map/qkv_weight_keep/pallas_call | solution.py:106
  125.2 5.0 %collective-permute-done.11.xr = f32[4,24,1536]{2,1,0:T(8,128)S(1)} collective-permute-done((f32[4,24,1536]{2,1,0:T(8,128)S(1)}, f32[4,24,1536]{2,1,0:T(8,128)S(1)}, u32[]{:S(2)}, u32[]{:S(2)}) %collective-permute-start.11) | collective-permute-done | bytes 589856 | tf_op jit(solution)/shard_map/ppermute | solution.py:1144
  132.2 5.4 %token_grad.1 = (f32[1024,768]{1,0:T(8,128)}, f32[8,128]{1,0:T(8,128)S(1)}) custom-call(f32[2,24,3072]{2,1,0:T(8,128)S(1)} %get-tuple-element.204.after_ref.xyk, f32[1024,768]{1,0:T(8,128)S(1)} %get-tuple-element.205.dr1_ref, bf16[768,768]{1,0:T(8,128)(2,1)S(1)} %copy-done.6, bf16[768,768]{1,0:T(8,128)(2,1)S(1)} %copy-done.7, ...), custom_call_target="tpu_custom_call" | custom-call | flops 3000000000 | bytes 1024 | tf_op jit(solution)/shard_map/token_grad/pallas_call | solution.py:106
  138.2 4.2 %collective-permute-start.17 = (f32[144,512]{1,0:T(8,128)S(1)}, f32[144,512]{1,0:T(8,128)S(1)}, u32[]{:S(2)}, u32[]{:S(2)}) collective-permute-start(f32[144,512]{1,0:T(8,128)S(1)} %get-tuple-element.220), channel_id=1, source_target_pairs={{0,6},{1,7},{2,4},{3,5},{4,2},{5,3},{6,0},{7,1},{8,14},{9,15},{10,... | collective-permute-start | bytes 884744 | tf_op jit(solution)/shard_map/ppermute | solution.py:1144
  142.4 11.2 %collective-permute-done.16.rz = f32[192,1024]{1,0:T(8,128)S(1)} collective-permute-done((f32[192,1024]{1,0:T(8,128)S(1)}, f32[192,1024]{1,0:T(8,128)S(1)}, u32[]{:S(2)}, u32[]{:S(2)}) %collective-permute-start.16) | collective-permute-done | bytes 786464 | tf_op jit(solution)/shard_map/ppermute | solution.py:1144
  154.4 5.7 %collective-permute-start.20 = (f32[96,1024]{1,0:T(8,128)S(1)}, f32[96,1024]{1,0:T(8,128)S(1)}, u32[]{:S(2)}, u32[]{:S(2)}) collective-permute-start(f32[96,1024]{1,0:T(8,128)S(1)} %get-tuple-element.227), channel_id=1, source_target_pairs={{0,6},{1,7},{2,4},{3,5},{4,2},{5,3},{6,0},{7,1},{8,14},{9,15},{10,... | collective-permute-start | bytes 1179656 | tf_op jit(solution)/shard_map/ppermute | solution.py:1144
  160.7 1.5 collective-permute-start.18
  162.2 13.5 %collective-permute-done.20.zr = f32[96,1024]{1,0:T(8,128)S(1)} collective-permute-done((f32[96,1024]{1,0:T(8,128)S(1)}, f32[96,1024]{1,0:T(8,128)S(1)}, u32[]{:S(2)}, u32[]{:S(2)}) %collective-permute-start.20) | collective-permute-done | bytes 393248 | tf_op jit(solution)/shard_map/ppermute | solution.py:1144
  179.9 2.3 %collective-permute-done.23.zr = f32[48,1024]{1,0:T(8,128)S(1)} collective-permute-done((f32[48,1024]{1,0:T(8,128)S(1)}, f32[48,1024]{1,0:T(8,128)S(1)}, u32[]{:S(2)}, u32[]{:S(2)}) %collective-permute-start.23) | collective-permute-done | bytes 196640 | tf_op jit(solution)/shard_map/ppermute | solution.py:1144
  182.2 11.8 %collective-permute-done.22.got = f32[104,1024]{1,0:T(8,128)S(1)} collective-permute-done((f32[104,1024]{1,0:T(8,128)S(1)}, f32[104,1024]{1,0:T(8,128)S(1)}, u32[]{:S(2)}, u32[]{:S(2)}) %collective-permute-start.22) | collective-permute-done | bytes 426016 | tf_op jit(solution)/shard_map/ppermute | solution.py:1144
  194.7 1.6 collective-permute-start.25
  197.1 2.3 %collective-permute-done.25.zr = f32[24,1024]{1,0:T(8,128)S(1)} collective-permute-done((f32[24,1024]{1,0:T(8,128)S(1)}, f32[24,1024]{1,0:T(8,128)S(1)}, u32[]{:S(2)}, u32[]{:S(2)}) %collective-permute-start.25) | collective-permute-done | bytes 98336 | tf_op jit(solution)/shard_map/ppermute | solution.py:1144
  199.4 3.1 %collective-permute-done.24.got = f32[56,1024]{1,0:T(8,128)S(1)} collective-permute-done((f32[56,1024]{1,0:T(8,128)S(1)}, f32[56,1024]{1,0:T(8,128)S(1)}, u32[]{:S(2)}, u32[]{:S(2)}) %collective-permute-start.24) | collective-permute-done | bytes 229408 | tf_op jit(solution)/shard_map/ppermute | solution.py:1144
  (97 shorter events, 25.0 us)
Async XLA Ops:
  2.8 18.4 %copy-start.14 = (bf16[768]{0:T(1024)(128)(2,1)S(1)}, bf16[768]{0:T(1024)(128)(2,1)}, u32[]{:S(2)}) copy-start(bf16[768]{0:T(1024)(128)(2,1)} %bo_ref.1) | copy-start | bytes 4612
  2.8 18.4 %copy-start.15 = (bf16[768]{0:T(1024)(128)(2,1)S(1)}, bf16[768]{0:T(1024)(128)(2,1)}, u32[]{:S(2)}) copy-start(bf16[768]{0:T(1024)(128)(2,1)} %b1_ref.1) | copy-start | bytes 4612
  2.8 18.4 %copy-start.16 = (bf16[768]{0:T(1024)(128)(2,1)S(1)}, bf16[768]{0:T(1024)(128)(2,1)}, u32[]{:S(2)}) copy-start(bf16[768]{0:T(1024)(128)(2,1)} %bd_ref.1) | copy-start | bytes 4612
  2.8 18.4 %copy-start.17 = (bf16[768]{0:T(1024)(128)(2,1)S(1)}, bf16[768]{0:T(1024)(128)(2,1)}, u32[]{:S(2)}) copy-start(bf16[768]{0:T(1024)(128)(2,1)} %g2_ref.1) | copy-start | bytes 4612
  2.8 18.4 %copy-start.18 = (bf16[768]{0:T(1024)(128)(2,1)S(1)}, bf16[768]{0:T(1024)(128)(2,1)}, u32[]{:S(2)}) copy-start(bf16[768]{0:T(1024)(128)(2,1)} %b2_ref.1) | copy-start | bytes 4612
  43.3 13.8 %collective-permute-start = (f32[1568,768]{1,0:T(8,128)S(1)}, f32[1568,768]{1,0:T(8,128)S(1)}, u32[]{:S(2)}, u32[]{:S(2)}) collective-permute-start(f32[1568,768]{1,0:T(8,128)S(1)} %get-tuple-element.155), channel_id=1, source_target_pairs={{0,8},{1,9},{2,10},{3,11},{4,12},{5,13},{6,14},{7,15},{8,0},{9,1},... | collective-permute-start | bytes 14450696 | tf_op jit(solution)/shard_map/ppermute | solution.py:1144
  53.8 10.6 %collective-permute-start.1 = (f32[2,384,1536]{2,1,0:T(8,128)S(1)}, f32[2,384,1536]{2,1,0:T(8,128)S(1)}, u32[]{:S(2)}, u32[]{:S(2)}) collective-permute-start(f32[2,384,1536]{2,1,0:T(8,128)S(1)} %inner_weight_send.1.after_ref), channel_id=1, source_target_pairs={{0,8},{1,9},{2,10},{3,11},{4,12},{5,13},{6,14},{7,15},{8,0},{9,1},... | collective-permute-start | bytes 14155784 | tf_op jit(solution)/shard_map/ppermute | solution.py:1144
  58.3 28.2 %collective-permute-start.2 = (f32[9,96,256]{2,1,0:T(8,128)S(1)}, f32[9,96,256]{2,1,0:T(8,128)S(1)}, u32[]{:S(2)}, u32[]{:S(2)}) collective-permute-start(f32[9,96,256]{2,1,0:T(8,128)S(1)} %get-tuple-element.168), channel_id=1, source_target_pairs={{0,1},{1,0},{2,3},{3,2},{4,5},{5,4},{6,7},{7,6},{8,9},{9,8},{10,11... | collective-permute-start | bytes 2654216 | tf_op jit(solution)/shard_map/ppermute | solution.py:1144
  61.3 25.2 %collective-permute-start.3 = (f32[4,2,96,256]{3,2,1,0:T(8,128)S(1)}, f32[4,2,96,256]{3,2,1,0:T(8,128)S(1)}, u32[]{:S(2)}, u32[]{:S(2)}) collective-permute-start(f32[4,2,96,256]{3,2,1,0:T(8,128)S(1)} %get-tuple-element.170), channel_id=1, source_target_pairs={{0,16},{1,17},{2,18},{3,19},{4,20},{5,21},{6,22},{7,23},{8,24},{9,... | collective-permute-start | bytes 2359304 | tf_op jit(solution)/shard_map/ppermute | solution.py:1144
  62.8 23.7 %collective-permute-start.4 = (f32[2,2,2,96,256]{4,3,2,1,0:T(8,128)S(1)}, f32[2,2,2,96,256]{4,3,2,1,0:T(8,128)S(1)}, u32[]{:S(2)}, u32[]{:S(2)}) collective-permute-start(f32[2,2,2,96,256]{4,3,2,1,0:T(8,128)S(1)} %get-tuple-element.172), channel_id=1, source_target_pairs={{0,2},{1,3},{2,0},{3,1},{4,6},{5,7},{6,4},{7,5},{8,10},{9,11},{10,... | collective-permute-start | bytes 2359304 | tf_op jit(solution)/shard_map/ppermute | solution.py:1144
  67.6 40.9 %collective-permute-start.5 = (f32[2,4,24,1536]{3,2,1,0:T(8,128)S(1)}, f32[2,4,24,1536]{3,2,1,0:T(8,128)S(1)}, u32[]{:S(2)}, u32[]{:S(2)}) collective-permute-start(f32[2,4,24,1536]{3,2,1,0:T(8,128)S(1)} %get-tuple-element.188), channel_id=1, source_target_pairs={{0,1},{1,0},{2,3},{3,2},{4,5},{5,4},{6,7},{7,6},{8,9},{9,8},{10,11... | collective-permute-start | bytes 3538952 | tf_op jit(solution)/shard_map/ppermute | solution.py:1144
  68.2 40.4 %collective-permute-start.6 = (f32[4,2,24,1536]{3,2,1,0:T(8,128)S(1)}, f32[4,2,24,1536]{3,2,1,0:T(8,128)S(1)}, u32[]{:S(2)}, u32[]{:S(2)}) collective-permute-start(f32[4,2,24,1536]{3,2,1,0:T(8,128)S(1)} %get-tuple-element.190), channel_id=1, source_target_pairs={{0,16},{1,17},{2,18},{3,19},{4,20},{5,21},{6,22},{7,23},{8,24},{9,... | collective-permute-start | bytes 3538952 | tf_op jit(solution)/shard_map/ppermute | solution.py:1144
  87.3 30.2 %collective-permute-start.7 = (f32[5,96,256]{2,1,0:T(8,128)S(1)}, f32[5,96,256]{2,1,0:T(8,128)S(1)}, u32[]{:S(2)}, u32[]{:S(2)}) collective-permute-start(f32[5,96,256]{2,1,0:T(8,128)S(1)} %get-tuple-element.193), channel_id=1, source_target_pairs={{0,16},{1,17},{2,18},{3,19},{4,20},{5,21},{6,22},{7,23},{8,24},{9,... | collective-permute-start | bytes 1474568 | tf_op jit(solution)/shard_map/ppermute | solution.py:1144
  88.4 26.5 %collective-permute-start.8 = (f32[4,96,256]{2,1,0:T(8,128)S(1)}, f32[4,96,256]{2,1,0:T(8,128)S(1)}, u32[]{:S(2)}, u32[]{:S(2)}) collective-permute-start(f32[4,96,256]{2,1,0:T(8,128)S(1)} %get-tuple-element.195), channel_id=1, source_target_pairs={{0,1},{1,0},{2,3},{3,2},{4,5},{5,4},{6,7},{7,6},{8,9},{9,8},{10,11... | collective-permute-start | bytes 1179656 | tf_op jit(solution)/shard_map/ppermute | solution.py:1144
  89.9 26.7 %collective-permute-start.9 = (f32[2,2,96,256]{3,2,1,0:T(8,128)S(1)}, f32[2,2,96,256]{3,2,1,0:T(8,128)S(1)}, u32[]{:S(2)}, u32[]{:S(2)}) collective-permute-start(f32[2,2,96,256]{3,2,1,0:T(8,128)S(1)} %get-tuple-element.197), channel_id=1, source_target_pairs={{0,6},{1,7},{2,4},{3,5},{4,2},{5,3},{6,0},{7,1},{8,14},{9,15},{10,... | collective-permute-start | bytes 1179656 | tf_op jit(solution)/shard_map/ppermute | solution.py:1144
  108.6 11.3 %collective-permute-start.10 = (f32[1160,1024]{1,0:T(8,128)S(1)}, f32[1160,1024]{1,0:T(8,128)S(1)}, u32[]{:S(2)}, u32[]{:S(2)}) collective-permute-start(f32[1160,1024]{1,0:T(8,128)S(1)} %qkv_weight_send.1.after_ref.own_ref), channel_id=1, source_target_pairs={{0,8},{1,9},{2,10},{3,11},{4,12},{5,13},{6,14},{7,15},{8,0},{9,1},... | collective-permute-start | bytes 14254088 | tf_op jit(solution)/shard_map/ppermute | solution.py:1144
  109.5 20.7 %collective-permute-start.11 = (f32[4,24,1536]{2,1,0:T(8,128)S(1)}, f32[4,24,1536]{2,1,0:T(8,128)S(1)}, u32[]{:S(2)}, u32[]{:S(2)}) collective-permute-start(f32[4,24,1536]{2,1,0:T(8,128)S(1)} %get-tuple-element.201), channel_id=1, source_target_pairs={{0,16},{1,17},{2,18},{3,19},{4,20},{5,21},{6,22},{7,23},{8,24},{9,... | collective-permute-start | bytes 1769480 | tf_op jit(solution)/shard_map/ppermute | solution.py:1144
  114.8 15.4 %collective-permute-start.12 = (f32[4,24,1536]{2,1,0:T(8,128)S(1)}, f32[4,24,1536]{2,1,0:T(8,128)S(1)}, u32[]{:S(2)}, u32[]{:S(2)}) collective-permute-start(f32[4,24,1536]{2,1,0:T(8,128)S(1)} %get-tuple-element.203), channel_id=1, source_target_pairs={{0,1},{1,0},{2,3},{3,2},{4,5},{5,4},{6,7},{7,6},{8,9},{9,8},{10,11... | collective-permute-start | bytes 1769480 | tf_op jit(solution)/shard_map/ppermute | solution.py:1144
  118.2 19.4 %collective-permute-start.13 = (f32[240,512]{1,0:T(8,128)S(1)}, f32[240,512]{1,0:T(8,128)S(1)}, u32[]{:S(2)}, u32[]{:S(2)}) collective-permute-start(f32[240,512]{1,0:T(8,128)S(1)} %get-tuple-element.209), channel_id=1, source_target_pairs={{0,2},{1,3},{2,0},{3,1},{4,6},{5,7},{6,4},{7,5},{8,10},{9,11},{10,... | collective-permute-start | bytes 1474568 | tf_op jit(solution)/shard_map/ppermute | solution.py:1144
  123.2 30.5 %collective-permute-start.16 = (f32[192,1024]{1,0:T(8,128)S(1)}, f32[192,1024]{1,0:T(8,128)S(1)}, u32[]{:S(2)}, u32[]{:S(2)}) collective-permute-start(f32[192,1024]{1,0:T(8,128)S(1)} %get-tuple-element.216), channel_id=1, source_target_pairs={{0,2},{1,3},{2,0},{3,1},{4,6},{5,7},{6,4},{7,5},{8,10},{9,11},{10,... | collective-permute-start | bytes 2359304 | tf_op jit(solution)/shard_map/ppermute | solution.py:1144
  123.7 29.9 %collective-permute-start.15 = (f32[200,1024]{1,0:T(8,128)S(1)}, f32[200,1024]{1,0:T(8,128)S(1)}, u32[]{:S(2)}, u32[]{:S(2)}) collective-permute-start(f32[200,1024]{1,0:T(8,128)S(1)} %get-tuple-element.214), channel_id=1, source_target_pairs={{0,16},{1,17},{2,18},{3,19},{4,20},{5,21},{6,22},{7,23},{8,24},{9,... | collective-permute-start | bytes 2457608 | tf_op jit(solution)/shard_map/ppermute | solution.py:1144
  130.2 23.5 %collective-permute-start.14 = (f32[240,1024]{1,0:T(8,128)S(1)}, f32[240,1024]{1,0:T(8,128)S(1)}, u32[]{:S(2)}, u32[]{:S(2)}) collective-permute-start(f32[240,1024]{1,0:T(8,128)S(1)} %get-tuple-element.212), channel_id=1, source_target_pairs={{0,1},{1,0},{2,3},{3,2},{4,5},{5,4},{6,7},{7,6},{8,9},{9,8},{10,11... | collective-permute-start | bytes 2949128 | tf_op jit(solution)/shard_map/ppermute | solution.py:1144
  138.2 24.0 %collective-permute-start.17 = (f32[144,512]{1,0:T(8,128)S(1)}, f32[144,512]{1,0:T(8,128)S(1)}, u32[]{:S(2)}, u32[]{:S(2)}) collective-permute-start(f32[144,512]{1,0:T(8,128)S(1)} %get-tuple-element.220), channel_id=1, source_target_pairs={{0,6},{1,7},{2,4},{3,5},{4,2},{5,3},{6,0},{7,1},{8,14},{9,15},{10,... | collective-permute-start | bytes 884744 | tf_op jit(solution)/shard_map/ppermute | solution.py:1144
  142.4 34.7 %collective-permute-start.21 = (f32[2,24,3072]{2,1,0:T(8,128)S(1)}, f32[2,24,3072]{2,1,0:T(8,128)S(1)}, u32[]{:S(2)}, u32[]{:S(2)}) collective-permute-start(f32[2,24,3072]{2,1,0:T(8,128)S(1)} %get-tuple-element.229), channel_id=1, source_target_pairs={{0,2},{1,3},{2,0},{3,1},{4,6},{5,7},{6,4},{7,5},{8,10},{9,11},{10,... | collective-permute-start | bytes 1769480 | tf_op jit(solution)/shard_map/ppermute | solution.py:1144
  154.4 21.3 %collective-permute-start.20 = (f32[96,1024]{1,0:T(8,128)S(1)}, f32[96,1024]{1,0:T(8,128)S(1)}, u32[]{:S(2)}, u32[]{:S(2)}) collective-permute-start(f32[96,1024]{1,0:T(8,128)S(1)} %get-tuple-element.227), channel_id=1, source_target_pairs={{0,6},{1,7},{2,4},{3,5},{4,2},{5,3},{6,0},{7,1},{8,14},{9,15},{10,... | collective-permute-start | bytes 1179656 | tf_op jit(solution)/shard_map/ppermute | solution.py:1144
  160.1 15.6 %collective-permute-start.19 = (f32[104,1024]{1,0:T(8,128)S(1)}, f32[104,1024]{1,0:T(8,128)S(1)}, u32[]{:S(2)}, u32[]{:S(2)}) collective-permute-start(f32[104,1024]{1,0:T(8,128)S(1)} %get-tuple-element.225), channel_id=1, source_target_pairs={{0,1},{1,0},{2,3},{3,2},{4,5},{5,4},{6,7},{7,6},{8,9},{9,8},{10,11... | collective-permute-start | bytes 1277960 | tf_op jit(solution)/shard_map/ppermute | solution.py:1144
  160.7 15.0 %collective-permute-start.18 = (f32[120,1024]{1,0:T(8,128)S(1)}, f32[120,1024]{1,0:T(8,128)S(1)}, u32[]{:S(2)}, u32[]{:S(2)}) collective-permute-start(f32[120,1024]{1,0:T(8,128)S(1)} %get-tuple-element.223), channel_id=1, source_target_pairs={{0,16},{1,17},{2,18},{3,19},{4,20},{5,21},{6,22},{7,23},{8,24},{9,... | collective-permute-start | bytes 1474568 | tf_op jit(solution)/shard_map/ppermute | solution.py:1144
  176.4 17.6 %collective-permute-start.22 = (f32[104,1024]{1,0:T(8,128)S(1)}, f32[104,1024]{1,0:T(8,128)S(1)}, u32[]{:S(2)}, u32[]{:S(2)}) collective-permute-start(f32[104,1024]{1,0:T(8,128)S(1)} %get-tuple-element.235), channel_id=1, source_target_pairs={{0,2},{1,3},{2,0},{3,1},{4,6},{5,7},{6,4},{7,5},{8,10},{9,11},{10,... | collective-permute-start | bytes 1277960 | tf_op jit(solution)/shard_map/ppermute | solution.py:1144
  176.5 5.7 %collective-permute-start.23 = (f32[48,1024]{1,0:T(8,128)S(1)}, f32[48,1024]{1,0:T(8,128)S(1)}, u32[]{:S(2)}, u32[]{:S(2)}) collective-permute-start(f32[48,1024]{1,0:T(8,128)S(1)} %get-tuple-element.237), channel_id=1, source_target_pairs={{0,1},{1,0},{2,3},{3,2},{4,5},{5,4},{6,7},{7,6},{8,9},{9,8},{10,11... | collective-permute-start | bytes 589832 | tf_op jit(solution)/shard_map/ppermute | solution.py:1144
  177.7 18.6 %collective-permute-start.26 = (f32[24,3072]{1,0:T(8,128)S(1)}, f32[24,3072]{1,0:T(8,128)S(1)}, u32[]{:S(2)}, u32[]{:S(2)}) collective-permute-start(f32[24,3072]{1,0:T(8,128)S(1)} %get-tuple-element.253), channel_id=1, source_target_pairs={{0,6},{1,7},{2,4},{3,5},{4,2},{5,3},{6,0},{7,1},{8,14},{9,15},{10,... | collective-permute-start | bytes 884744 | tf_op jit(solution)/shard_map/ppermute | solution.py:1144
  194.6 7.9 %collective-permute-start.24 = (f32[56,1024]{1,0:T(8,128)S(1)}, f32[56,1024]{1,0:T(8,128)S(1)}, u32[]{:S(2)}, u32[]{:S(2)}) collective-permute-start(f32[56,1024]{1,0:T(8,128)S(1)} %get-tuple-element.239), channel_id=1, source_target_pairs={{0,6},{1,7},{2,4},{3,5},{4,2},{5,3},{6,0},{7,1},{8,14},{9,15},{10,... | collective-permute-start | bytes 688136 | tf_op jit(solution)/shard_map/ppermute | solution.py:1144
  194.7 4.7 %collective-permute-start.25 = (f32[24,1024]{1,0:T(8,128)S(1)}, f32[24,1024]{1,0:T(8,128)S(1)}, u32[]{:S(2)}, u32[]{:S(2)}) collective-permute-start(f32[24,1024]{1,0:T(8,128)S(1)} %get-tuple-element.241), channel_id=1, source_target_pairs={{0,16},{1,17},{2,18},{3,19},{4,20},{5,21},{6,22},{7,23},{8,24},{9,... | collective-permute-start | bytes 294920 | tf_op jit(solution)/shard_map/ppermute | solution.py:1144
  (17 other events, 147.7 us)

commit v3 on v2

--- a/solution.py
+++ b/solution.py
@@ -954,13 +954,15 @@
     inner_out[...] = pltpu.roll(one, lax.rem(width - (me % per_row) * part, width), 1)[0:1, :part]
     lane = lax.broadcasted_iota(jnp.int32, (1, width), 1)
     loss_out[...] = jnp.sum(jnp.where(lane == pos_ref[6], tables[3:4], 0.0), axis=1, keepdims=True)
-    for t in range(head_out.shape[0]):
-        head_out[t] = tables[4 + t * classes : 4 + (t + 1) * classes]
+    for t in range(head_out.shape[1]):
+        for c in range(classes):
+            row_at = 4 + t * classes + c
+            head_out[c, t : t + 1, :] = tables[row_at : row_at + 1]
 
 
 def last_qkv(pos, k, got, zk, zr, small, table, classes, tables, bias_rows):
     r, width = zk.shape[0], table.shape[1]
-    shapes = [(r, width)] * 4 + [(1, r)] * 8 + [(1, r * bias_rows), (1, 1), (tables, classes, width)]
+    shapes = [(r, width)] * 4 + [(1, r)] * 8 + [(1, r * bias_rows), (1, 1), (classes, tables, width)]
     return call(
         functools.partial(last_qkv_kernel, classes=classes, bias_rows=bias_rows),
         "last_qkv_stage",
@@ -1380,7 +1382,7 @@
         query_s, key_s, value_s, output_s, *rest = e["last"]
         inner_s, outer_s = e["inner_s"], e["outer_s"]
         vector_s = [v.reshape(-1) for v in rest[:-1]]
-        head_grad = rest[-1]
+        head_grad = rest[-1].transpose(1, 0, 2)
     else:
         after = do_first_norm(send_inner(do_inner_grad(send_outer(sums2))))
         after = rest_outer(after)

time: 208 us -> 207 us (level)
  no operation moved by 1% of the time
where the time goes in v3:
time: 207 us; the launch traced here: 204 us
  Pallas kernels  109 us (53%)
  waiting for transfers between devices  54.3 us (26%)
  starting transfers between devices  35.9 us (17%)
  between operations  2.76 us (1%)
  local copies, waits for them, and re-layouts  2.13 us (1%)
    pallas_call x28, Pallas kernels, call(): pl.pallas_call(kernel, in_specs=[specs[p] for _, p in inputs], out_specs=...  109 us
    ppermute x27, waiting for transfers between devices, swap(): return lax.ppermute(array, ALL_AXES, PAIRS[name])  54.3 us
    ppermute x27, starting transfers between devices, swap(): return lax.ppermute(array, ALL_AXES, PAIRS[name])  35.9 us
  transfers between devices with their start and end apart: 27, of which 9 were waited for; matrix products, arithmetic and copies ran while one was open for 0% of the time, Pallas kernels for 33%

profile of v3, /device:TPU:0, one launch (start us, length us, event | category | flops | bytes accessed | tf_op | source)
XLA Modules:
  0.0 204.1 jit_solution(731979106575480392)
XLA Ops:
  2.8 18.3 %attention_forward.1 = (bf16[1024,768]{1,0:T(8,128)(2,1)S(1)}, bf16[1024,768]{1,0:T(8,128)(2,1)}, bf16[1024,768]{1,0:T(8,128)(2,1)}, bf16[1024,768]{1,0:T(8,128)...) custom-call(s32[2]{0:T(128)S(1)} %copy-done.11, ...), custom_call_target="tpu_custom_call" | custom-call | flops 1000000 | bytes 1024 | tf_op jit(solution)/shard_map/attention_forward/pallas_call | solution.py:106
  21.2 18.9 %middle_forward.1 = (bf16[1024,768]{1,0:T(8,128)(2,1)}, bf16[1024,768]{1,0:T(8,128)(2,1)S(1)}, f32[1024,128]{1,0:T(8,128)S(1)}, bf16[768,1024]{1,0:T(8,128)(2,1)...) custom-call(s32[1]{0:T(128)S(6)} %copy.43.task_ref, ...), custom_call_target="tpu_custom_call" | custom-call | flops 1000000 | bytes 1024 | tf_op jit(solution)/shard_map/middle_forward/pallas_call | solution.py:106
  40.1 3.2 %outer_weight_send.1 = (f32[1568,768]{1,0:T(8,128)S(1)}, f32[32,768]{1,0:T(8,128)S(1)}) custom-call(s32[7]{0:T(128)S(1)} %stack.31.pos_ref, s32[1]{0:T(128)S(6)} %copy.43.task_ref, f32[8,768]{1,0:T(8,128)S(1)} %get-tuple-element.147.after_ref.sums2, bf16[1024,3072]{1,0:T(8,128)(2,1)S(1)} %get-tuple-element.148.act_ref, ...), custom_call_target="tpu_custom_call" | custom-call | flops 3000000000 | bytes 1024 | tf_op jit(solution)/shard_map/outer_weight_send/pallas_call | solution.py:106
  43.8 6.8 %inner_grad.1 = (bf16[1024,3072]{1,0:T(8,128)(2,1)S(1)}, f32[4,768]{1,0:T(4,128)S(1)}) custom-call(f32[32,768]{1,0:T(8,128)S(1)} %get-tuple-element.150.after_ref.table_ref, bf16[1024,768]{1,0:T(8,128)(2,1)S(1)} %get-tuple-element.149.ddown_ref, bf16[3072,768]{1,0:T(8,128)(2,1)S(1)} %get-tuple-element.145.wd_ref, ...), custom_call_target="tpu_custom_call", output_to_operand_aliasing={{0}: (3, {})} | custom-call | flops 3000000000 | bytes 1024 | tf_op jit(solution)/shard_map/inner_grad/pallas_call | solution.py:106
  50.6 3.2 %inner_weight_send.1.after_ref = f32[2,384,1536]{2,1,0:T(8,128)S(1)} custom-call(s32[7]{0:T(128)S(1)} %stack.31.pos_ref, f32[4,768]{1,0:T(4,128)S(1)} %get-tuple-element.152.after_ref.refs_13_, bf16[768,1024]{1,0:T(8,128)(2,1)S(1)} %get-tuple-element.153.left_ref, bf16[1024,3072]{1,0:T(8,128)(2,1)S(1)} %get-tuple-element.154.right_ref.dinner_ref), custom_call_target="tpu_custom_call" | custom-call | flops 10000000000 | bytes 1024 | tf_op jit(solution)/shard_map/inner_weight_send/pallas_call | solution.py:106
  53.9 3.2 %outer_weight_rest.1.after_ref.own_ref = f32[2,768,768]{2,1,0:T(8,128)S(1)} custom-call(s32[7]{0:T(128)S(1)} %stack.31.pos_ref, f32[2,384,1536]{2,1,0:T(8,128)S(1)} %inner_weight_send.1.after_ref, bf16[1024,3072]{1,0:T(8,128)(2,1)S(1)} %get-tuple-element.148.act_ref, bf16[1024,768]{1,0:T(8,128)(2,1)S(1)} %get-tuple-element.149.ddown_ref), custom_call_target="tpu_custom_call" | custom-call | flops 1000000 | bytes 1024 | tf_op jit(solution)/shard_map/outer_weight_rest/pallas_call | solution.py:106
  58.3 3.0 %collective-permute-start.2 = (f32[9,96,256]{2,1,0:T(8,128)S(1)}, f32[9,96,256]{2,1,0:T(8,128)S(1)}, u32[]{:S(2)}, u32[]{:S(2)}) collective-permute-start(f32[9,96,256]{2,1,0:T(8,128)S(1)} %get-tuple-element.168), channel_id=1, source_target_pairs={{0,1},{1,0},{2,3},{3,2},{4,5},{5,4},{6,7},{7,6},{8,9},{9,8},{10,11... | collective-permute-start | bytes 2654216 | tf_op jit(solution)/shard_map/ppermute | solution.py:1146
  61.3 1.5 collective-permute-start.3
  62.8 1.6 collective-permute-start.4
  64.4 3.2 %inner_weight_keep.1 = (f32[2,4,24,1536]{3,2,1,0:T(8,128)S(1)}, f32[2,4,24,1536]{3,2,1,0:T(8,128)S(1)}, f32[4,2,24,1536]{3,2,1,0:T(8,128)S(1)}, f32[4,2,24,1536]{3,2,1,0:T(8,128)S(1)}) custom-call(s32[7]{0:T(128)S(1)} %stack.31.pos_ref, f32[96,256]{1,0:T(8,128)S(1)} %get-tuple-element.156.after_ref.block, bf16[768,1024]{1,0:T(8,128)(2,1)S(1)} %get-tuple-element.153.left_ref, ...), custom_call_target="tpu_custom_call" | custom-call | flops 1000000000 | bytes 1024 | tf_op jit(solution)/shard_map/inner_weight_keep/pallas_call | solution.py:106
  69.3 10.5 %first_norm_back.1 = (f32[1024,768]{1,0:T(8,128)S(1)}, bf16[1024,768]{1,0:T(8,128)(2,1)S(1)}, bf16[1024,768]{1,0:T(8,128)(2,1)S(1)}, bf16[768,1024]{1,0:T(8,128)(2,1)S(1)}, f32[8,768]{1,0:T(8,128)S(1)}) custom-call(f32[2,4,24,1536]{3,2,1,0:T(8,128)S(1)} %get-tuple-element.157.after_ref.kx, bf16[1024,3072]{1,0:T(8,128)(2,1)S(1)} %get-tuple-element.154.right_ref.dinner_ref, ...), custom_call_target="tpu_custom_call" | custom-call | flops 300000000 | bytes 1024 | tf_op jit(solution)/shard_map/first_norm_back/pallas_call | solution.py:106
  79.9 6.6 %attention_back_0.1 = (bf16[1024,256]{1,0:T(8,128)(2,1)S(1)}, bf16[1024,256]{1,0:T(8,128)(2,1)S(1)}, bf16[1024,256]{1,0:T(8,128)(2,1)S(1)}, f32[8,256]{1,0:T(8,128)S(1)}) custom-call(s32[2]{0:T(128)S(1)} %copy-done.12, f32[8,768]{1,0:T(8,128)S(1)} %get-tuple-element.160.after_ref.refs_12_, bf16[1024,768]{1,0:T(8,128)(2,1)S(1)} %copy-done, ...), custom_call_target="tpu_custom_call" | custom-call | flops 1000000 | bytes 1024 | tf_op jit(solution)/shard_map/attention_back_0/pallas_call | solution.py:106
  89.9 2.5 %collective-permute-start.9 = (f32[2,2,96,256]{3,2,1,0:T(8,128)S(1)}, f32[2,2,96,256]{3,2,1,0:T(8,128)S(1)}, u32[]{:S(2)}, u32[]{:S(2)}) collective-permute-start(f32[2,2,96,256]{3,2,1,0:T(8,128)S(1)} %get-tuple-element.197), channel_id=1, source_target_pairs={{0,6},{1,7},{2,4},{3,5},{4,2},{5,3},{6,0},{7,1},{8,14},{9,15},{10,... | collective-permute-start | bytes 1179656 | tf_op jit(solution)/shard_map/ppermute | solution.py:1146
  92.4 6.4 %attention_back_1.1 = (bf16[1024,256]{1,0:T(8,128)(2,1)S(1)}, bf16[1024,256]{1,0:T(8,128)(2,1)S(1)}, bf16[1024,256]{1,0:T(8,128)(2,1)S(1)}, f32[8,256]{1,0:T(8,128)S(1)}) custom-call(s32[2]{0:T(128)S(1)} %copy-done.12, f32[96,256]{1,0:T(8,128)S(1)} %get-tuple-element.173.after_ref.block, bf16[1024,768]{1,0:T(8,128)(2,1)S(1)} %copy-done, ...), custom_call_target="tpu_custom_call" | custom-call | flops 1000000000 | bytes 1024 | tf_op jit(solution)/shard_map/attention_back_1/pallas_call | solution.py:106
  98.7 6.6 %attention_back_2.1 = (bf16[1024,256]{1,0:T(8,128)(2,1)S(1)}, bf16[1024,256]{1,0:T(8,128)(2,1)S(1)}, bf16[1024,256]{1,0:T(8,128)(2,1)S(1)}, f32[8,256]{1,0:T(8,128)S(1)}) custom-call(s32[2]{0:T(128)S(1)} %copy-done.12, f32[8,256]{1,0:T(8,128)S(1)} %get-tuple-element.174.after_ref.refs_10_, bf16[1024,768]{1,0:T(8,128)(2,1)S(1)} %copy-done, ...), custom_call_target="tpu_custom_call" | custom-call | flops 1000000 | bytes 1024 | tf_op jit(solution)/shard_map/attention_back_2/pallas_call | solution.py:106
  105.4 3.2 %qkv_weight_send.1.after_ref.own_ref = f32[1160,1024]{1,0:T(8,128)S(1)} custom-call(s32[7]{0:T(128)S(1)} %stack.31.pos_ref, f32[8,256]{1,0:T(8,128)S(1)} %get-tuple-element.175.after_ref.refs_11_, bf16[768,1024]{1,0:T(8,128)(2,1)S(1)} %get-tuple-element.176.left_ref, bf16[768,1024]{1,0:T(8,128)(2,1)S(1)} %copy-done.4, ...), custom_call_target="tpu_custom_call" | custom-call | flops 3000000000 | bytes 1024 | tf_op jit(solution)/shard_map/qkv_weight_send/pallas_call | solution.py:106
  110.7 4.1 %collective-permute-done.8.yr = f32[4,96,256]{2,1,0:T(8,128)S(1)} collective-permute-done((f32[4,96,256]{2,1,0:T(8,128)S(1)}, f32[4,96,256]{2,1,0:T(8,128)S(1)}, u32[]{:S(2)}, u32[]{:S(2)}) %collective-permute-start.8) | collective-permute-done | bytes 393248 | tf_op jit(solution)/shard_map/ppermute | solution.py:1146
  114.8 1.7 collective-permute-start.12
  118.2 1.6 collective-permute-start.13
  119.9 3.3 %qkv_weight_keep.1 = (f32[240,1024]{1,0:T(8,128)S(1)}, f32[192,1024]{1,0:T(8,128)S(1)}, f32[200,1024]{1,0:T(8,128)S(1)}, f32[192,1024]{1,0:T(8,128)S(1)}, f32[19...) custom-call(s32[7]{0:T(128)S(1)} %stack.31.pos_ref, ...), custom_call_target="tpu_custom_call" | custom-call | flops 100000000 | bytes 1024 | tf_op jit(solution)/shard_map/qkv_weight_keep/pallas_call | solution.py:106
  125.2 5.0 %collective-permute-done.11.xr = f32[4,24,1536]{2,1,0:T(8,128)S(1)} collective-permute-done((f32[4,24,1536]{2,1,0:T(8,128)S(1)}, f32[4,24,1536]{2,1,0:T(8,128)S(1)}, u32[]{:S(2)}, u32[]{:S(2)}) %collective-permute-start.11) | collective-permute-done | bytes 589856 | tf_op jit(solution)/shard_map/ppermute | solution.py:1146
  132.2 5.4 %token_grad.1 = (f32[1024,768]{1,0:T(8,128)}, f32[8,128]{1,0:T(8,128)S(1)}) custom-call(f32[2,24,3072]{2,1,0:T(8,128)S(1)} %get-tuple-element.204.after_ref.xyk, f32[1024,768]{1,0:T(8,128)S(1)} %get-tuple-element.205.dr1_ref, bf16[768,768]{1,0:T(8,128)(2,1)S(1)} %copy-done.6, bf16[768,768]{1,0:T(8,128)(2,1)S(1)} %copy-done.7, ...), custom_call_target="tpu_custom_call" | custom-call | flops 3000000000 | bytes 1024 | tf_op jit(solution)/shard_map/token_grad/pallas_call | solution.py:106
  138.2 4.2 %collective-permute-start.17 = (f32[144,512]{1,0:T(8,128)S(1)}, f32[144,512]{1,0:T(8,128)S(1)}, u32[]{:S(2)}, u32[]{:S(2)}) collective-permute-start(f32[144,512]{1,0:T(8,128)S(1)} %get-tuple-element.220), channel_id=1, source_target_pairs={{0,6},{1,7},{2,4},{3,5},{4,2},{5,3},{6,0},{7,1},{8,14},{9,15},{10,... | collective-permute-start | bytes 884744 | tf_op jit(solution)/shard_map/ppermute | solution.py:1146
  142.4 11.2 %collective-permute-done.16.rz = f32[192,1024]{1,0:T(8,128)S(1)} collective-permute-done((f32[192,1024]{1,0:T(8,128)S(1)}, f32[192,1024]{1,0:T(8,128)S(1)}, u32[]{:S(2)}, u32[]{:S(2)}) %collective-permute-start.16) | collective-permute-done | bytes 786464 | tf_op jit(solution)/shard_map/ppermute | solution.py:1146
  154.4 5.7 %collective-permute-start.20 = (f32[96,1024]{1,0:T(8,128)S(1)}, f32[96,1024]{1,0:T(8,128)S(1)}, u32[]{:S(2)}, u32[]{:S(2)}) collective-permute-start(f32[96,1024]{1,0:T(8,128)S(1)} %get-tuple-element.227), channel_id=1, source_target_pairs={{0,6},{1,7},{2,4},{3,5},{4,2},{5,3},{6,0},{7,1},{8,14},{9,15},{10,... | collective-permute-start | bytes 1179656 | tf_op jit(solution)/shard_map/ppermute | solution.py:1146
  160.7 1.5 collective-permute-start.18
  162.2 13.5 %collective-permute-done.20.zr = f32[96,1024]{1,0:T(8,128)S(1)} collective-permute-done((f32[96,1024]{1,0:T(8,128)S(1)}, f32[96,1024]{1,0:T(8,128)S(1)}, u32[]{:S(2)}, u32[]{:S(2)}) %collective-permute-start.20) | collective-permute-done | bytes 393248 | tf_op jit(solution)/shard_map/ppermute | solution.py:1146
  179.9 2.3 %collective-permute-done.23.zr = f32[48,1024]{1,0:T(8,128)S(1)} collective-permute-done((f32[48,1024]{1,0:T(8,128)S(1)}, f32[48,1024]{1,0:T(8,128)S(1)}, u32[]{:S(2)}, u32[]{:S(2)}) %collective-permute-start.23) | collective-permute-done | bytes 196640 | tf_op jit(solution)/shard_map/ppermute | solution.py:1146
  182.2 11.8 %collective-permute-done.22.got = f32[104,1024]{1,0:T(8,128)S(1)} collective-permute-done((f32[104,1024]{1,0:T(8,128)S(1)}, f32[104,1024]{1,0:T(8,128)S(1)}, u32[]{:S(2)}, u32[]{:S(2)}) %collective-permute-start.22) | collective-permute-done | bytes 426016 | tf_op jit(solution)/shard_map/ppermute | solution.py:1146
  194.7 1.6 collective-permute-start.25
  197.1 2.3 %collective-permute-done.25.zr = f32[24,1024]{1,0:T(8,128)S(1)} collective-permute-done((f32[24,1024]{1,0:T(8,128)S(1)}, f32[24,1024]{1,0:T(8,128)S(1)}, u32[]{:S(2)}, u32[]{:S(2)}) %collective-permute-start.25) | collective-permute-done | bytes 98336 | tf_op jit(solution)/shard_map/ppermute | solution.py:1146
  199.4 3.1 %collective-permute-done.24.got = f32[56,1024]{1,0:T(8,128)S(1)} collective-permute-done((f32[56,1024]{1,0:T(8,128)S(1)}, f32[56,1024]{1,0:T(8,128)S(1)}, u32[]{:S(2)}, u32[]{:S(2)}) %collective-permute-start.24) | collective-permute-done | bytes 229408 | tf_op jit(solution)/shard_map/ppermute | solution.py:1146
  (96 shorter events, 24.3 us)
Async XLA Ops:
  2.8 18.4 %copy-start.14 = (bf16[768]{0:T(1024)(128)(2,1)S(1)}, bf16[768]{0:T(1024)(128)(2,1)}, u32[]{:S(2)}) copy-start(bf16[768]{0:T(1024)(128)(2,1)} %bo_ref.1) | copy-start | bytes 4612
  2.8 18.4 %copy-start.15 = (bf16[768]{0:T(1024)(128)(2,1)S(1)}, bf16[768]{0:T(1024)(128)(2,1)}, u32[]{:S(2)}) copy-start(bf16[768]{0:T(1024)(128)(2,1)} %b1_ref.1) | copy-start | bytes 4612
  2.8 18.4 %copy-start.16 = (bf16[768]{0:T(1024)(128)(2,1)S(1)}, bf16[768]{0:T(1024)(128)(2,1)}, u32[]{:S(2)}) copy-start(bf16[768]{0:T(1024)(128)(2,1)} %bd_ref.1) | copy-start | bytes 4612
  2.8 18.4 %copy-start.17 = (bf16[768]{0:T(1024)(128)(2,1)S(1)}, bf16[768]{0:T(1024)(128)(2,1)}, u32[]{:S(2)}) copy-start(bf16[768]{0:T(1024)(128)(2,1)} %g2_ref.1) | copy-start | bytes 4612
  2.8 18.4 %copy-start.18 = (bf16[768]{0:T(1024)(128)(2,1)S(1)}, bf16[768]{0:T(1024)(128)(2,1)}, u32[]{:S(2)}) copy-start(bf16[768]{0:T(1024)(128)(2,1)} %b2_ref.1) | copy-start | bytes 4612
  43.3 13.8 %collective-permute-start = (f32[1568,768]{1,0:T(8,128)S(1)}, f32[1568,768]{1,0:T(8,128)S(1)}, u32[]{:S(2)}, u32[]{:S(2)}) collective-permute-start(f32[1568,768]{1,0:T(8,128)S(1)} %get-tuple-element.155), channel_id=1, source_target_pairs={{0,8},{1,9},{2,10},{3,11},{4,12},{5,13},{6,14},{7,15},{8,0},{9,1},... | collective-permute-start | bytes 14450696 | tf_op jit(solution)/shard_map/ppermute | solution.py:1146
  53.8 10.6 %collective-permute-start.1 = (f32[2,384,1536]{2,1,0:T(8,128)S(1)}, f32[2,384,1536]{2,1,0:T(8,128)S(1)}, u32[]{:S(2)}, u32[]{:S(2)}) collective-permute-start(f32[2,384,1536]{2,1,0:T(8,128)S(1)} %inner_weight_send.1.after_ref), channel_id=1, source_target_pairs={{0,8},{1,9},{2,10},{3,11},{4,12},{5,13},{6,14},{7,15},{8,0},{9,1},... | collective-permute-start | bytes 14155784 | tf_op jit(solution)/shard_map/ppermute | solution.py:1146
  58.3 28.2 %collective-permute-start.2 = (f32[9,96,256]{2,1,0:T(8,128)S(1)}, f32[9,96,256]{2,1,0:T(8,128)S(1)}, u32[]{:S(2)}, u32[]{:S(2)}) collective-permute-start(f32[9,96,256]{2,1,0:T(8,128)S(1)} %get-tuple-element.168), channel_id=1, source_target_pairs={{0,1},{1,0},{2,3},{3,2},{4,5},{5,4},{6,7},{7,6},{8,9},{9,8},{10,11... | collective-permute-start | bytes 2654216 | tf_op jit(solution)/shard_map/ppermute | solution.py:1146
  61.3 25.2 %collective-permute-start.3 = (f32[4,2,96,256]{3,2,1,0:T(8,128)S(1)}, f32[4,2,96,256]{3,2,1,0:T(8,128)S(1)}, u32[]{:S(2)}, u32[]{:S(2)}) collective-permute-start(f32[4,2,96,256]{3,2,1,0:T(8,128)S(1)} %get-tuple-element.170), channel_id=1, source_target_pairs={{0,16},{1,17},{2,18},{3,19},{4,20},{5,21},{6,22},{7,23},{8,24},{9,... | collective-permute-start | bytes 2359304 | tf_op jit(solution)/shard_map/ppermute | solution.py:1146
  62.8 23.7 %collective-permute-start.4 = (f32[2,2,2,96,256]{4,3,2,1,0:T(8,128)S(1)}, f32[2,2,2,96,256]{4,3,2,1,0:T(8,128)S(1)}, u32[]{:S(2)}, u32[]{:S(2)}) collective-permute-start(f32[2,2,2,96,256]{4,3,2,1,0:T(8,128)S(1)} %get-tuple-element.172), channel_id=1, source_target_pairs={{0,2},{1,3},{2,0},{3,1},{4,6},{5,7},{6,4},{7,5},{8,10},{9,11},{10,... | collective-permute-start | bytes 2359304 | tf_op jit(solution)/shard_map/ppermute | solution.py:1146
  67.6 40.9 %collective-permute-start.5 = (f32[2,4,24,1536]{3,2,1,0:T(8,128)S(1)}, f32[2,4,24,1536]{3,2,1,0:T(8,128)S(1)}, u32[]{:S(2)}, u32[]{:S(2)}) collective-permute-start(f32[2,4,24,1536]{3,2,1,0:T(8,128)S(1)} %get-tuple-element.188), channel_id=1, source_target_pairs={{0,1},{1,0},{2,3},{3,2},{4,5},{5,4},{6,7},{7,6},{8,9},{9,8},{10,11... | collective-permute-start | bytes 3538952 | tf_op jit(solution)/shard_map/ppermute | solution.py:1146
  68.2 40.4 %collective-permute-start.6 = (f32[4,2,24,1536]{3,2,1,0:T(8,128)S(1)}, f32[4,2,24,1536]{3,2,1,0:T(8,128)S(1)}, u32[]{:S(2)}, u32[]{:S(2)}) collective-permute-start(f32[4,2,24,1536]{3,2,1,0:T(8,128)S(1)} %get-tuple-element.190), channel_id=1, source_target_pairs={{0,16},{1,17},{2,18},{3,19},{4,20},{5,21},{6,22},{7,23},{8,24},{9,... | collective-permute-start | bytes 3538952 | tf_op jit(solution)/shard_map/ppermute | solution.py:1146
  87.3 30.2 %collective-permute-start.7 = (f32[5,96,256]{2,1,0:T(8,128)S(1)}, f32[5,96,256]{2,1,0:T(8,128)S(1)}, u32[]{:S(2)}, u32[]{:S(2)}) collective-permute-start(f32[5,96,256]{2,1,0:T(8,128)S(1)} %get-tuple-element.193), channel_id=1, source_target_pairs={{0,16},{1,17},{2,18},{3,19},{4,20},{5,21},{6,22},{7,23},{8,24},{9,... | collective-permute-start | bytes 1474568 | tf_op jit(solution)/shard_map/ppermute | solution.py:1146
  88.4 26.5 %collective-permute-start.8 = (f32[4,96,256]{2,1,0:T(8,128)S(1)}, f32[4,96,256]{2,1,0:T(8,128)S(1)}, u32[]{:S(2)}, u32[]{:S(2)}) collective-permute-start(f32[4,96,256]{2,1,0:T(8,128)S(1)} %get-tuple-element.195), channel_id=1, source_target_pairs={{0,1},{1,0},{2,3},{3,2},{4,5},{5,4},{6,7},{7,6},{8,9},{9,8},{10,11... | collective-permute-start | bytes 1179656 | tf_op jit(solution)/shard_map/ppermute | solution.py:1146
  89.9 26.7 %collective-permute-start.9 = (f32[2,2,96,256]{3,2,1,0:T(8,128)S(1)}, f32[2,2,96,256]{3,2,1,0:T(8,128)S(1)}, u32[]{:S(2)}, u32[]{:S(2)}) collective-permute-start(f32[2,2,96,256]{3,2,1,0:T(8,128)S(1)} %get-tuple-element.197), channel_id=1, source_target_pairs={{0,6},{1,7},{2,4},{3,5},{4,2},{5,3},{6,0},{7,1},{8,14},{9,15},{10,... | collective-permute-start | bytes 1179656 | tf_op jit(solution)/shard_map/ppermute | solution.py:1146
  108.6 11.3 %collective-permute-start.10 = (f32[1160,1024]{1,0:T(8,128)S(1)}, f32[1160,1024]{1,0:T(8,128)S(1)}, u32[]{:S(2)}, u32[]{:S(2)}) collective-permute-start(f32[1160,1024]{1,0:T(8,128)S(1)} %qkv_weight_send.1.after_ref.own_ref), channel_id=1, source_target_pairs={{0,8},{1,9},{2,10},{3,11},{4,12},{5,13},{6,14},{7,15},{8,0},{9,1},... | collective-permute-start | bytes 14254088 | tf_op jit(solution)/shard_map/ppermute | solution.py:1146
  109.5 20.7 %collective-permute-start.11 = (f32[4,24,1536]{2,1,0:T(8,128)S(1)}, f32[4,24,1536]{2,1,0:T(8,128)S(1)}, u32[]{:S(2)}, u32[]{:S(2)}) collective-permute-start(f32[4,24,1536]{2,1,0:T(8,128)S(1)} %get-tuple-element.201), channel_id=1, source_target_pairs={{0,16},{1,17},{2,18},{3,19},{4,20},{5,21},{6,22},{7,23},{8,24},{9,... | collective-permute-start | bytes 1769480 | tf_op jit(solution)/shard_map/ppermute | solution.py:1146
  114.8 15.4 %collective-permute-start.12 = (f32[4,24,1536]{2,1,0:T(8,128)S(1)}, f32[4,24,1536]{2,1,0:T(8,128)S(1)}, u32[]{:S(2)}, u32[]{:S(2)}) collective-permute-start(f32[4,24,1536]{2,1,0:T(8,128)S(1)} %get-tuple-element.203), channel_id=1, source_target_pairs={{0,1},{1,0},{2,3},{3,2},{4,5},{5,4},{6,7},{7,6},{8,9},{9,8},{10,11... | collective-permute-start | bytes 1769480 | tf_op jit(solution)/shard_map/ppermute | solution.py:1146
  118.2 19.4 %collective-permute-start.13 = (f32[240,512]{1,0:T(8,128)S(1)}, f32[240,512]{1,0:T(8,128)S(1)}, u32[]{:S(2)}, u32[]{:S(2)}) collective-permute-start(f32[240,512]{1,0:T(8,128)S(1)} %get-tuple-element.209), channel_id=1, source_target_pairs={{0,2},{1,3},{2,0},{3,1},{4,6},{5,7},{6,4},{7,5},{8,10},{9,11},{10,... | collective-permute-start | bytes 1474568 | tf_op jit(solution)/shard_map/ppermute | solution.py:1146
  123.2 30.5 %collective-permute-start.16 = (f32[192,1024]{1,0:T(8,128)S(1)}, f32[192,1024]{1,0:T(8,128)S(1)}, u32[]{:S(2)}, u32[]{:S(2)}) collective-permute-start(f32[192,1024]{1,0:T(8,128)S(1)} %get-tuple-element.216), channel_id=1, source_target_pairs={{0,2},{1,3},{2,0},{3,1},{4,6},{5,7},{6,4},{7,5},{8,10},{9,11},{10,... | collective-permute-start | bytes 2359304 | tf_op jit(solution)/shard_map/ppermute | solution.py:1146
  123.7 29.9 %collective-permute-start.15 = (f32[200,1024]{1,0:T(8,128)S(1)}, f32[200,1024]{1,0:T(8,128)S(1)}, u32[]{:S(2)}, u32[]{:S(2)}) collective-permute-start(f32[200,1024]{1,0:T(8,128)S(1)} %get-tuple-element.214), channel_id=1, source_target_pairs={{0,16},{1,17},{2,18},{3,19},{4,20},{5,21},{6,22},{7,23},{8,24},{9,... | collective-permute-start | bytes 2457608 | tf_op jit(solution)/shard_map/ppermute | solution.py:1146
  130.2 23.5 %collective-permute-start.14 = (f32[240,1024]{1,0:T(8,128)S(1)}, f32[240,1024]{1,0:T(8,128)S(1)}, u32[]{:S(2)}, u32[]{:S(2)}) collective-permute-start(f32[240,1024]{1,0:T(8,128)S(1)} %get-tuple-element.212), channel_id=1, source_target_pairs={{0,1},{1,0},{2,3},{3,2},{4,5},{5,4},{6,7},{7,6},{8,9},{9,8},{10,11... | collective-permute-start | bytes 2949128 | tf_op jit(solution)/shard_map/ppermute | solution.py:1146
  138.2 24.0 %collective-permute-start.17 = (f32[144,512]{1,0:T(8,128)S(1)}, f32[144,512]{1,0:T(8,128)S(1)}, u32[]{:S(2)}, u32[]{:S(2)}) collective-permute-start(f32[144,512]{1,0:T(8,128)S(1)} %get-tuple-element.220), channel_id=1, source_target_pairs={{0,6},{1,7},{2,4},{3,5},{4,2},{5,3},{6,0},{7,1},{8,14},{9,15},{10,... | collective-permute-start | bytes 884744 | tf_op jit(solution)/shard_map/ppermute | solution.py:1146
  142.4 34.7 %collective-permute-start.21 = (f32[2,24,3072]{2,1,0:T(8,128)S(1)}, f32[2,24,3072]{2,1,0:T(8,128)S(1)}, u32[]{:S(2)}, u32[]{:S(2)}) collective-permute-start(f32[2,24,3072]{2,1,0:T(8,128)S(1)} %get-tuple-element.229), channel_id=1, source_target_pairs={{0,2},{1,3},{2,0},{3,1},{4,6},{5,7},{6,4},{7,5},{8,10},{9,11},{10,... | collective-permute-start | bytes 1769480 | tf_op jit(solution)/shard_map/ppermute | solution.py:1146
  154.4 21.3 %collective-permute-start.20 = (f32[96,1024]{1,0:T(8,128)S(1)}, f32[96,1024]{1,0:T(8,128)S(1)}, u32[]{:S(2)}, u32[]{:S(2)}) collective-permute-start(f32[96,1024]{1,0:T(8,128)S(1)} %get-tuple-element.227), channel_id=1, source_target_pairs={{0,6},{1,7},{2,4},{3,5},{4,2},{5,3},{6,0},{7,1},{8,14},{9,15},{10,... | collective-permute-start | bytes 1179656 | tf_op jit(solution)/shard_map/ppermute | solution.py:1146
  160.1 15.6 %collective-permute-start.19 = (f32[104,1024]{1,0:T(8,128)S(1)}, f32[104,1024]{1,0:T(8,128)S(1)}, u32[]{:S(2)}, u32[]{:S(2)}) collective-permute-start(f32[104,1024]{1,0:T(8,128)S(1)} %get-tuple-element.225), channel_id=1, source_target_pairs={{0,1},{1,0},{2,3},{3,2},{4,5},{5,4},{6,7},{7,6},{8,9},{9,8},{10,11... | collective-permute-start | bytes 1277960 | tf_op jit(solution)/shard_map/ppermute | solution.py:1146
  160.7 15.0 %collective-permute-start.18 = (f32[120,1024]{1,0:T(8,128)S(1)}, f32[120,1024]{1,0:T(8,128)S(1)}, u32[]{:S(2)}, u32[]{:S(2)}) collective-permute-start(f32[120,1024]{1,0:T(8,128)S(1)} %get-tuple-element.223), channel_id=1, source_target_pairs={{0,16},{1,17},{2,18},{3,19},{4,20},{5,21},{6,22},{7,23},{8,24},{9,... | collective-permute-start | bytes 1474568 | tf_op jit(solution)/shard_map/ppermute | solution.py:1146
  176.4 17.6 %collective-permute-start.22 = (f32[104,1024]{1,0:T(8,128)S(1)}, f32[104,1024]{1,0:T(8,128)S(1)}, u32[]{:S(2)}, u32[]{:S(2)}) collective-permute-start(f32[104,1024]{1,0:T(8,128)S(1)} %get-tuple-element.235), channel_id=1, source_target_pairs={{0,2},{1,3},{2,0},{3,1},{4,6},{5,7},{6,4},{7,5},{8,10},{9,11},{10,... | collective-permute-start | bytes 1277960 | tf_op jit(solution)/shard_map/ppermute | solution.py:1146
  176.5 5.7 %collective-permute-start.23 = (f32[48,1024]{1,0:T(8,128)S(1)}, f32[48,1024]{1,0:T(8,128)S(1)}, u32[]{:S(2)}, u32[]{:S(2)}) collective-permute-start(f32[48,1024]{1,0:T(8,128)S(1)} %get-tuple-element.237), channel_id=1, source_target_pairs={{0,1},{1,0},{2,3},{3,2},{4,5},{5,4},{6,7},{7,6},{8,9},{9,8},{10,11... | collective-permute-start | bytes 589832 | tf_op jit(solution)/shard_map/ppermute | solution.py:1146
  177.7 18.6 %collective-permute-start.26 = (f32[24,3072]{1,0:T(8,128)S(1)}, f32[24,3072]{1,0:T(8,128)S(1)}, u32[]{:S(2)}, u32[]{:S(2)}) collective-permute-start(f32[24,3072]{1,0:T(8,128)S(1)} %get-tuple-element.253), channel_id=1, source_target_pairs={{0,6},{1,7},{2,4},{3,5},{4,2},{5,3},{6,0},{7,1},{8,14},{9,15},{10,... | collective-permute-start | bytes 884744 | tf_op jit(solution)/shard_map/ppermute | solution.py:1146
  194.6 7.9 %collective-permute-start.24 = (f32[56,1024]{1,0:T(8,128)S(1)}, f32[56,1024]{1,0:T(8,128)S(1)}, u32[]{:S(2)}, u32[]{:S(2)}) collective-permute-start(f32[56,1024]{1,0:T(8,128)S(1)} %get-tuple-element.239), channel_id=1, source_target_pairs={{0,6},{1,7},{2,4},{3,5},{4,2},{5,3},{6,0},{7,1},{8,14},{9,15},{10,... | collective-permute-start | bytes 688136 | tf_op jit(solution)/shard_map/ppermute | solution.py:1146
  194.7 4.7 %collective-permute-start.25 = (f32[24,1024]{1,0:T(8,128)S(1)}, f32[24,1024]{1,0:T(8,128)S(1)}, u32[]{:S(2)}, u32[]{:S(2)}) collective-permute-start(f32[24,1024]{1,0:T(8,128)S(1)} %get-tuple-element.241), channel_id=1, source_target_pairs={{0,16},{1,17},{2,18},{3,19},{4,20},{5,21},{6,22},{7,23},{8,24},{9,... | collective-permute-start | bytes 294920 | tf_op jit(solution)/shard_map/ppermute | solution.py:1146
  (17 other events, 147.7 us)
